TPU v7x, 32 devices: a whole 2x2x4 slice. The times are simulated.
32 devices in a mesh: dp: 8 (over z, y), mp: 4 (over x, core).
Axes of the slice: x: 2, y: 2, z: 4, core: 2. Of those that a mesh axis runs over, the one named last changes fastest.
Arguments:
- inputs: bfloat16 [9216, 2304], P('dp', 'mp'), may hold values from -6 to 6
- lengths: int32 [8], P('dp'), may hold values from 896 to 1152, as said below
- start_cell: float32 [8, 2304], P('dp', 'mp'), may hold values from -6 to 6
- weight: bfloat16 [2, 2304, 3, 2304], P(None, None, None, 'mp'), may hold values from -0.09375 to 0.09375
- bias: bfloat16 [3, 2304], P(None, 'mp'), may hold values from -1 to 7
- out_grad: bfloat16 [9216, 2304], P('dp', 'mp'), may hold values from -6 to 6
- cell_grad: float32 [8, 2304], P('dp', 'mp'), may hold values from -6 to 6
Outputs:
- hidden: bfloat16 [9216, 2304], P('dp', 'mp')
- last_cell: float32 [8, 2304], P('dp', 'mp')
- input_grad: bfloat16 [9216, 2304], P('dp', 'mp')
- start_grad: float32 [8, 2304], P('dp', 'mp')
- weight_grad: float32 [2, 2304, 3, 2304], P(None, None, None, 'mp')
- bias_grad: float32 [3, 2304], P(None, 'mp')
Inputs may be any that keep to these rules, and one draw needn't show every extreme that they name: `lengths`: each length is 896, 1024 or 1152; every draw has a window of 1152 and one of 896.
All inputs are finite; a program needn't handle non-finite values.
Results may differ from a plain program's by a relative error of at most 0.0049.
Values may be sent and summed in bfloat16 or wider, within the bound.
No kernel may reach another device: no remote copies, remote signals or barrier semaphores. Data moves between devices by JAX's collectives and lax.ppermute only.
A program may use at most 192 MiB of HBM per device.

v0:
```python
import jax
import jax.numpy as jnp
from jax import lax
from jax.sharding import PartitionSpec as P


def shift_down(block, win_count):
    shaped = block.reshape(win_count, -1, block.shape[-1])
    moved = jnp.concatenate([jnp.zeros_like(shaped[:, :1]), shaped[:, :-1]], axis=1)
    return moved.reshape(block.shape)


def shift_up(block, win_count):
    shaped = block.reshape(win_count, -1, block.shape[-1])
    moved = jnp.concatenate([shaped[:, 1:], jnp.zeros_like(shaped[:, :1])], axis=1)
    return moved.reshape(block.shape)


def contract_rows(left_side, right_side):
    return lax.dot_general(
        left_side, right_side, (((0,), (0,)), ((), ())), preferred_element_type=jnp.float32
    )


def contract_cols(left_side, right_side):
    return lax.dot_general(
        left_side, right_side, (((1,), (1,)), ((), ())), preferred_element_type=jnp.float32
    )


def pool_forward(decay_rate, new_input, start_cell, block_len):
    later_iota = lax.broadcasted_iota(jnp.int32, (1, block_len, block_len, 1), 1)
    early_iota = lax.broadcasted_iota(jnp.int32, (1, block_len, block_len, 1), 2)
    lower_mask = later_iota >= early_iota
    carry = start_cell
    pieces = []
    for block_num in range(decay_rate.shape[1] // block_len):
        decay_piece = decay_rate[:, block_num * block_len : (block_num + 1) * block_len]
        input_piece = new_input[:, block_num * block_len : (block_num + 1) * block_len]
        running = jnp.cumsum(jnp.log(decay_piece), axis=1)
        spread = running[:, :, None, :] - running[:, None, :, :]
        factors = jnp.where(lower_mask, jnp.exp(jnp.minimum(spread, 0.0)), 0.0)
        current = (
            jnp.sum(factors * input_piece[:, None, :, :], axis=2)
            + jnp.exp(running) * carry[:, None, :]
        )
        pieces.append(current)
        carry = current[:, -1]
    return jnp.concatenate(pieces, axis=1)


def pool_backward(decay_rate, emitted, block_len):
    later_iota = lax.broadcasted_iota(jnp.int32, (1, block_len, block_len, 1), 1)
    early_iota = lax.broadcasted_iota(jnp.int32, (1, block_len, block_len, 1), 2)
    upper_mask = early_iota >= later_iota
    carry = jnp.zeros_like(emitted[:, 0])
    block_total = decay_rate.shape[1] // block_len
    pieces = [None] * block_total
    for block_num in range(block_total - 1, -1, -1):
        decay_piece = decay_rate[:, block_num * block_len : (block_num + 1) * block_len]
        emit_piece = emitted[:, block_num * block_len : (block_num + 1) * block_len]
        running = jnp.cumsum(jnp.log(decay_piece), axis=1)
        spread = running[:, None, :, :] - running[:, :, None, :]
        factors = jnp.where(upper_mask, jnp.exp(jnp.minimum(spread, 0.0)), 0.0)
        current = jnp.sum(factors * emit_piece[:, None, :, :], axis=2)
        current = current + jnp.exp(running[:, -1:] - running) * carry[:, None, :]
        pieces[block_num] = current
        carry = decay_piece[:, 0] * current[:, 0]
    return jnp.concatenate(pieces, axis=1)


def on_device(inputs, lengths, start_cell, weight, bias, out_grad, cell_grad):
    row_count = inputs.shape[0]
    win_count = lengths.shape[0]
    win_span = row_count // win_count
    block_len = win_span // 9
    in_width = weight.shape[1]
    own_width = weight.shape[3]
    gate_count = 3 * own_width
    flat_weight = weight.reshape(2, in_width, gate_count)
    gathered = lax.all_gather(inputs, "mp", axis=1, tiled=True)
    shifted = shift_down(gathered, win_count)
    gates = jnp.dot(gathered, flat_weight[0], preferred_element_type=jnp.float32)
    gates = gates + jnp.dot(shifted, flat_weight[1], preferred_element_type=jnp.float32)
    gates = gates + bias.reshape(1, gate_count).astype(jnp.float32)
    window_shape = (win_count, win_span, own_width)
    candidate = jnp.tanh(gates[:, :own_width]).reshape(window_shape)
    forget_gate = jax.nn.sigmoid(gates[:, own_width : 2 * own_width]).reshape(window_shape)
    output_gate = jax.nn.sigmoid(gates[:, 2 * own_width :]).reshape(window_shape)
    positions = lax.broadcasted_iota(jnp.int32, (win_count, win_span, 1), 1)
    live_mask = (positions < lengths[:, None, None]).astype(jnp.float32)
    decay_rate = 1.0 - live_mask * (1.0 - forget_gate)
    new_input = live_mask * (1.0 - forget_gate) * candidate
    cell_states = pool_forward(decay_rate, new_input, start_cell, block_len)
    hidden = (
        (live_mask * output_gate * cell_states).reshape(row_count, own_width).astype(jnp.bfloat16)
    )
    last_cell = cell_states[:, -1]
    grad_hidden = out_grad.astype(jnp.float32).reshape(window_shape)
    emitted = live_mask * output_gate * grad_hidden
    last_flag = (positions == win_span - 1).astype(jnp.float32)
    emitted = emitted + last_flag * cell_grad[:, None, :]
    cell_grads = pool_backward(decay_rate, emitted, block_len)
    start_grad = decay_rate[:, 0] * cell_grads[:, 0]
    previous = jnp.concatenate([start_cell[:, None, :], cell_states[:, :-1]], axis=1)
    grad_cand = cell_grads * live_mask * (1.0 - forget_gate) * (1.0 - candidate * candidate)
    grad_forget = (
        cell_grads * live_mask * (previous - candidate) * forget_gate * (1.0 - forget_gate)
    )
    grad_output = live_mask * cell_states * grad_hidden * output_gate * (1.0 - output_gate)
    gate_grads = jnp.concatenate([grad_cand, grad_forget, grad_output], axis=2)
    gate_grads = gate_grads.reshape(row_count, gate_count).astype(jnp.bfloat16)
    back_term = contract_cols(gate_grads, flat_weight[0])
    back_term = back_term + contract_cols(shift_up(gate_grads, win_count), flat_weight[1])
    input_grad = lax.psum_scatter(back_term, "mp", scatter_dimension=1, tiled=True).astype(
        jnp.bfloat16
    )
    weight_part = jnp.stack(
        [contract_rows(gathered, gate_grads), contract_rows(shifted, gate_grads)]
    )
    ones_column = jnp.ones((row_count,), jnp.bfloat16)
    bias_part = jnp.dot(ones_column, gate_grads, preferred_element_type=jnp.float32)
    weight_sum, bias_sum = lax.psum((weight_part, bias_part), "dp")
    return (
        hidden,
        last_cell,
        input_grad,
        start_grad,
        weight_sum.reshape(2, in_width, 3, own_width),
        bias_sum.reshape(3, own_width),
    )


def solution(mesh):
    in_specs = (
        P("dp", "mp"),
        P("dp"),
        P("dp", "mp"),
        P(None, None, None, "mp"),
        P(None, "mp"),
        P("dp", "mp"),
        P("dp", "mp"),
    )
    out_specs = (
        P("dp", "mp"),
        P("dp", "mp"),
        P("dp", "mp"),
        P("dp", "mp"),
        P(None, None, None, "mp"),
        P(None, "mp"),
    )
    return jax.shard_map(
        on_device, mesh=mesh, in_specs=in_specs, out_specs=out_specs, check_vma=False
    )
```

profile of v0, /device:TPU:0, one launch (start us, length us, event | category | flops | bytes accessed | tf_op | source)
XLA Modules:
  0.0 1619.3 jit_solution(11349436806023497405)
XLA Ops:
  13.5 11.9 fusion.74
  25.5 27.6 %all-gather.2.cloned.1.call-done = bf16[1152,2304]{0,1:T(8,128)(2,1)} async-done(((bf16[1152,576]{0,1:T(8,128)(2,1)}), bf16[1152,2304]{0,1:T(8,128)(2,1)}) %all-gather.2.cloned.1.call-update) | async-done | bytes 5308432 | tf_op jit(solution)/shard_map/all_gather | solution.py:81
  53.1 16.1 fusion.75
  69.2 14.9 fusion
  84.1 4.2 multiply_bitcast_fusion
  93.3 1.9 copy.199
  95.1 2.0 reduce_window_sum.75
  101.5 2.0 reduce_window_sum.74
  104.3 1.9 copy.194
  108.0 2.0 reduce_window_sum.73
  114.4 2.0 reduce_window_sum.72
  124.9 2.0 reduce_window_sum.57
  134.5 4.9 slice_bitcast_fusion.7
  139.4 40.8 %multiply_reduce_fusion.6 = (f32[128,576]{1,0:T(8,128)}, f32[128,576]{1,0:T(8,128)}) fusion(f32[128,576]{0,1:T(8,128)} %get-tuple-element.82, f32[128,576]{0,1:T(8,128)} %bitcast.172, f32[128,576]{1,0:T(8,128)} %bitcast.189, pred[128,128]{1,0:T(8,128)(4,1)S(1)} %get-tuple-element.118, f32[128,576]{0,1:T(8,128)} %get-tuple-element.117, ...), kind=kLoop, calls=%fused_computation.6 | loop fusion | flops 94224384 | bytes 1802240 | tf_op jit(solution)/shard_map/reduce_sum | solution.py:65
  183.9 146.0 %multiply_reduce_fusion.7 = (f32[128,576]{1,0:T(8,128)}, f32[128,576]{1,0:T(8,128)}, f32[128,576]{1,0:T(8,128)}, f32[128,576]{1,0:T(8,128)}, f32[128,576]{1,0:T(...) fusion(f32[128,576]{0,1:T(8,128)} %get-tuple-element.89, f32[128,576]{0,1:T(8,128)} %bitcast.175, ...), kind=kLoop, calls=%fused_computation.7 | loop fusion | flops 376897536 | bytes 7110656 | tf_op jit(solution)/shard_map/reduce_sum | solution.py:65
  344.6 146.5 %multiply_reduce_fusion.8 = (f32[128,576]{1,0:T(8,128)}, f32[128,576]{1,0:T(8,128)}, f32[128,576]{1,0:T(8,128)}, f32[128,576]{1,0:T(8,128)}, f32[128,576]{1,0:T(...) fusion(f32[128,576]{0,1:T(8,128)} %get-tuple-element.90, f32[128,576]{0,1:T(8,128)S(1)} %bitcast.167, ...), kind=kLoop, calls=%fused_computation.8 | loop fusion | flops 376897536 | bytes 7110656 | tf_op jit(solution)/shard_map/reduce_sum | solution.py:65
  491.1 1.9 copy.229
  521.8 2.7 fusion.73
  524.5 2.8 subtract_multiply_fusion
  527.3 16.2 fusion.23
  543.5 6.6 maximum_convert_fusion
  550.1 1.9 copy-done.1
  552.0 4.1 slice.379
  556.1 16.8 %convolution_add_fusion = f32[1152,2304]{0,1:T(8,128)} fusion(f32[1152,2304]{0,1:T(8,128)} %fusion.23, bf16[2304,1728]{0,1:T(8,128)(2,1)S(1)} %bitcast.160, bf16[1,1151,1728]{1,2,0:T(8,128)(2,1)} %slice.379), kind=kOutput, calls=%fused_computation.19 | convolution fusion | flops 9175597056 | bytes 33174144 | tf_op jit(solution)/shard_map/dot_general | solution.py:26
  573.0 16.8 %convolution_bitcast_fusion = f32[1,2304,1728]{1,2,0:T(8,128)} fusion(bf16[1,1151,2304]{1,2,0:T(8,128)(2,1)} %bitcast.194, bf16[1152,576]{0,1:T(8,128)(2,1)} %get-tuple-element.58, bf16[1152,576]{0,1:T(8,128)(2,1)} %copy-done.6, bf16[1152,576]{0,1:T(8,128)(2,1)} %copy-done.5), kind=kOutput, calls=%fused_computation.20 | convolution fusion | flops 9184886784 | bytes 25210368 | tf_op jit(solution)/shard_map/dot_general | solution.py:20
  589.7 15.1 convolution_bitcast_fusion.1
  604.8 22.3 %pad_maximum_fusion = f32[2,2304,1728]{1,2,0:T(8,128)} fusion(f32[1,2304,1728]{1,2,0:T(8,128)} %convolution_bitcast_fusion, f32[1,2304,1728]{1,2,0:T(8,128)} %convolution_bitcast_fusion.1), kind=kLoop, calls=%fused_computation.18 | loop fusion | flops 7962624 | bytes 63700992 | tf_op jit(solution)/shard_map/stack | solution.py:118
  630.8 3.4 fusion.24
  634.3 37.2 %psum.15 = f32[3,576]{1,0:T(4,128)} all-reduce(f32[3,576]{1,0:T(4,128)S(1)} %reshape.2108), channel_id=1, replica_groups=mesh['dp'=8,'mp'=4] {'dp'}, use_global_device_ids=true, to_apply=%region_29.30 | all-reduce | flops 1728 | bytes 13824 | tf_op jit(solution)/shard_map/psum | solution.py:123
  671.5 2.9 convert_element_type.59
  674.5 916.0 %all-reduce.4.cloned.1.call-done = f32[2,2304,3,576]{1,3,2,0:T(8,128)} async-done(((f32[2,2304,3,576]{1,3,2,0:T(8,128)}), f32[2,2304,3,576]{1,3,2,0:T(8,128)}) %all-reduce.4.cloned.1.call-update) | async-done | bytes 31850512 | tf_op jit(solution)/shard_map/psum | solution.py:123
  1590.5 21.9 %copy.276 = f32[2,2304,3,576]{1,3,2,0:T(8,128)} copy(f32[2,2304,3,576]{1,3,2,0:T(8,128)} %all-reduce.4.cloned.1.call-done) | data formatting | bytes 63700992
  (197 shorter events, 88.7 us)
Async XLA Ops:
  7.2 45.9 %all-gather.2.cloned.1.call-start = ((), (), s32[]{:S(2)}) async-start(), calls=%async_computation.1 | async-start | bytes 6635520 | tf_op jit(solution)/shard_map/all_gather | solution.py:81
  7.9 663.6 %reduce-scatter.2.cloned.1.call-start = ((), (), s32[]{:S(2)}) async-start(), calls=%async_computation.2 | async-start | bytes 13271040 | tf_op jit(solution)/shard_map/reduce_scatter | solution.py:115
  53.1 16.1 copy-start.40
  69.2 14.9 copy-start.3
  84.1 4.7 copy-start
  93.1 25.9 %copy-start.33 = (f32[1,128,576]{2,1,0:T(8,128)}, f32[1,128,576]{2,1,0:T(8,128)S(1)}, u32[]{:S(2)}) copy-start(f32[1,128,576]{2,1,0:T(8,128)S(1)} %reduce_window_sum.76) | copy-start | bytes 884740
  122.2 7.3 copy-start.36
  134.5 4.9 copy-start.39
  491.1 14.7 copy-start.38
  505.8 7.4 copy-start.9
  505.8 7.4 copy-start.24
  507.0 6.6 copy-start.8
  507.0 6.6 copy-start.30
  508.5 5.6 copy-start.7
  508.5 5.6 copy-start.28
  510.0 4.5 copy-start.25
  515.6 2.5 copy-start.13
  515.7 2.5 copy-start.23
  515.7 2.9 copy-start.14
  515.7 2.9 copy-start.32
  516.0 2.9 copy-start.31
  516.3 2.8 copy-start.26
  516.3 4.9 slice-start
  521.8 2.7 copy-start.37
  521.8 5.5 slice-start.4
  524.5 2.8 slice-start.5
  527.2 16.2 %copy-start.5 = (bf16[1152,576]{0,1:T(8,128)(2,1)}, bf16[1152,576]{0,1:T(8,128)(2,1)S(1)}, u32[]{:S(2)}) copy-start(bf16[1152,576]{0,1:T(8,128)(2,1)S(1)} %get-tuple-element.56) | copy-start | bytes 3981316
  527.3 16.2 %copy-start.6 = (bf16[1152,576]{0,1:T(8,128)(2,1)}, bf16[1152,576]{0,1:T(8,128)(2,1)S(1)}, u32[]{:S(2)}) copy-start(bf16[1152,576]{0,1:T(8,128)(2,1)S(1)} %get-tuple-element.57) | copy-start | bytes 3981316
  543.5 12.6 slice-start.2
  552.0 4.1 slice-start.3
  572.9 1017.6 %all-reduce.4.cloned.1.call-start = ((), (), s32[]{:S(2)}) async-start(), calls=%async_computation.3 | async-start | bytes 63700992 | tf_op jit(solution)/shard_map/psum | solution.py:123
  573.0 16.8 %copy-start.2 = (bf16[1,1152,1728]{1,2,0:T(8,128)(2,1)S(1)}, bf16[1,1152,1728]{1,2,0:T(8,128)(2,1)}, u32[]{:S(2)}) copy-start(bf16[1,1152,1728]{1,2,0:T(8,128)(2,1)} %copy-done.1) | copy-start | bytes 11943940
  (18 other events, 31.1 us)
Sparse Core Ops, SparseCore 0:
  9.6 43.4 all-gather.1
  573.0 86.1 reduce-scatter.1
  664.0 926.3 all-reduce.3
where the time goes:
time: 1630 us; the launch traced here: 1620 us
  waiting for transfers between devices  944 us (58%)
  other arithmetic  403 us (25%)
  local copies, waits for them, and re-layouts  119 us (7%)
  matrix products  99.2 us (6%)
  blocking collectives  37.2 us (2%)
    psum x1, waiting for transfers between devices, on_device(): weight_sum, bias_sum = lax.psum((weight_part, bias_part), 'dp')  916 us
    reduce_sum x3, other arithmetic, pool_backward(): current = jnp.sum(factors * emit_piece[:, None, :, :], axis=2)  333 us
    psum x1, blocking collectives, on_device(): weight_sum, bias_sum = lax.psum((weight_part, bias_part), 'dp')  37.2 us
    dot_general x2, matrix products, contract_cols(): lax.dot_general(left_side, right_side, (((1,), (1,)), ((), ())), preferre...  33 us
  transfers between devices with their start and end apart: 3, of which 2 were waited for; matrix products, arithmetic and copies ran while one was open for 5% of the time, Pallas kernels for 0%

commit v1 on v0

v1 whole, which is shorter than its diff:
```python
import functools

import jax
import jax.numpy as jnp
from jax import lax
from jax.experimental import pallas as pl
from jax.experimental.pallas import tpu as pltpu
from jax.sharding import PartitionSpec as P

LANES = 128
ROWS = 16


def pool_kernel(length_ref, gates_ref, small_ref, grad_ref, hidden_ref, sums_ref, gg_ref):
    span = grad_ref.shape[-1]
    tiles = span // LANES
    length = length_ref[0]
    lane = lax.broadcasted_iota(jnp.int32, (ROWS, LANES), 1)
    zero = jnp.zeros((ROWS, LANES), jnp.float32)

    def block(step, unused):
        row = pl.multiple_of(step * ROWS, ROWS)
        rows = pl.ds(row, ROWS)
        small = small_ref[rows, :]

        def column(index):
            return jnp.broadcast_to(small[:, index : index + 1], (ROWS, LANES))

        bias = [column(k) for k in range(3)]
        carry = column(3)
        ahead_last = [zero] * 3
        cand, forget, keep, out_gate, live, decay, cell, before = ([] for _ in range(8))
        for j in range(tiles):
            cols = pl.ds(j * LANES, LANES)
            gates = []
            for k in range(3):
                later = pltpu.roll(gates_ref[1, k, rows, cols], 1, 1)
                gates.append(
                    gates_ref[0, k, rows, cols]
                    + jnp.where(lane == 0, ahead_last[k], later)
                    + bias[k]
                )
                ahead_last[k] = later
            alive = (lane + j * LANES < length).astype(jnp.float32)
            c = jnp.tanh(gates[0])
            f = jax.nn.sigmoid(gates[1])
            o = jax.nn.sigmoid(gates[2])
            kept = alive * (1.0 - f)
            d = 1.0 - kept
            product, total = d, kept * c
            for k in (1, 2, 4, 8, 16, 32, 64):
                inside = lane >= k
                total = total + product * jnp.where(inside, pltpu.roll(total, k, 1), 0.0)
                product = product * jnp.where(inside, pltpu.roll(product, k, 1), 1.0)
            total = total + product * carry
            moved = pltpu.roll(total, 1, 1)
            before.append(jnp.where(lane == 0, carry, moved))
            carry = jnp.broadcast_to(total[:, LANES - 1 :], (ROWS, LANES))
            cand.append(c)
            forget.append(f)
            keep.append(kept)
            out_gate.append(o)
            live.append(alive)
            decay.append(d)
            cell.append(total)
        last_cell = carry[:, :1]
        carry = zero
        decay_next = zero
        first_next = [zero] * 3
        bias_sum = [zero] * 3
        for j in range(tiles - 1, -1, -1):
            cols = pl.ds(j * LANES, LANES)
            grad = grad_ref[rows, cols].astype(jnp.float32)
            lo = live[j] * out_gate[j]
            emitted = lo * grad
            if j == tiles - 1:
                emitted = emitted + jnp.where(lane == LANES - 1, column(4), 0.0)
            hidden_ref[rows, cols] = (lo * cell[j]).astype(jnp.bfloat16)
            back = pltpu.roll(decay[j], LANES - 1, 1)
            product = jnp.where(lane == LANES - 1, decay_next, back)
            decay_next = back
            total = emitted
            for k in (1, 2, 4, 8, 16, 32, 64):
                inside = lane < LANES - k
                total = total + product * jnp.where(inside, pltpu.roll(total, LANES - k, 1), 0.0)
                product = product * jnp.where(inside, pltpu.roll(product, LANES - k, 1), 1.0)
            total = total + product * carry
            carry = jnp.broadcast_to(total[:, :1], (ROWS, LANES))
            shared = total * keep[j]
            outs = [
                shared * (1.0 - cand[j] * cand[j]),
                shared * (before[j] - cand[j]) * forget[j],
                emitted * cell[j] * (1.0 - out_gate[j])
                if j < tiles - 1
                else lo * grad * cell[j] * (1.0 - out_gate[j]),
            ]
            for k in range(3):
                rounded = outs[k].astype(jnp.bfloat16)
                gg_ref[0, k, rows, cols] = rounded
                wide = rounded.astype(jnp.float32)
                bias_sum[k] = bias_sum[k] + wide
                moved = pltpu.roll(wide, LANES - 1, 1)
                gg_ref[1, k, rows, cols] = jnp.where(
                    lane == LANES - 1, first_next[k], moved
                ).astype(jnp.bfloat16)
                first_next[k] = moved
        start_grad = decay[0][:, :1] * carry[:, :1]
        columns = [last_cell, start_grad] + [
            jnp.sum(s, axis=1, keepdims=True) for s in bias_sum
        ]
        answer = zero
        for index, value in enumerate(columns):
            answer = jnp.where(lane == index, jnp.broadcast_to(value, (ROWS, LANES)), answer)
        sums_ref[rows, :] = answer
        return unused

    lax.fori_loop(0, grad_ref.shape[0] // ROWS, block, 0)


def pool(length, gates, small, grad):
    taps, kinds, width, span = gates.shape
    part = 48
    return pl.pallas_call(
        pool_kernel,
        grid=(width // part,),
        in_specs=[
            pl.BlockSpec(memory_space=pltpu.SMEM),
            pl.BlockSpec((2, 3, part, span), lambda i: (0, 0, i, 0)),
            pl.BlockSpec((part, LANES), lambda i: (i, 0)),
            pl.BlockSpec((part, span), lambda i: (i, 0)),
        ],
        out_specs=[
            pl.BlockSpec((part, span), lambda i: (i, 0)),
            pl.BlockSpec((part, LANES), lambda i: (i, 0)),
            pl.BlockSpec((2, 3, part, span), lambda i: (0, 0, i, 0)),
        ],
        out_shape=[
            jax.ShapeDtypeStruct((width, span), jnp.bfloat16),
            jax.ShapeDtypeStruct((width, LANES), jnp.float32),
            jax.ShapeDtypeStruct((2, 3, width, span), jnp.bfloat16),
        ],
        compiler_params=pltpu.CompilerParams(vmem_limit_bytes=40 * 2**20),
        cost_estimate=pl.CostEstimate(
            flops=150 * width * span, bytes_accessed=48 * width * span, transcendentals=6 * width * span
        ),
        name="pool",
    )(length, gates, small, grad)


def small_columns(bias, start_cell, cell_grad):
    stacked = jnp.concatenate([bias.astype(jnp.float32), start_cell, cell_grad], axis=0)
    return jnp.pad(stacked.T, ((0, 0), (0, LANES - 5)))


def on_device(inputs, lengths, start_cell, weight, bias, out_grad, cell_grad):
    span, width = inputs.shape
    depth = weight.shape[1]
    x_own = inputs.T
    w_rows = jnp.transpose(weight, (0, 2, 3, 1))
    x_all = lax.all_gather(x_own, "mp", axis=0, tiled=True)
    w_flat = w_rows.reshape(6 * width, depth)
    gates = jnp.dot(w_flat, x_all, preferred_element_type=jnp.float32)
    small = small_columns(bias, start_cell, cell_grad)
    hidden, sums, gg = pool(lengths, gates.reshape(2, 3, width, span), small, out_grad.T)
    gg = gg.reshape(6 * width, span)
    back = lax.dot_general(w_flat, gg, (((0,), (0,)), ((), ())), preferred_element_type=jnp.float32)
    input_grad = lax.psum_scatter(
        back.astype(jnp.bfloat16), "mp", scatter_dimension=0, tiled=True
    )
    wgrad = lax.dot_general(gg, x_all, (((1,), (1,)), ((), ())), preferred_element_type=jnp.float32)
    wgrad = lax.psum(wgrad.astype(jnp.bfloat16), "dp").astype(jnp.float32)
    bias_grad = lax.psum(sums[:, 2:5].T, "dp")
    return (
        hidden.T,
        sums[:, 0:1].T,
        input_grad.T,
        sums[:, 1:2].T,
        jnp.transpose(wgrad.reshape(2, 3, width, depth), (0, 3, 1, 2)),
        bias_grad,
    )


def solution(mesh):
    in_specs = (
        P("dp", "mp"),
        P("dp"),
        P("dp", "mp"),
        P(None, None, None, "mp"),
        P(None, "mp"),
        P("dp", "mp"),
        P("dp", "mp"),
    )
    out_specs = (
        P("dp", "mp"),
        P("dp", "mp"),
        P("dp", "mp"),
        P("dp", "mp"),
        P(None, None, None, "mp"),
        P(None, "mp"),
    )
    return jax.shard_map(
        on_device, mesh=mesh, in_specs=in_specs, out_specs=out_specs, check_vma=False
    )
```

time: 1630 us -> 724 us (0.44)
  waiting for transfers between devices: 944 us -> 486 us
  other arithmetic: 403 us -> 19.8 us
  local copies, waits for them, and re-layouts: 119 us -> 11.1 us
  Pallas kernels: 0 us -> 64 us
  matrix products: 99.2 us -> 79.5 us
    psum x1, waiting for transfers between devices: 916 us -> 407 us  [on_device(): wgrad = lax.psum(wgrad.astype(jnp.bfloat16), 'dp').astype(jnp.float32)]
    reduce_sum x3 -> x0, other arithmetic: 333 us -> none  [pool_backward(): current = jnp.sum(factors * emit_piece[:, None, :, :], axis=2)]
    pallas_call x0 -> x1, Pallas kernels: none -> 64 us  [pool(): pl.pallas_call(pool_kernel, grid=(width // part,), in_specs=[pl.BlockSpec...]
    another operation x11 -> x0, other arithmetic: 38.1 us -> none  [the longest x1 22.3 us: on_device(): jnp.stack([contract_rows(gathered, gate_grads), contract_rows(shifted, ga...]
    unnamed x3 -> x4, waiting for transfers between devices: 0.71 us -> 36.5 us
    reduce_sum x18 -> x0, local copies, waits for them, and re-layouts: 33.1 us -> none  [the longest x9 16.6 us: pool_backward(): current = jnp.sum(factors * emit_piece[:, None, :, :], axis=2)]
    slice x20 -> x1, local copies, waits for them, and re-layouts: 23.1 us -> 0.34 us  [on_device(): sums[:, 1:2]]
    dot_general x7 -> x3, matrix products: 99.2 us -> 79.5 us  [the longest x1 26.9 us: on_device(): gates = jnp.dot(w_flat, x_all, preferred_element_type=jnp.float32)]
  transfers between devices with their start and end apart: 3 -> 3, of which waited for: 2 -> 3; matrix products, arithmetic and copies ran while one was open for 5% -> 8% of each run, Pallas kernels for 0% -> 0%
where the time goes in v1:
time: 724 us; the launch traced here: 723 us
  waiting for transfers between devices  486 us (67%)
  matrix products  79.5 us (11%)
  Pallas kernels  64 us (9%)
  blocking collectives  47.6 us (7%)
  other arithmetic  19.8 us (3%)
  between operations  14.4 us (2%)
  local copies, waits for them, and re-layouts  11.1 us (2%)
    psum x1, waiting for transfers between devices, on_device(): wgrad = lax.psum(wgrad.astype(jnp.bfloat16), 'dp').astype(jnp.float32)  407 us
    pallas_call x1, Pallas kernels, pool(): pl.pallas_call(pool_kernel, grid=(width // part,), in_specs=[pl.BlockSpec...  64 us
    psum x1, blocking collectives, on_device(): bias_grad = lax.psum(sums[:, 2:5].T, 'dp')  47.6 us
    all_gather x1, waiting for transfers between devices, on_device(): x_all = lax.all_gather(x_own, 'mp', axis=0, tiled=True)  42.9 us
    unnamed x4, waiting for transfers between devices  36.5 us
    dot_general x1, matrix products, on_device(): gates = jnp.dot(w_flat, x_all, preferred_element_type=jnp.float32)  26.9 us
    dot_general x1, matrix products, on_device(): lax.dot_general(gg, x_all, (((1,), (1,)), ((), ())), preferred_element_ty...  26.5 us
    dot_general x1, matrix products, on_device(): lax.dot_general(w_flat, gg, (((0,), (0,)), ((), ())), preferred_element_t...  26.2 us
  transfers between devices with their start and end apart: 3, of which 3 were waited for; matrix products, arithmetic and copies ran while one was open for 8% of the time, Pallas kernels for 0%

profile of v1, /device:TPU:0, one launch (start us, length us, event | category | flops | bytes accessed | tf_op | source)
XLA Modules:
  0.0 723.0 jit_solution(2065666871200115554)
XLA Ops:
  7.2 0.0 all-gather.2.cloned.1.call-start
  7.2 0.7 all-gather.2.cloned.1.call-update
  7.9 0.0 all-reduce.3.cloned.1.call-start
  8.6 0.7 convert_element_type.15
  9.3 0.7 pad_maximum_fusion
  10.0 0.2 copy.23
  10.2 0.0 copy-start
  10.2 42.9 %all-gather.2.cloned.1.call-done = bf16[2304,1152]{1,0:T(8,128)(2,1)} async-done(((bf16[576,1152]{1,0:T(8,128)(2,1)}), bf16[2304,1152]{1,0:T(8,128)(2,1)}) %all-gather.2.cloned.1.call-update) | async-done | bytes 5308432 | tf_op jit(solution)/shard_map/all_gather | solution.py:160
  53.1 26.9 %fusion.2.gates_ref = f32[2,3,576,1152]{3,2,1,0:T(8,128)} fusion(bf16[2,2304,3,576]{1,3,2,0:T(8,128)(2,1)} %param.10, bf16[2304,1152]{1,0:T(8,128)(2,1)} %all-gather.2.cloned.1.call-done), kind=kOutput, calls=%fused_computation.3 | convolution fusion | flops 18345885696 | bytes 37158912 | tf_op jit(solution)/shard_map/dot_general | solution.py:162
  80.0 0.0 copy-done
  80.0 64.0 %pool.1 = (bf16[576,1152]{1,0:T(8,128)(2,1)}, f32[576,128]{1,0:T(8,128)S(1)}, bf16[2,3,576,1152]{3,2,1,0:T(8,128)(2,1)S(1)}) custom-call(s32[1]{0:T(128)S(6)} %copy.32.length_ref, f32[2,3,576,1152]{3,2,1,0:T(8,128)} %fusion.2.gates_ref, f32[576,128]{1,0:T(8,128)S(1)} %pad.4.small_ref, bf16[576,1152]{1,0:T(8,128)(2,1)S(1)} %bitcast.42), custom_call_target="tpu_custom_call" | custom-call | flops 99532800 | bytes 31850496 | tf_op jit(solution)/shard_map/pool/pallas_call | solution.py:123
  144.0 0.0 copy-start.1
  144.0 26.5 %convolution_convert_fusion = bf16[3456,2304]{1,0:T(8,128)(2,1)} fusion(bf16[3456,1152]{1,0:T(8,128)(2,1)S(1)} %bitcast.43, bf16[2304,1152]{1,0:T(8,128)(2,1)} %all-gather.2.cloned.1.call-done), kind=kOutput, calls=%fused_computation | convolution fusion | flops 18353848320 | bytes 29196288 | tf_op jit(solution)/shard_map/dot_general | solution.py:170
  170.5 0.0 copy-done.1
  170.5 0.0 all-reduce.3.cloned.1.call-update
  170.6 0.2 reduce-scatter.4.cloned.1.call-start
  170.8 26.2 %fusion.10 = bf16[2304,1152]{0,1:T(8,128)(2,1)} fusion(bf16[2,3,576,1152]{3,2,1,0:T(8,128)(2,1)} %copy-done.1, bf16[2,2304,3,576]{1,3,2,0:T(8,128)(2,1)} %param.10), kind=kOutput, calls=%fused_computation.7 | convolution fusion | flops 18348539904 | bytes 29196288 | tf_op jit(solution)/shard_map/dot_general | solution.py:166
  196.9 8.6 %copy.28 = bf16[2304,1152]{1,0:T(8,128)(2,1)} copy(bf16[2304,1152]{0,1:T(8,128)(2,1)} %fusion.10) | data formatting | bytes 10616832
  205.5 0.0 reduce-scatter.4.cloned.1.call-update
  205.5 0.1 slice_bitcast_fusion
  205.7 47.6 %psum.15 = f32[3,576]{0,1:T(8,128)S(1)} all-reduce(f32[3,576]{0,1:T(8,128)S(1)} %slice_bitcast_fusion), channel_id=1, replica_groups=mesh['dp'=8,'mp'=4] {'dp'}, use_global_device_ids=true, to_apply=%region_2.3 | all-reduce | flops 1728 | bytes 13824 | tf_op jit(solution)/shard_map/psum | solution.py:172
  253.3 0.7 copy.25
  254.0 0.3 slice_reduce_fusion
  254.4 0.6 transpose.44
  254.9 0.6 transpose.42
  255.5 406.8 %all-reduce.3.cloned.1.call-done = bf16[2,2304,3,576]{1,3,2,0:T(8,128)(2,1)} async-done(((bf16[2,2304,3,576]{1,3,2,0:T(8,128)(2,1)}), bf16[2,2304,3,576]{1,3,2,0:T(8,128)(2,1)}) %all-reduce.3.cloned.1.call-update) | async-done | bytes 15925264 | tf_op jit(solution)/shard_map/psum | solution.py:171
  662.3 18.4 %transpose.46 = f32[2,2304,3,576]{1,3,2,0:T(8,128)} convert(bf16[2,2304,3,576]{1,3,2,0:T(8,128)(2,1)} %all-reduce.3.cloned.1.call-done) | non-fusion elementwise | flops 7962624 | bytes 47775744 | tf_op jit(solution)/shard_map/transpose | solution.py:178
  680.7 35.7 %reduce-scatter.4.cloned.1.call-done = bf16[576,1152]{1,0:T(8,128)(2,1)} async-done(((bf16[2304,1152]{1,0:T(8,128)(2,1)}), bf16[576,1152]{1,0:T(8,128)(2,1)}) %reduce-scatter.4.cloned.1.call-update) | async-done | bytes 1327120
  (1 shorter events, 0.0 us)
Async XLA Ops:
  7.2 45.9 %all-gather.2.cloned.1.call-start = ((), (), s32[]{:S(2)}) async-start(), calls=%async_computation.1 | async-start | bytes 6635520 | tf_op jit(solution)/shard_map/all_gather | solution.py:160
  7.9 654.4 %all-reduce.3.cloned.1.call-start = ((), (), s32[]{:S(2)}) async-start(), calls=%async_computation.2 | async-start | bytes 31850496 | tf_op jit(solution)/shard_map/psum | solution.py:171
  10.2 69.8 %copy-start = (bf16[1152,576]{0,1:T(8,128)(2,1)S(1)}, bf16[1152,576]{0,1:T(8,128)(2,1)}, u32[]{:S(2)}) copy-start(bf16[1152,576]{0,1:T(8,128)(2,1)} %param.12) | copy-start | bytes 3981316
  144.0 26.5 %copy-start.1 = (bf16[2,3,576,1152]{3,2,1,0:T(8,128)(2,1)}, bf16[2,3,576,1152]{3,2,1,0:T(8,128)(2,1)S(1)}, u32[]{:S(2)}) copy-start(bf16[2,3,576,1152]{3,2,1,0:T(8,128)(2,1)S(1)} %get-tuple-element.11) | copy-start | bytes 23887876
  170.6 545.9 %reduce-scatter.4.cloned.1.call-start = ((), (), s32[]{:S(2)}) async-start(), calls=%async_computation.3 | async-start | bytes 6635520
Sparse Core Ops, SparseCore 0:
  9.6 43.4 all-gather.1
  170.7 491.5 all-reduce.2
  665.6 50.8 reduce-scatter.3

commit v2 on v1

v2 whole, which is shorter than its diff:
```python
import functools

import jax
import jax.numpy as jnp
from jax import lax
from jax.experimental import pallas as pl
from jax.experimental.pallas import tpu as pltpu
from jax.sharding import PartitionSpec as P

LANES = 128
ROWS = 16
CHUNKS = 18
LAG = 4
HIDDEN_COST = pl.CostEstimate(flops=1, bytes_accessed=1, transcendentals=0)


def pool_kernel(length_ref, gates_ref, small_ref, grad_ref, hidden_ref, sums_ref, gg_ref, held):
    part, span = grad_ref.shape
    tiles = span // LANES
    length = length_ref[0]
    lane = lax.broadcasted_iota(jnp.int32, (ROWS, LANES), 1)
    zero = jnp.zeros((ROWS, LANES), jnp.float32)
    one = zero + 1.0
    first_lane = lane == 0
    last_lane = lane == LANES - 1
    cand_at, forget_at, out_at = 0, 1, 2
    run_at, back_at, decay_at = 0, 1, 2
    held_gates, held_runs = held

    def tile_of(j):
        return pl.ds(j * LANES, LANES)

    def is_live(j):
        return lane * tiles + j < length

    def local(step, unused):
        rows = pl.ds(pl.multiple_of(step * ROWS, ROWS), ROWS)
        small = small_ref[rows, :]
        bias = [jnp.broadcast_to(small[:, k : k + 1], (ROWS, LANES)) for k in range(3)]
        end_grad = jnp.where(last_lane, jnp.broadcast_to(small[:, 4:5], (ROWS, LANES)), 0.0)
        earlier = [
            jnp.where(first_lane, 0.0, pltpu.roll(gates_ref[1, k, rows, tile_of(tiles - 1)], 1, 1))
            for k in range(3)
        ]
        run, product, back = zero, one, zero
        for j in range(tiles):
            gates = []
            for k in range(3):
                gates.append(gates_ref[0, k, rows, tile_of(j)] + earlier[k] + bias[k])
                earlier[k] = gates_ref[1, k, rows, tile_of(j)]
            live = is_live(j)
            cand = jnp.tanh(gates[0])
            forget = jax.nn.sigmoid(gates[1])
            out_gate = jnp.where(live, jax.nn.sigmoid(gates[2]), 0.0)
            kept = jnp.where(live, 1.0 - forget, 0.0)
            decay = 1.0 - kept
            emitted = out_gate * grad_ref[rows, tile_of(j)].astype(jnp.float32)
            if j == tiles - 1:
                emitted = emitted + end_grad
            run = decay * run + kept * cand
            product = product * decay
            back = back + product * emitted
            held_gates[cand_at, rows, tile_of(j)] = cand
            held_gates[forget_at, rows, tile_of(j)] = forget
            held_gates[out_at, rows, tile_of(j)] = out_gate
        held_runs[run_at, rows, :] = run
        held_runs[back_at, rows, :] = back
        held_runs[decay_at, rows, :] = product
        return unused

    lax.fori_loop(0, part // ROWS, local, 0)

    wide = lax.broadcasted_iota(jnp.int32, (part, LANES), 1)
    begin = jnp.broadcast_to(small_ref[:, 3:4], (part, LANES))
    run, back, product = held_runs[run_at], held_runs[back_at], held_runs[decay_at]
    run = jnp.where(wide == 0, run + product * begin, run)
    up = product
    for k in (1, 2, 4, 8, 16, 32, 64):
        inside = wide >= k
        run = run + up * jnp.where(inside, pltpu.roll(run, k, 1), 0.0)
        up = up * jnp.where(inside, pltpu.roll(up, k, 1), 1.0)
        inside = wide < LANES - k
        back = back + product * jnp.where(inside, pltpu.roll(back, LANES - k, 1), 0.0)
        product = product * jnp.where(inside, pltpu.roll(product, LANES - k, 1), 1.0)
    held_runs[run_at] = jnp.where(wide == 0, begin, pltpu.roll(run, 1, 1))
    held_runs[decay_at] = jnp.where(wide == LANES - 1, 0.0, pltpu.roll(back, LANES - 1, 1))
    last_cell = jnp.broadcast_to(run[:, LANES - 1 :], (part, LANES))
    sums_ref[...] = jnp.where(wide == 0, last_cell, 0.0) + jnp.where(
        wide == 1, jnp.broadcast_to(back[:, :1], (part, LANES)), 0.0
    )

    def final(step, unused):
        rows = pl.ds(pl.multiple_of(step * ROWS, ROWS), ROWS)
        small = small_ref[rows, :]
        end_grad = jnp.where(last_lane, jnp.broadcast_to(small[:, 4:5], (ROWS, LANES)), 0.0)
        before = held_runs[run_at, rows, :]
        cells, befores = [], []
        for j in range(tiles):
            cand = held_gates[cand_at, rows, tile_of(j)]
            kept = jnp.where(is_live(j), 1.0 - held_gates[forget_at, rows, tile_of(j)], 0.0)
            cell = (1.0 - kept) * before + kept * cand
            befores.append(before)
            cells.append(cell)
            before = cell
        follow = held_runs[decay_at, rows, :]
        bias_sum = [zero] * 3
        for j in range(tiles - 1, -1, -1):
            cand = held_gates[cand_at, rows, tile_of(j)]
            forget = held_gates[forget_at, rows, tile_of(j)]
            out_gate = held_gates[out_at, rows, tile_of(j)]
            kept = jnp.where(is_live(j), 1.0 - forget, 0.0)
            emitted = out_gate * grad_ref[rows, tile_of(j)].astype(jnp.float32)
            hidden_ref[rows, tile_of(j)] = (out_gate * cells[j]).astype(jnp.bfloat16)
            out_part = emitted * cells[j] * (1.0 - out_gate)
            if j == tiles - 1:
                emitted = emitted + end_grad
            cell_grad = emitted + follow
            follow = (1.0 - kept) * cell_grad
            shared = cell_grad * kept
            parts = [
                shared * (1.0 - cand * cand),
                shared * (befores[j] - cand) * forget,
                out_part,
            ]
            for k in range(3):
                rounded = parts[k].astype(jnp.bfloat16)
                gg_ref[0, k, rows, tile_of(j)] = rounded
                wide_part = rounded.astype(jnp.float32)
                bias_sum[k] = bias_sum[k] + wide_part
                if j > 0:
                    gg_ref[1, k, rows, tile_of(j - 1)] = rounded
                else:
                    moved = jnp.where(last_lane, 0.0, pltpu.roll(wide_part, LANES - 1, 1))
                    gg_ref[1, k, rows, tile_of(tiles - 1)] = moved.astype(jnp.bfloat16)
        answer = sums_ref[rows, :]
        for k in range(3):
            total = jnp.sum(bias_sum[k], axis=1, keepdims=True)
            answer = jnp.where(lane == 2 + k, jnp.broadcast_to(total, (ROWS, LANES)), answer)
        sums_ref[rows, :] = answer
        return unused

    lax.fori_loop(0, part // ROWS, final, 0)


def pool(length, gates, small, grad):
    taps, kinds, width, span = gates.shape
    part = next(p for p in (96, 48, 16) if width % p == 0)
    return pl.pallas_call(
        lambda *refs: pool_kernel(*refs[:-2], refs[-2:]),
        grid=(width // part,),
        in_specs=[
            pl.BlockSpec(memory_space=pltpu.SMEM),
            pl.BlockSpec((2, 3, part, span), lambda i: (0, 0, i, 0)),
            pl.BlockSpec((part, LANES), lambda i: (i, 0)),
            pl.BlockSpec((part, span), lambda i: (i, 0)),
        ],
        out_specs=[
            pl.BlockSpec((part, span), lambda i: (i, 0)),
            pl.BlockSpec((part, LANES), lambda i: (i, 0)),
            pl.BlockSpec((2, 3, part, span), lambda i: (0, 0, i, 0)),
        ],
        out_shape=[
            jax.ShapeDtypeStruct((width, span), jnp.bfloat16),
            jax.ShapeDtypeStruct((width, LANES), jnp.float32),
            jax.ShapeDtypeStruct((2, 3, width, span), jnp.bfloat16),
        ],
        scratch_shapes=[
            pltpu.VMEM((3, part, span), jnp.float32),
            pltpu.VMEM((3, part, LANES), jnp.float32),
        ],
        compiler_params=pltpu.CompilerParams(vmem_limit_bytes=40 * 2**20),
        cost_estimate=HIDDEN_COST,
        name="pool",
    )(length, gates, small, grad)


def small_columns(bias, start_cell, cell_grad):
    stacked = jnp.concatenate([bias.astype(jnp.float32), start_cell, cell_grad], axis=0)
    return jnp.pad(stacked.T, ((0, 0), (0, LANES - 5)))


def slot_order(span):
    tiles = span // LANES
    slot = lax.broadcasted_iota(jnp.int32, (span, span), 0)
    place = lax.broadcasted_iota(jnp.int32, (span, span), 1)
    return (place == (slot % tiles) * LANES + slot // tiles).astype(jnp.bfloat16)


def mix(block, order, back=False):
    dims = (((1,), (1 if back else 0,)), ((), ()))
    return lax.dot_general(block, order, dims, preferred_element_type=jnp.float32).astype(jnp.bfloat16)


def times(left, right):
    return jnp.dot(left, right, preferred_element_type=jnp.float32)


def rows_dot(left, right):
    return lax.dot_general(left, right, (((0,), (0,)), ((), ())), preferred_element_type=jnp.float32)


def cols_dot(left, right):
    return lax.dot_general(left, right, (((1,), (1,)), ((), ())), preferred_element_type=jnp.float32)


def once(shape):
    zeros = (0,) * len(shape)
    return pl.BlockSpec(shape, lambda *at: zeros, pipeline_mode=pl.Buffered(1))


def gates_kernel(pick_ref, low_ref, high_ref, w_ref, *refs):
    base_ref = refs[0] if len(refs) == 3 else None
    out_ref, x_ref = refs[-2:]
    half_rows = low_ref.shape[0]

    @pl.when(pl.program_id(0) == 0)
    def _():
        at = pl.multiple_of(pick_ref[2] * half_rows, 64)
        x_ref[pl.ds(at, half_rows), :] = low_ref[...]
        at = pl.multiple_of((1 - pick_ref[2]) * half_rows, 64)
        x_ref[pl.ds(at, half_rows), :] = high_ref[...]

    kinds, width = w_ref.shape[1:3]
    weights = w_ref[0].reshape(kinds * width, w_ref.shape[3])
    total = jnp.dot(weights, x_ref[...], preferred_element_type=jnp.float32)
    total = total.reshape(out_ref.shape)
    if base_ref is not None:
        total = total + base_ref[...]
    out_ref[...] = total


def gates_step(pick, w_rows, own, sibling, base=None):
    taps, kinds, width, depth = w_rows.shape
    rows, span = own.shape
    block = lambda: pl.BlockSpec((1, kinds, width // 2, span), lambda g, p: (g, 0, 0, 0))
    specs = [
        once((rows, span)),
        once((rows, span)),
        pl.BlockSpec((1, kinds, width // 2, 2 * rows), lambda g, p: (g, 0, p[0], p[1])),
    ]
    operands = [own, sibling, w_rows]
    if base is not None:
        specs.append(block())
        operands.append(base)
    return pl.pallas_call(
        gates_kernel,
        grid_spec=pltpu.PrefetchScalarGridSpec(
            num_scalar_prefetch=1,
            grid=(taps,),
            in_specs=specs,
            out_specs=[block(), pl.BlockSpec((2 * rows, span), lambda g, p: (0, 0))],
        ),
        out_shape=[
            jax.ShapeDtypeStruct((taps, kinds, width // 2, span), jnp.float32),
            jax.ShapeDtypeStruct((2 * rows, span), jnp.bfloat16),
        ],
        compiler_params=pltpu.CompilerParams(vmem_limit_bytes=48 * 2**20),
        cost_estimate=HIDDEN_COST,
        name="gates_step",
    )(pick, *operands)


def gates_both_kernel(pick_ref, near_ref, far_ref, w_near_ref, w_far_ref, out_ref):
    kinds, width, rows = w_near_ref.shape[1:]

    def product(w_ref, x_ref):
        weights = w_ref[0].reshape(kinds * width, rows)
        return jnp.dot(weights, x_ref[...], preferred_element_type=jnp.float32)

    total = product(w_near_ref, near_ref) + product(w_far_ref, far_ref)
    out_ref[...] = total.reshape(out_ref.shape)


def gates_both(pick, w_rows, near, far):
    taps, kinds, width, depth = w_rows.shape
    rows, span = near.shape
    return pl.pallas_call(
        gates_both_kernel,
        grid_spec=pltpu.PrefetchScalarGridSpec(
            num_scalar_prefetch=1,
            grid=(taps,),
            in_specs=[
                once((rows, span)),
                once((rows, span)),
                pl.BlockSpec((1, kinds, width // 2, rows), lambda g, p: (g, 0, p[0], p[1])),
                pl.BlockSpec((1, kinds, width // 2, rows), lambda g, p: (g, 0, p[0], 1 - p[1])),
            ],
            out_specs=pl.BlockSpec((1, kinds, width // 2, span), lambda g, p: (g, 0, 0, 0)),
        ),
        out_shape=jax.ShapeDtypeStruct((taps, kinds, width // 2, span), jnp.float32),
        compiler_params=pltpu.CompilerParams(vmem_limit_bytes=48 * 2**20),
        cost_estimate=HIDDEN_COST,
        name="gates_both",
    )(pick, near, far, w_rows, w_rows)


def back_kernel(pick_ref, w_ref, mine_ref, other_ref, keep_ref, give_ref, total_ref):
    step = pl.program_id(0)
    kinds, width, columns = w_ref.shape[1:]
    weights = w_ref[0].reshape(kinds * width, columns)

    def add(grads):
        product = lax.dot_general(
            weights, grads, (((0,), (0,)), ((), ())), preferred_element_type=jnp.float32
        )

        @pl.when(step == 0)
        def _():
            total_ref[...] = product

        @pl.when(step > 0)
        def _():
            total_ref[...] += product

    @pl.when(step % 2 == 0)
    def _():
        add(mine_ref[0].reshape(kinds * width, mine_ref.shape[-1]))

    @pl.when(step % 2 == 1)
    def _():
        add(other_ref[0].reshape(kinds * width, other_ref.shape[-1]))

    @pl.when(step == pl.num_programs(0) - 1)
    def _():
        rows = keep_ref.shape[0]
        keep_ref[...] = total_ref[pl.ds(pl.multiple_of(pick_ref[2] * rows, 64), rows), :]
        give_ref[...] = total_ref[
            pl.ds(pl.multiple_of((1 - pick_ref[2]) * rows, 64), rows), :
        ].astype(jnp.bfloat16)


def back_products(pick, w_rows, mine, other):
    taps, kinds, width, depth = w_rows.shape
    span = mine.shape[-1]
    columns = depth // 2
    grads = pl.BlockSpec((1, kinds, width // 2, span), lambda i, p: (i // 2, 0, 0, 0))
    return pl.pallas_call(
        back_kernel,
        grid_spec=pltpu.PrefetchScalarGridSpec(
            num_scalar_prefetch=1,
            grid=(2 * taps,),
            in_specs=[
                pl.BlockSpec(
                    (1, kinds, width // 2, columns),
                    lambda i, p: (i // 2, 0, jnp.where(i % 2 == 0, p[0], 1 - p[0]), p[1]),
                ),
                grads,
                grads,
            ],
            out_specs=[
                pl.BlockSpec((columns // 2, span), lambda i, p: (0, 0)),
                pl.BlockSpec((columns // 2, span), lambda i, p: (0, 0)),
            ],
            scratch_shapes=[pltpu.VMEM((columns, span), jnp.float32)],
        ),
        out_shape=[
            jax.ShapeDtypeStruct((columns // 2, span), jnp.float32),
            jax.ShapeDtypeStruct((columns // 2, span), jnp.bfloat16),
        ],
        compiler_params=pltpu.CompilerParams(vmem_limit_bytes=48 * 2**20),
        cost_estimate=HIDDEN_COST,
        name="back_products",
    )(pick, w_rows, mine, other)


def weight_kernel(mine_ref, pair_ref, near_ref, far_ref, pair_near_ref, pair_far_ref, out_ref):
    def product(gg_ref, x_ref):
        return lax.dot_general(
            gg_ref[...], x_ref[...], (((1,), (1,)), ((), ())), preferred_element_type=jnp.float32
        )

    middle = near_ref.shape[0]
    out_ref[:, :middle] = (
        product(mine_ref, near_ref) + product(pair_ref, pair_near_ref)
    ).astype(jnp.bfloat16)
    out_ref[:, middle:] = (
        product(mine_ref, far_ref) + product(pair_ref, pair_far_ref)
    ).astype(jnp.bfloat16)


def weight_products(gg_mine, gg_pair, near, far, pair_near, pair_far, block, first, last):
    rows, span = gg_mine.shape
    columns = near.shape[0]
    grads = pl.BlockSpec((block, span), lambda i: (i + first, 0))
    return pl.pallas_call(
        weight_kernel,
        grid=(last - first,),
        in_specs=[grads, grads] + [once((columns, span))] * 4,
        out_specs=pl.BlockSpec((block, 2 * columns), lambda i: (i, 0)),
        out_shape=jax.ShapeDtypeStruct(((last - first) * block, 2 * columns), jnp.bfloat16),
        compiler_params=pltpu.CompilerParams(vmem_limit_bytes=48 * 2**20),
        cost_estimate=HIDDEN_COST,
        name="weight_products",
    )(gg_mine, gg_pair, near, far, pair_near, pair_far)


def even_odd(count):
    return [(i, i ^ 1) for i in range(count)]


def line_pairs(moves):
    return [(2 * a + s, 2 * b + s) for a, b in moves for s in range(2)]


class Order:
    def __init__(self, token):
        self.token = token

    def __call__(self, values):
        values, self.token = lax.optimization_barrier((values, self.token))
        return values


def line_sum(part, length):
    if length & (length - 1) == 0:
        step = 1
        while step < length:
            part = part + lax.ppermute(part, "dp", line_pairs([(i, i ^ step) for i in range(length)]))
            step *= 2
        return part
    total = part
    for _ in range(length - 1):
        part = lax.ppermute(part, "dp", line_pairs([(i, (i + 1) % length) for i in range(length)]))
        total = total + part
    return total


def half(array, axis, which):
    size = array.shape[axis] // 2
    return lax.dynamic_slice_in_dim(array, which * size, size, axis)


def join(low_first, mine, other, axis):
    return jnp.where(
        low_first,
        jnp.concatenate([mine, other], axis=axis),
        jnp.concatenate([other, mine], axis=axis),
    )


def write_kernel(count, flags_ref, *refs):
    out_ref = refs[-1]
    size = refs[0].shape[0]
    middle = refs[0].shape[1] // 2
    mine = flags_ref[0] == pl.program_id(0)
    straight = flags_ref[1] == 0
    for j in range(count):
        at = pl.ds(j * size, size)
        block = jnp.where(mine, refs[j][...], refs[count + j][...]).astype(jnp.float32)
        left, right = block[:, :middle], block[:, middle:]
        out_ref[at, :middle] = jnp.where(straight, left, right)
        out_ref[at, middle:] = jnp.where(straight, right, left)


def write_chunks(flags, mine, theirs, group, whole, shape):
    count = len(mine)
    size, depth = mine[0].shape
    specs = [pl.BlockSpec(memory_space=pltpu.SMEM)]
    specs += [pl.BlockSpec((size, depth), lambda i: (0, 0))] * (2 * count)
    operands = [flags, *mine, *theirs]
    aliases = {}
    if whole is not None:
        specs.append(pl.BlockSpec(memory_space=pl.ANY))
        operands.append(whole)
        aliases = {len(operands) - 1: 0}
    return pl.pallas_call(
        functools.partial(write_kernel, count),
        grid=(2,),
        in_specs=specs,
        out_specs=pl.BlockSpec((count * size, depth), lambda i: (2 * group + i, 0)),
        out_shape=jax.ShapeDtypeStruct(shape, jnp.float32),
        input_output_aliases=aliases,
        compiler_params=pltpu.CompilerParams(vmem_limit_bytes=40 * 2**20),
        cost_estimate=HIDDEN_COST,
        name="write_chunks",
    )(*operands)


def add_times(total, left, right):
    return total + times(left, right)


def add_rounded(left, right):
    return (left.astype(jnp.float32) + right.astype(jnp.float32)).astype(jnp.bfloat16)


def piped_sums(order, chunks, pairs, fillers, arrived):
    position = lax.axis_index("dp") // 2
    inner = (position == 1) | (position == 2)
    edge = line_pairs([(0, 1), (1, 0), (2, 3), (3, 2)])
    middle = line_pairs([(1, 2), (2, 1)])
    sums, totals, finals, swapped = {}, {}, {}, {}
    got_edge, got_middle, got_pair = {}, {}, {}
    for n in range(CHUNKS + LAG + 3):
        k = n - 3
        if 0 <= k < CHUNKS:
            got = order(got_middle.pop(k))
            totals[k] = order(add_rounded(sums.pop(k), got))
        k = n - LAG
        if n < CHUNKS and 0 <= k < CHUNKS:
            payload = jnp.where(inner, totals[k], chunks[n])
        elif n < CHUNKS:
            payload = chunks[n]
        elif 0 <= k < CHUNKS:
            payload = totals[k]
        else:
            payload = None
        if payload is not None:
            got_edge[n] = lax.ppermute(order(payload), "dp", edge)
        if n in fillers:
            fillers[n]()
        k = n - 1
        if k in got_edge:
            got = order(got_edge.pop(k))
            if k < CHUNKS:
                sums[k] = order(add_rounded(chunks.pop(k), got))
                got_middle[k] = lax.ppermute(sums[k], "dp", middle)
            k = k - LAG
            if 0 <= k < CHUNKS:
                finals[k] = order(jnp.where(inner, totals.pop(k), got))
                got_pair[k] = lax.ppermute(finals[k], "dp", pairs)
        k = n - LAG - 3
        if 0 <= k < CHUNKS:
            swapped[k] = order(got_pair.pop(k))
            arrived(k, finals, swapped)
    for k in sorted(got_pair):
        swapped[k] = order(got_pair.pop(k))
        arrived(k, finals, swapped)


def on_device(line, channel_parts, inputs, lengths, start_cell, weight, bias, out_grad, cell_grad):
    span, width = inputs.shape
    depth = weight.shape[1]
    own = width // 2
    rows = 6 * own
    side = lax.axis_index("dp") % 2
    other_side = 1 - side
    is_low = side == 0
    pairs = even_odd(2 * line)
    slots = slot_order(span)

    place = lax.axis_index("mp")
    core_low = place % 2 == 0
    near_low = place < 2
    core_pairs = even_odd(channel_parts)
    chip_pairs = [(i, i ^ 2) for i in range(4)]

    def split(array, axis):
        return half(array, axis, place // 2), half(array, axis, 1 - place // 2)

    small = small_columns(bias, start_cell, cell_grad)
    lane = lax.broadcasted_iota(jnp.int32, small.shape, 1)
    small = jnp.where(lane == 5, lengths[0].astype(jnp.float32), small)
    small_mine, small_other = half(small, 0, side), half(small, 0, other_side)
    w_rows = jnp.transpose(weight, (0, 2, 3, 1))

    def pooled(total, length, small_part, grad_part):
        hidden, sums, gg = pool(length, total.reshape(2, 3, own, span), small_part, grad_part)
        return hidden, sums, gg.reshape(rows, span)

    if line == 4 and channel_parts == 4:
        done = Order(small_mine)

        def run(function, *operands):
            return done(function(*done(operands)))

        pick_mine = jnp.stack([side, place // 2, place % 2]).astype(jnp.int32)
        pick_mine_far = jnp.stack([side, 1 - place // 2, place % 2]).astype(jnp.int32)
        pick_other = jnp.stack([other_side, place // 2, place % 2]).astype(jnp.int32)
        x_own = run(lambda x: mix(x.T, slots), inputs)
        far_got = lax.ppermute(x_own, "mp", chip_pairs)
        pair_got = lax.ppermute(x_own, "dp", pairs)
        near_got = lax.ppermute(x_own, "mp", core_pairs)
        grads = run(lambda g: mix(g.T, slots), out_grad)
        grads_mine, grads_other = done((half(grads, 0, side), half(grads, 0, other_side)))
        gates, near = run(gates_step, pick_mine, w_rows, x_own, near_got)
        far_own = done(far_got)
        far_got = lax.ppermute(far_own, "mp", core_pairs)
        x_pair = done(pair_got)
        pair_far_got = lax.ppermute(x_pair, "mp", chip_pairs)
        grads_pair = lax.ppermute(grads_other, "dp", pairs)
        small_pair = lax.ppermute(small_other, "dp", pairs)
        far_got = done(far_got)
        pair_near_got = lax.ppermute(done(x_pair), "mp", core_pairs)
        gates, far = run(gates_step, pick_mine_far, w_rows, far_own, far_got, gates)
        pair_gates, pair_near = run(gates_step, pick_mine, w_rows, x_pair, pair_near_got)
        gates, grads_mine = done((gates, grads_mine))
        hidden_mine, sums_mine, gg_mine = pooled(gates, lengths, done.token, grads_mine)
        done.token = sums_mine
        gg_mine = done(gg_mine)
        pair_far_own = done(pair_far_got)
        pair_far_got = lax.ppermute(pair_far_own, "mp", core_pairs)
        gates_other = run(gates_both, pick_other, w_rows, near, far)
        pair_gates, pair_far = run(
            gates_step, pick_mine_far, w_rows, pair_far_own, pair_far_got, pair_gates
        )
        small_pair, grads_pair = done((small_pair, grads_pair))
        length_pair = small_pair[0, 5:6].astype(jnp.int32)
        small_pair = jnp.where(lane[:own] < 3, small_mine, small_pair)
        _, sums_pair, gg_pair = run(pooled, pair_gates, length_pair, small_pair, grads_pair)

        size = rows // CHUNKS
        chunks = {}

        def products(first, last):
            def fill():
                part = run(
                    lambda *at: weight_products(*at, own, first, last),
                    gg_mine,
                    gg_pair,
                    near,
                    far,
                    pair_near,
                    pair_far,
                )
                for k in range(first * per, last * per):
                    at = (k - first * per) * size
                    chunks[k] = part[at : at + size]

            return fill

        kept = {}

        def fill_pool():
            kept["pool"] = run(pooled, gates_other, lengths, small_other, grads_other)

        def fill_back(part):
            def stage():
                keep, give = run(
                    back_products,
                    (pick_mine, pick_mine_far)[part],
                    w_rows,
                    gg_mine.reshape(2, 3, own, span),
                    kept["pool"][2].reshape(2, 3, own, span),
                )
                kept["keep", part] = keep
                kept["got", part] = lax.ppermute(give, "mp", core_pairs)

            return stage

        def fill_cross():
            far_sum = run(
                lambda a, b: (a + b.astype(jnp.float32)).astype(jnp.bfloat16),
                kept["keep", 1],
                kept["got", 1],
            )
            kept["cross"] = lax.ppermute(far_sum, "mp", chip_pairs)

        def fill_input():
            def total(a, b, c):
                total = a + b.astype(jnp.float32) + c.astype(jnp.float32)
                return mix(total.astype(jnp.bfloat16), slots, back=True).T

            kept["input"] = run(total, kept["keep", 0], kept["got", 0], kept["cross"])

        def fill_hidden():
            def whole(mine, other):
                return mix(join(is_low, mine, other, 0), slots, back=True).T

            kept["hidden"] = run(whole, hidden_mine, kept["pool"][0])

        per = own // size
        bias_sums = run(jnp.add, sums_mine, sums_pair)
        position = lax.axis_index("dp") // 2
        inner = (position == 1) | (position == 2)

        def fill_bias(stage):
            def run_stage():
                if stage == 0:
                    kept["bias"] = done(bias_sums)
                    moves = [(0, 1), (1, 0), (2, 3), (3, 2)]
                elif stage == 1:
                    kept["bias"] = run(jnp.add, kept["bias"], kept["bias got"])
                    moves = [(1, 2), (2, 1)]
                elif stage == 2:
                    kept["bias"] = run(jnp.add, kept["bias"], kept["bias got"])
                    moves = [(1, 0), (2, 3), (0, 1), (3, 2)]
                elif stage == 3:
                    kept["bias"] = run(
                        lambda a, b: jnp.where(inner, a, b), kept["bias"], kept["bias got"]
                    )
                if stage < 3:
                    kept["bias got"] = lax.ppermute(kept["bias"], "dp", line_pairs(moves))
                elif stage == 3:
                    kept["bias got"] = lax.ppermute(kept["bias"], "dp", pairs)
                else:
                    kept["bias got"] = done(kept["bias got"])

            return run_stage

        flags = jnp.stack([side, place // 2]).astype(jnp.int32)
        kept["out"] = None

        def arrived(k, finals, swapped):
            group = k // per
            members = range(group * per, (group + 1) * per)
            if k == members[-1]:
                parts = done(([finals[m] for m in members], [swapped[m] for m in members]))
                kept["out"] = done(write_chunks(flags, *parts, group, kept["out"], (2 * rows, depth)))

        products(0, 1)()
        fillers = {
            1: products(1, 3),
            2: fill_pool,
            3: fill_back(1),
            4: products(3, 6),
            5: fill_back(0),
            6: fill_cross,
            7: fill_bias(0),
            8: fill_hidden,
            9: fill_bias(1),
            11: fill_input,
            12: fill_bias(2),
            14: fill_bias(3),
            16: fill_bias(4),
        }
        piped_sums(done, chunks, pairs, fillers, arrived)
        hidden_other, sums_other, _ = kept["pool"]
        input_grad, hidden = kept["input"], kept["hidden"]
        wgrad = kept["out"].reshape(2, 3, width, depth)
        bias_grad = join(is_low, kept["bias"], kept["bias got"], 0)[:, 2:5].T
        sums_mine = done.token
    else:
        x_own = mix(inputs.T, slots)
        grads = mix(out_grad.T, slots)
        grads_mine, grads_other = half(grads, 0, side), half(grads, 0, other_side)
        grads_pair = lax.ppermute(grads_other, "dp", pairs)
        small_pair = lax.ppermute(small_other, "dp", pairs)
        length_pair = small_pair[0, 5:6].astype(jnp.int32)
        small_pair = jnp.where(lane[:own] < 3, small_mine, small_pair)
        x_all = lax.all_gather(x_own, "mp", axis=0, tiled=True)
        x_pair = lax.all_gather(lax.ppermute(x_own, "dp", pairs), "mp", axis=0, tiled=True)
        w_mine = half(w_rows, 2, side).reshape(rows, depth)
        w_other = half(w_rows, 2, other_side).reshape(rows, depth)
        hidden_mine, sums_mine, gg_mine = pooled(
            times(w_mine, x_all), lengths, small_mine, grads_mine
        )
        _, sums_pair, gg_pair = pooled(times(w_mine, x_pair), length_pair, small_pair, grads_pair)
        hidden_other, sums_other, gg_other = pooled(
            times(w_other, x_all), lengths, small_other, grads_other
        )
        part = cols_dot(gg_mine, x_all) + cols_dot(gg_pair, x_pair)
        total = line_sum(part.astype(jnp.bfloat16), line)
        theirs = lax.ppermute(total, "dp", pairs)
        shape = (2, 3, own, depth)
        wgrad = join(is_low, total.reshape(shape), theirs.reshape(shape), 2).astype(jnp.float32)
        back = rows_dot(w_mine, gg_mine) + rows_dot(w_other, gg_other)
        input_grad = lax.psum_scatter(
            back.astype(jnp.bfloat16), "mp", scatter_dimension=0, tiled=True
        )
        input_grad = mix(input_grad, slots, back=True).T
        hidden = mix(join(is_low, hidden_mine, hidden_other, 0), slots, back=True).T
        bias_mine = line_sum(sums_mine + sums_pair, line)
        bias_pair = lax.ppermute(bias_mine, "dp", pairs)
        bias_grad = join(is_low, bias_mine, bias_pair, 0)[:, 2:5].T

    sums = join(is_low, sums_mine, sums_other, 0)
    return (
        hidden,
        sums[:, 0:1].T,
        input_grad,
        sums[:, 1:2].T,
        jnp.transpose(wgrad, (0, 3, 1, 2)),
        bias_grad,
    )


def solution(mesh):
    in_specs = (
        P("dp", "mp"),
        P("dp"),
        P("dp", "mp"),
        P(None, None, None, "mp"),
        P(None, "mp"),
        P("dp", "mp"),
        P("dp", "mp"),
    )
    out_specs = (
        P("dp", "mp"),
        P("dp", "mp"),
        P("dp", "mp"),
        P("dp", "mp"),
        P(None, None, None, "mp"),
        P(None, "mp"),
    )
    body = functools.partial(on_device, mesh.shape["dp"] // 2, mesh.shape["mp"])
    return jax.shard_map(
        body, mesh=mesh, in_specs=in_specs, out_specs=out_specs, check_vma=False
    )
```

time: 724 us -> 494 us (0.68)
  waiting for transfers between devices: 486 us -> 102 us
  starting transfers between devices: 0.3 us -> 137 us
  Pallas kernels: 64 us -> 185 us
  matrix products: 79.5 us -> 15 us
  blocking collectives: 47.6 us -> 0 us
  local copies, waits for them, and re-layouts: 11.1 us -> 33.8 us
  between operations: 14.4 us -> 3.42 us
  other arithmetic: 19.8 us -> 11.5 us
    psum x1 -> x0, waiting for transfers between devices: 407 us -> none  [on_device(): wgrad = lax.psum(wgrad.astype(jnp.bfloat16), 'dp').astype(jnp.float32)]
    ppermute x0 -> x74, starting transfers between devices: none -> 137 us  [the longest x22 91.4 us: piped_sums(): got_edge[n] = lax.ppermute(order(payload), 'dp', edge)]
    pallas_call x1 -> x19, Pallas kernels: 64 us -> 185 us  [the longest x4 46.1 us: gates_step(): pl.pallas_call(gates_kernel, grid_spec=pltpu.PrefetchScalarGridSpec(num_s...]
    ppermute x0 -> x74, waiting for transfers between devices: none -> 102 us  [the longest x22 69.4 us: piped_sums(): got_edge[n] = lax.ppermute(order(payload), 'dp', edge)]
    dot_general x3 -> x4, matrix products: 79.5 us -> 15 us  [mix(): lax.dot_general(block, order, dims, preferred_element_type=jnp.float32)]
    psum x1 -> x0, blocking collectives: 47.6 us -> none  [on_device(): bias_grad = lax.psum(sums[:, 2:5].T, 'dp')]
    all_gather x1 -> x0, waiting for transfers between devices: 42.9 us -> none  [on_device(): x_all = lax.all_gather(x_own, 'mp', axis=0, tiled=True)]
    unnamed x4 -> x0, waiting for transfers between devices: 36.5 us -> none
  transfers between devices with their start and end apart: 3 -> 74, of which waited for: 3 -> 21; matrix products, arithmetic and copies ran while one was open for 8% -> 4% of each run, Pallas kernels for 0% -> 34%
where the time goes in v2:
time: 494 us; the launch traced here: 488 us
  Pallas kernels  185 us (37%)
  starting transfers between devices  137 us (28%)
  waiting for transfers between devices  102 us (21%)
  local copies, waits for them, and re-layouts  33.8 us (7%)
  matrix products  15 us (3%)
  other arithmetic  11.5 us (2%)
    ppermute x22, starting transfers between devices, piped_sums(): got_edge[n] = lax.ppermute(order(payload), 'dp', edge)  91.4 us
    ppermute x22, waiting for transfers between devices, piped_sums(): got_edge[n] = lax.ppermute(order(payload), 'dp', edge)  69.4 us
    pallas_call x4, Pallas kernels, gates_step(): pl.pallas_call(gates_kernel, grid_spec=pltpu.PrefetchScalarGridSpec(num_s...  46.1 us
    pallas_call x2, Pallas kernels, back_products(): pl.pallas_call(back_kernel, grid_spec=pltpu.PrefetchScalarGridSpec(num_sc...  38.5 us
    pallas_call x3, Pallas kernels, weight_products(): pl.pallas_call(weight_kernel, grid=(last - first,), in_specs=[grads, grad...  35.8 us
    pallas_call x3, Pallas kernels, pool(): pl.pallas_call(lambda *refs: pool_kernel(*refs[:-2], refs[-2:]), grid=(wi...  28.5 us
    unnamed x87, local copies, waits for them, and re-layouts  28 us
    pallas_call x6, Pallas kernels, write_chunks(): pl.pallas_call(functools.partial(write_kernel, count), grid=(2,), in_spec...  19.6 us
  transfers between devices with their start and end apart: 74, of which 21 were waited for; matrix products, arithmetic and copies ran while one was open for 4% of the time, Pallas kernels for 34%

profile of v2, /device:TPU:0, one launch (start us, length us, event | category | flops | bytes accessed | tf_op | source)
XLA Modules:
  0.0 488.4 jit_solution(12448591046592654076)
XLA Ops:
  19.7 10.9 %gates_step.4 = (f32[2,3,288,1152]{3,2,1,0:T(8,128)}, bf16[1152,1152]{1,0:T(8,128)(2,1)S(1)}) custom-call(s32[3]{0:T(128)S(1)} %add_add_fusion.1.pick_ref, bf16[576,1152]{1,0:T(8,128)(2,1)} %convolution_convert_fusion.3.low_ref, bf16[576,1152]{1,0:T(8,128)(2,1)S(1)} %copy-done.16, bf16[2,3,576,2304]{3,2,1,0:T(8,128)(2,1)} %bitcast.28), custom_call_target="tpu_custom_call" | custom-call | flops 1 | bytes 1 | tf_op jit(solution)/shard_map/gates_step/pallas_call | solution.py:245
  30.6 10.1 %collective-permute-done.low_ref = bf16[576,1152]{1,0:T(8,128)(2,1)} collective-permute-done((bf16[576,1152]{1,0:T(8,128)(2,1)}, bf16[576,1152]{1,0:T(8,128)(2,1)}, u32[]{:S(2)}, u32[]{:S(2)}) %collective-permute-start) | collective-permute-done | bytes 1327136 | tf_op jit(solution)/shard_map/ppermute | solution.py:571
  48.3 11.8 %gates_step.5 = (f32[2,3,288,1152]{3,2,1,0:T(8,128)}, bf16[1152,1152]{1,0:T(8,128)(2,1)S(1)}) custom-call(s32[3]{0:T(128)S(1)} %get-tuple-element.661.pick_ref, bf16[576,1152]{1,0:T(8,128)(2,1)} %collective-permute-done.low_ref, bf16[576,1152]{1,0:T(8,128)(2,1)S(1)} %copy-done.18, bf16[2,3,576,2304]{3,2,1,0:T(8,128)(2,1)} %bitcast.29, ...), custom_call_target="tpu_custom_call" | custom-call | flops 1 | bytes 1 | tf_op jit(solution)/shard_map/gates_step/pallas_call | solution.py:245
  60.1 11.6 %gates_step.6 = (f32[2,3,288,1152]{3,2,1,0:T(8,128)}, bf16[1152,1152]{1,0:T(8,128)(2,1)S(1)}) custom-call(s32[3]{0:T(128)S(1)} %add_add_fusion.1.pick_ref, bf16[576,1152]{1,0:T(8,128)(2,1)} %collective-permute-done.3.low_ref, bf16[576,1152]{1,0:T(8,128)(2,1)} %collective-permute-done.4.high_ref, bf16[2,3,576,2304]{3,2,1,0:T(8,128)(2,1)} %bitcast.30), custom_call_target="tpu_custom_call" | custom-call | flops 1 | bytes 1 | tf_op jit(solution)/shard_map/gates_step/pallas_call | solution.py:245
  76.6 9.3 %pool.3 = (bf16[288,1152]{1,0:T(8,128)(2,1)S(1)}, f32[288,128]{1,0:T(8,128)S(1)}, bf16[2,3,288,1152]{3,2,1,0:T(8,128)(2,1)S(1)}) custom-call(s32[1]{0:T(128)S(6)} %copy.33.refs_0_, f32[2,3,288,1152]{3,2,1,0:T(8,128)S(1)} %copy-done.13, f32[288,128]{1,0:T(8,128)S(1)} %get-tuple-element.564.refs_2_, bf16[288,1152]{1,0:T(8,128)(2,1)S(1)} %copy-done.14), custom_call_target="tpu_custom_call" | custom-call | flops 1 | bytes 1 | tf_op jit(solution)/shard_map/pool/pallas_call | solution.py:148
  89.9 16.8 %gates_both.1.refs_1_ = f32[2,3,288,1152]{3,2,1,0:T(8,128)} custom-call(s32[3]{0:T(128)S(1)} %get-tuple-element.573.pick_ref, bf16[1152,1152]{1,0:T(8,128)(2,1)S(1)} %get-tuple-element.682.near_ref, bf16[1152,1152]{1,0:T(8,128)(2,1)S(1)} %get-tuple-element.683.far_ref, bf16[2,3,576,2304]{3,2,1,0:T(8,128)(2,1)} %bitcast.31, bf16[2,3,576,2304]{3,2,1,0:T(8,128)(2,1)} %bitcast.32), custom_call_target="tpu_custom_call" | custom-call | flops 1 | bytes 1 | tf_op jit(solution)/shard_map/gates_both/pallas_call | solution.py:277
  106.7 11.8 %gates_step.7 = (f32[2,3,288,1152]{3,2,1,0:T(8,128)}, bf16[1152,1152]{1,0:T(8,128)(2,1)S(1)}) custom-call(s32[3]{0:T(128)S(1)} %get-tuple-element.661.pick_ref, bf16[576,1152]{1,0:T(8,128)(2,1)} %collective-permute-done.5.low_ref, bf16[576,1152]{1,0:T(8,128)(2,1)S(1)} %collective-permute-done.6.high_ref, bf16[2,3,576,2304]{3,2,1,0:T(8,128)(2,1)} %bitcast.33, ...), custom_call_target="tpu_custom_call" | custom-call | flops 1 | bytes 1 | tf_op jit(solution)/shard_map/gates_step/pallas_call | solution.py:245
  124.6 9.9 %pool.4 = (bf16[288,1152]{1,0:T(8,128)(2,1)}, f32[288,128]{1,0:T(8,128)S(1)}, bf16[2,3,288,1152]{3,2,1,0:T(8,128)(2,1)S(1)}) custom-call(s32[1]{0:T(128)} %bitcast.9.refs_0_, f32[2,3,288,1152]{3,2,1,0:T(8,128)S(1)} %copy-done.12, f32[288,128]{1,0:T(8,128)S(1)} %broadcast_select_fusion.33.refs_2_, bf16[288,1152]{1,0:T(8,128)(2,1)S(1)} %collective-permute-done.8.refs_3_), custom_call_target="tpu_custom_call" | custom-call | flops 1 | bytes 1 | tf_op jit(solution)/shard_map/pool/pallas_call | solution.py:148
  137.1 7.7 %weight_products.3 = bf16[288,2304]{1,0:T(8,128)(2,1)S(1)} custom-call(bf16[1728,1152]{1,0:T(8,128)(2,1)} %bitcast.21, bf16[1728,1152]{1,0:T(8,128)(2,1)} %bitcast.24, bf16[1152,1152]{1,0:T(8,128)(2,1)S(1)} %get-tuple-element.682.near_ref, bf16[1152,1152]{1,0:T(8,128)(2,1)} %copy-done.3, bf16[1152,1152]{1,0:T(8,128)(2,1)} %copy-done.7, ...), custom_call_target="tpu_custom_call" | custom-call | flops 1 | bytes 1 | tf_op jit(solution)/shard_map/weight_products/pallas_call | solution.py:385
  148.7 11.9 %weight_products.4 = bf16[576,2304]{1,0:T(8,128)(2,1)S(1)} custom-call(bf16[1728,1152]{1,0:T(8,128)(2,1)} %bitcast.22, bf16[1728,1152]{1,0:T(8,128)(2,1)} %bitcast.25, bf16[1152,1152]{1,0:T(8,128)(2,1)S(1)} %get-tuple-element.682.near_ref, bf16[1152,1152]{1,0:T(8,128)(2,1)} %copy-done.3, bf16[1152,1152]{1,0:T(8,128)(2,1)} %copy-done.7, ...), custom_call_target="tpu_custom_call" | custom-call | flops 1 | bytes 1 | tf_op jit(solution)/shard_map/weight_products/pallas_call | solution.py:385
  166.3 9.3 %pool.5 = (bf16[288,1152]{1,0:T(8,128)(2,1)S(1)}, f32[288,128]{1,0:T(8,128)S(1)}, bf16[2,3,288,1152]{3,2,1,0:T(8,128)(2,1)S(1)}) custom-call(s32[1]{0:T(128)S(6)} %copy.33.refs_0_, f32[2,3,288,1152]{3,2,1,0:T(8,128)S(1)} %copy-done.6, f32[288,128]{1,0:T(8,128)S(1)} %copy-done.22, bf16[288,1152]{1,0:T(8,128)(2,1)S(1)} %get-tuple-element.640.refs_3_), custom_call_target="tpu_custom_call" | custom-call | flops 1 | bytes 1 | tf_op jit(solution)/shard_map/pool/pallas_call | solution.py:148
  178.4 4.4 collective-permute-start.13
  183.6 19.2 %back_products.2 = (f32[576,1152]{1,0:T(8,128)S(1)}, bf16[576,1152]{1,0:T(8,128)(2,1)S(1)}) custom-call(s32[3]{0:T(128)S(1)} %get-tuple-element.661.pick_ref, bf16[2,3,576,2304]{3,2,1,0:T(8,128)(2,1)} %bitcast.34, bf16[2,3,288,1152]{3,2,1,0:T(8,128)(2,1)} %copy-done.2, bf16[2,3,288,1152]{3,2,1,0:T(8,128)(2,1)} %copy-done.9), custom_call_target="tpu_custom_call" | custom-call | flops 1 | bytes 1 | tf_op jit(solution)/shard_map/back_products/pallas_call | solution.py:337
  203.9 10.6 %collective-permute-start.16 = (bf16[96,2304]{1,0:T(8,128)(2,1)S(1)}, bf16[96,2304]{1,0:T(8,128)(2,1)S(1)}, u32[]{:S(2)}, u32[]{:S(2)}) collective-permute-start(bf16[96,2304]{1,0:T(8,128)(2,1)S(1)} %copy-done.32), channel_id=1, source_target_pairs={{0,8},{4,12},{8,0},{12,4},{16,24},{20,28},{24,16},{28,20},{1,9},{5... | collective-permute-start | bytes 1327112 | tf_op jit(solution)/shard_map/ppermute | solution.py:509
  215.6 16.1 %weight_products.5 = bf16[864,2304]{1,0:T(8,128)(2,1)} custom-call(bf16[1728,1152]{1,0:T(8,128)(2,1)} %bitcast.23, bf16[1728,1152]{1,0:T(8,128)(2,1)} %bitcast.26, bf16[1152,1152]{1,0:T(8,128)(2,1)S(1)} %get-tuple-element.682.near_ref, bf16[1152,1152]{1,0:T(8,128)(2,1)S(1)} %copy-done.4, bf16[1152,1152]{1,0:T(8,128)(2,1)} %copy-done.7, ...), custom_call_target="tpu_custom_call" | custom-call | flops 1 | bytes 1 | tf_op jit(solution)/shard_map/weight_products/pallas_call | solution.py:385
  235.5 19.3 %back_products.3 = (f32[576,1152]{1,0:T(8,128)S(1)}, bf16[576,1152]{1,0:T(8,128)(2,1)S(1)}) custom-call(s32[3]{0:T(128)S(1)} %add_add_fusion.1.pick_ref, bf16[2,3,576,2304]{3,2,1,0:T(8,128)(2,1)} %bitcast.35, bf16[2,3,288,1152]{3,2,1,0:T(8,128)(2,1)} %copy-done.2, bf16[2,3,288,1152]{3,2,1,0:T(8,128)(2,1)} %copy-done.9), custom_call_target="tpu_custom_call" | custom-call | flops 1 | bytes 1 | tf_op jit(solution)/shard_map/back_products/pallas_call | solution.py:337
  255.8 9.7 %collective-permute-start.18 = (bf16[96,2304]{1,0:T(8,128)(2,1)S(1)}, bf16[96,2304]{1,0:T(8,128)(2,1)S(1)}, u32[]{:S(2)}, u32[]{:S(2)}) collective-permute-start(bf16[96,2304]{1,0:T(8,128)(2,1)S(1)} %copy-done.33), channel_id=1, source_target_pairs={{0,8},{4,12},{8,0},{12,4},{16,24},{20,28},{24,16},{28,20},{1,9},{5... | collective-permute-start | bytes 1327112 | tf_op jit(solution)/shard_map/ppermute | solution.py:509
  268.1 8.6 %collective-permute-start.23 = (bf16[96,2304]{1,0:T(8,128)(2,1)S(1)}, bf16[96,2304]{1,0:T(8,128)(2,1)S(1)}, u32[]{:S(2)}, u32[]{:S(2)}) collective-permute-start(bf16[96,2304]{1,0:T(8,128)(2,1)S(1)} %get-tuple-element.730), channel_id=1, source_target_pairs={{0,8},{4,12},{8,0},{12,4},{16,24},{20,28},{24,16},{28,20},{1,9},{5... | collective-permute-start | bytes 1327112 | tf_op jit(solution)/shard_map/ppermute | solution.py:509
  278.5 6.9 %collective-permute-start.24 = (bf16[96,2304]{1,0:T(8,128)(2,1)S(1)}, bf16[96,2304]{1,0:T(8,128)(2,1)S(1)}, u32[]{:S(2)}, u32[]{:S(2)}) collective-permute-start(bf16[96,2304]{1,0:T(8,128)(2,1)S(1)} %get-tuple-element.750), channel_id=1, source_target_pairs={{0,8},{4,12},{8,0},{12,4},{16,24},{20,28},{24,16},{28,20},{1,9},{5... | collective-permute-start | bytes 1327112 | tf_op jit(solution)/shard_map/ppermute | solution.py:509
  301.1 11.3 %collective-permute-start.28 = (bf16[96,2304]{1,0:T(8,128)(2,1)S(1)}, bf16[96,2304]{1,0:T(8,128)(2,1)S(1)}, u32[]{:S(2)}, u32[]{:S(2)}) collective-permute-start(bf16[96,2304]{1,0:T(8,128)(2,1)S(1)} %broadcast_select_fusion.26), channel_id=1, source_target_pairs={{0,8},{4,12},{8,0},{12,4},{16,24},{20,28},{24,16},{28,20},{1,9},{5... | collective-permute-start | bytes 1327112 | tf_op jit(solution)/shard_map/ppermute | solution.py:509
  313.4 7.8 %collective-permute-done.28 = bf16[96,2304]{1,0:T(8,128)(2,1)S(1)} collective-permute-done((bf16[96,2304]{1,0:T(8,128)(2,1)S(1)}, bf16[96,2304]{1,0:T(8,128)(2,1)S(1)}, u32[]{:S(2)}, u32[]{:S(2)}) %collective-permute-start.28) | collective-permute-done | bytes 442400 | tf_op jit(solution)/shard_map/ppermute | solution.py:509
  344.6 5.7 %collective-permute-done.37.refs_4_ = bf16[96,2304]{1,0:T(8,128)(2,1)S(1)} collective-permute-done((bf16[96,2304]{1,0:T(8,128)(2,1)S(1)}, bf16[96,2304]{1,0:T(8,128)(2,1)S(1)}, u32[]{:S(2)}, u32[]{:S(2)}) %collective-permute-start.37) | collective-permute-done | bytes 442400 | tf_op jit(solution)/shard_map/ppermute | solution.py:521
  350.3 7.5 %collective-permute-start.34 = (bf16[96,2304]{1,0:T(8,128)(2,1)S(1)}, bf16[96,2304]{1,0:T(8,128)(2,1)S(1)}, u32[]{:S(2)}, u32[]{:S(2)}) collective-permute-start(bf16[96,2304]{1,0:T(8,128)(2,1)S(1)} %get-tuple-element.805), channel_id=1, source_target_pairs={{0,8},{4,12},{8,0},{12,4},{16,24},{20,28},{24,16},{28,20},{1,9},{5... | collective-permute-start | bytes 1327112 | tf_op jit(solution)/shard_map/ppermute | solution.py:509
  362.2 5.2 %collective-permute-done.34 = bf16[96,2304]{1,0:T(8,128)(2,1)S(1)} collective-permute-done((bf16[96,2304]{1,0:T(8,128)(2,1)S(1)}, bf16[96,2304]{1,0:T(8,128)(2,1)S(1)}, u32[]{:S(2)}, u32[]{:S(2)}) %collective-permute-start.34) | collective-permute-done | bytes 442400 | tf_op jit(solution)/shard_map/ppermute | solution.py:509
  378.8 7.6 %collective-permute-done.48 = bf16[96,2304]{1,0:T(8,128)(2,1)S(1)} collective-permute-done((bf16[96,2304]{1,0:T(8,128)(2,1)S(1)}, bf16[96,2304]{1,0:T(8,128)(2,1)S(1)}, u32[]{:S(2)}, u32[]{:S(2)}) %collective-permute-start.48) | collective-permute-done | bytes 442400 | tf_op jit(solution)/shard_map/ppermute | solution.py:509
  392.8 8.6 %collective-permute-done.54 = bf16[96,2304]{1,0:T(8,128)(2,1)S(1)} collective-permute-done((bf16[96,2304]{1,0:T(8,128)(2,1)S(1)}, bf16[96,2304]{1,0:T(8,128)(2,1)S(1)}, u32[]{:S(2)}, u32[]{:S(2)}) %collective-permute-start.54) | collective-permute-done | bytes 442400 | tf_op jit(solution)/shard_map/ppermute | solution.py:509
  413.9 8.0 %collective-permute-done.57 = bf16[96,2304]{1,0:T(8,128)(2,1)S(1)} collective-permute-done((bf16[96,2304]{1,0:T(8,128)(2,1)S(1)}, bf16[96,2304]{1,0:T(8,128)(2,1)S(1)}, u32[]{:S(2)}, u32[]{:S(2)}) %collective-permute-start.57) | collective-permute-done | bytes 442400 | tf_op jit(solution)/shard_map/ppermute | solution.py:509
  426.9 8.2 %collective-permute-done.62 = bf16[96,2304]{1,0:T(8,128)(2,1)S(1)} collective-permute-done((bf16[96,2304]{1,0:T(8,128)(2,1)S(1)}, bf16[96,2304]{1,0:T(8,128)(2,1)S(1)}, u32[]{:S(2)}, u32[]{:S(2)}) %collective-permute-start.62) | collective-permute-done | bytes 442400 | tf_op jit(solution)/shard_map/ppermute | solution.py:509
  445.5 8.7 %collective-permute-done.63 = bf16[96,2304]{1,0:T(8,128)(2,1)S(1)} collective-permute-done((bf16[96,2304]{1,0:T(8,128)(2,1)S(1)}, bf16[96,2304]{1,0:T(8,128)(2,1)S(1)}, u32[]{:S(2)}, u32[]{:S(2)}) %collective-permute-start.63) | collective-permute-done | bytes 442400 | tf_op jit(solution)/shard_map/ppermute | solution.py:509
  456.3 6.1 %collective-permute-done.67 = bf16[96,2304]{1,0:T(8,128)(2,1)S(1)} collective-permute-done((bf16[96,2304]{1,0:T(8,128)(2,1)S(1)}, bf16[96,2304]{1,0:T(8,128)(2,1)S(1)}, u32[]{:S(2)}, u32[]{:S(2)}) %collective-permute-start.67) | collective-permute-done | bytes 442400 | tf_op jit(solution)/shard_map/ppermute | solution.py:509
  470.3 5.5 %collective-permute-done.72.refs_4_ = bf16[96,2304]{1,0:T(8,128)(2,1)S(1)} collective-permute-done((bf16[96,2304]{1,0:T(8,128)(2,1)S(1)}, bf16[96,2304]{1,0:T(8,128)(2,1)S(1)}, u32[]{:S(2)}, u32[]{:S(2)}) %collective-permute-start.72) | collective-permute-done | bytes 442400 | tf_op jit(solution)/shard_map/ppermute | solution.py:521
  475.9 4.7 collective-permute-done.73.refs_5_
  (316 shorter events, 173.7 us)
Async XLA Ops:
  8.1 32.6 %collective-permute-start = (bf16[576,1152]{1,0:T(8,128)(2,1)}, bf16[576,1152]{1,0:T(8,128)(2,1)}, u32[]{:S(2)}, u32[]{:S(2)}) collective-permute-start(bf16[576,1152]{1,0:T(8,128)(2,1)} %convolution_convert_fusion.3.low_ref), channel_id=1, source_target_pairs={{0,2},{1,3},{2,0},{3,1},{4,6},{5,7},{6,4},{7,5},{8,10},{9,11},{10,... | collective-permute-start | bytes 3981320 | tf_op jit(solution)/shard_map/ppermute | solution.py:571
  10.6 31.6 %collective-permute-start.3 = (bf16[576,1152]{1,0:T(8,128)(2,1)}, bf16[576,1152]{1,0:T(8,128)(2,1)}, u32[]{:S(2)}, u32[]{:S(2)}) collective-permute-start(bf16[576,1152]{1,0:T(8,128)(2,1)} %convolution_convert_fusion.3.low_ref), channel_id=1, source_target_pairs={{0,4},{4,0},{8,12},{12,8},{16,20},{20,16},{24,28},{28,24},{1,5},{5... | collective-permute-start | bytes 3981320 | tf_op jit(solution)/shard_map/ppermute | solution.py:572
  45.2 42.6 %collective-permute-start.5 = (bf16[576,1152]{1,0:T(8,128)(2,1)}, bf16[576,1152]{1,0:T(8,128)(2,1)}, u32[]{:S(2)}, u32[]{:S(2)}) collective-permute-start(bf16[576,1152]{1,0:T(8,128)(2,1)} %collective-permute-done.3.low_ref), channel_id=1, source_target_pairs={{0,2},{1,3},{2,0},{3,1},{4,6},{5,7},{6,4},{7,5},{8,10},{9,11},{10,... | collective-permute-start | bytes 3981320 | tf_op jit(solution)/shard_map/ppermute | solution.py:580
  87.8 18.9 %collective-permute-start.6 = (bf16[576,1152]{1,0:T(8,128)(2,1)}, bf16[576,1152]{1,0:T(8,128)(2,1)S(1)}, u32[]{:S(2)}, u32[]{:S(2)}) collective-permute-start(bf16[576,1152]{1,0:T(8,128)(2,1)} %collective-permute-done.5.low_ref), channel_id=1, source_target_pairs={{0,1},{1,0},{2,3},{3,2},{4,5},{5,4},{6,7},{7,6},{8,9},{9,8},{10,11... | collective-permute-start | bytes 3981320 | tf_op jit(solution)/shard_map/ppermute | solution.py:592
  87.9 32.2 %collective-permute-start.8 = (bf16[288,1152]{1,0:T(8,128)(2,1)S(1)}, bf16[288,1152]{1,0:T(8,128)(2,1)S(1)}, u32[]{:S(2)}, u32[]{:S(2)}) collective-permute-start(bf16[288,1152]{1,0:T(8,128)(2,1)S(1)} %get-tuple-element.640.refs_3_), channel_id=1, source_target_pairs={{0,4},{4,0},{8,12},{12,8},{16,20},{20,16},{24,28},{28,24},{1,5},{5... | collective-permute-start | bytes 1990664 | tf_op jit(solution)/shard_map/ppermute | solution.py:581
  89.4 30.7 %collective-permute-start.7 = (f32[288,128]{1,0:T(8,128)S(1)}, f32[288,128]{1,0:T(8,128)S(1)}, u32[]{:S(2)}, u32[]{:S(2)}) collective-permute-start(f32[288,128]{1,0:T(8,128)S(1)} %copy-done.21), channel_id=1, source_target_pairs={{0,4},{4,0},{8,12},{12,8},{16,20},{20,16},{24,28},{28,24},{1,5},{5... | collective-permute-start | bytes 442376 | tf_op jit(solution)/shard_map/ppermute | solution.py:582
  160.6 17.0 %collective-permute-start.11 = (bf16[96,2304]{1,0:T(8,128)(2,1)S(1)}, bf16[96,2304]{1,0:T(8,128)(2,1)S(1)}, u32[]{:S(2)}, u32[]{:S(2)}) collective-permute-start(bf16[96,2304]{1,0:T(8,128)(2,1)S(1)} %copy-done.34), channel_id=1, source_target_pairs={{0,8},{4,12},{8,0},{12,4},{16,24},{20,28},{24,16},{28,20},{1,9},{5... | collective-permute-start | bytes 1327112 | tf_op jit(solution)/shard_map/ppermute | solution.py:509
  178.4 24.5 %collective-permute-start.13 = (bf16[96,2304]{1,0:T(8,128)(2,1)}, bf16[96,2304]{1,0:T(8,128)(2,1)S(1)}, u32[]{:S(2)}, u32[]{:S(2)}) collective-permute-start(bf16[96,2304]{1,0:T(8,128)(2,1)} %get-tuple-element.657), channel_id=1, source_target_pairs={{0,8},{4,12},{8,0},{12,4},{16,24},{20,28},{24,16},{28,20},{1,9},{5... | collective-permute-start | bytes 1327112 | tf_op jit(solution)/shard_map/ppermute | solution.py:509
  182.8 20.2 %collective-permute-start.12 = (bf16[96,2304]{1,0:T(8,128)(2,1)S(1)}, bf16[96,2304]{1,0:T(8,128)(2,1)S(1)}, u32[]{:S(2)}, u32[]{:S(2)}) collective-permute-start(bf16[96,2304]{1,0:T(8,128)(2,1)S(1)} %add_convert_fusion.37), channel_id=1, source_target_pairs={{8,16},{12,20},{16,8},{20,12},{9,17},{13,21},{17,9},{21,13},{10,18... | collective-permute-start | bytes 1327112 | tf_op jit(solution)/shard_map/ppermute | solution.py:517
  203.9 31.4 %collective-permute-start.16 = (bf16[96,2304]{1,0:T(8,128)(2,1)S(1)}, bf16[96,2304]{1,0:T(8,128)(2,1)S(1)}, u32[]{:S(2)}, u32[]{:S(2)}) collective-permute-start(bf16[96,2304]{1,0:T(8,128)(2,1)S(1)} %copy-done.32), channel_id=1, source_target_pairs={{0,8},{4,12},{8,0},{12,4},{16,24},{20,28},{24,16},{28,20},{1,9},{5... | collective-permute-start | bytes 1327112 | tf_op jit(solution)/shard_map/ppermute | solution.py:509
  232.4 22.4 %collective-permute-start.14 = (bf16[96,2304]{1,0:T(8,128)(2,1)}, bf16[96,2304]{1,0:T(8,128)(2,1)S(1)}, u32[]{:S(2)}, u32[]{:S(2)}) collective-permute-start(bf16[96,2304]{1,0:T(8,128)(2,1)} %get-tuple-element.675), channel_id=1, source_target_pairs={{0,8},{4,12},{8,0},{12,4},{16,24},{20,28},{24,16},{28,20},{1,9},{5... | collective-permute-start | bytes 1327112 | tf_op jit(solution)/shard_map/ppermute | solution.py:509
  235.3 32.8 %collective-permute-start.19 = (bf16[576,1152]{1,0:T(8,128)(2,1)S(1)}, bf16[576,1152]{1,0:T(8,128)(2,1)S(1)}, u32[]{:S(2)}, u32[]{:S(2)}) collective-permute-start(bf16[576,1152]{1,0:T(8,128)(2,1)S(1)} %get-tuple-element.708), channel_id=1, source_target_pairs={{0,1},{1,0},{2,3},{3,2},{4,5},{5,4},{6,7},{7,6},{8,9},{9,8},{10,11... | collective-permute-start | bytes 3981320 | tf_op jit(solution)/shard_map/ppermute | solution.py:637
  255.8 21.1 %collective-permute-start.18 = (bf16[96,2304]{1,0:T(8,128)(2,1)S(1)}, bf16[96,2304]{1,0:T(8,128)(2,1)S(1)}, u32[]{:S(2)}, u32[]{:S(2)}) collective-permute-start(bf16[96,2304]{1,0:T(8,128)(2,1)S(1)} %copy-done.33), channel_id=1, source_target_pairs={{0,8},{4,12},{8,0},{12,4},{16,24},{20,28},{24,16},{28,20},{1,9},{5... | collective-permute-start | bytes 1327112 | tf_op jit(solution)/shard_map/ppermute | solution.py:509
  266.2 23.2 %collective-permute-start.22 = (bf16[96,2304]{1,0:T(8,128)(2,1)S(1)}, bf16[96,2304]{1,0:T(8,128)(2,1)S(1)}, u32[]{:S(2)}, u32[]{:S(2)}) collective-permute-start(bf16[96,2304]{1,0:T(8,128)(2,1)S(1)} %broadcast_select_fusion.28.refs_0_), channel_id=1, source_target_pairs={{0,4},{4,0},{8,12},{12,8},{16,20},{20,16},{24,28},{28,24},{1,5},{5... | collective-permute-start | bytes 1327112 | tf_op jit(solution)/shard_map/ppermute | solution.py:521
  267.8 70.7 %collective-permute-start.39 = (bf16[576,1152]{1,0:T(8,128)(2,1)S(1)}, bf16[576,1152]{1,0:T(8,128)(2,1)S(1)}, u32[]{:S(2)}, u32[]{:S(2)}) collective-permute-start(bf16[576,1152]{1,0:T(8,128)(2,1)S(1)} %get-tuple-element.812), channel_id=1, source_target_pairs={{0,1},{1,0},{2,3},{3,2},{4,5},{5,4},{6,7},{7,6},{8,9},{9,8},{10,11... | collective-permute-start | bytes 3981320 | tf_op jit(solution)/shard_map/ppermute | solution.py:637
  268.1 19.6 %collective-permute-start.23 = (bf16[96,2304]{1,0:T(8,128)(2,1)S(1)}, bf16[96,2304]{1,0:T(8,128)(2,1)S(1)}, u32[]{:S(2)}, u32[]{:S(2)}) collective-permute-start(bf16[96,2304]{1,0:T(8,128)(2,1)S(1)} %get-tuple-element.730), channel_id=1, source_target_pairs={{0,8},{4,12},{8,0},{12,4},{16,24},{20,28},{24,16},{28,20},{1,9},{5... | collective-permute-start | bytes 1327112 | tf_op jit(solution)/shard_map/ppermute | solution.py:509
  278.5 18.6 %collective-permute-start.24 = (bf16[96,2304]{1,0:T(8,128)(2,1)S(1)}, bf16[96,2304]{1,0:T(8,128)(2,1)S(1)}, u32[]{:S(2)}, u32[]{:S(2)}) collective-permute-start(bf16[96,2304]{1,0:T(8,128)(2,1)S(1)} %get-tuple-element.750), channel_id=1, source_target_pairs={{0,8},{4,12},{8,0},{12,4},{16,24},{20,28},{24,16},{28,20},{1,9},{5... | collective-permute-start | bytes 1327112 | tf_op jit(solution)/shard_map/ppermute | solution.py:509
  289.4 23.2 %collective-permute-start.29 = (f32[288,128]{1,0:T(8,128)S(1)}, f32[288,128]{1,0:T(8,128)S(1)}, u32[]{:S(2)}, u32[]{:S(2)}) collective-permute-start(f32[288,128]{1,0:T(8,128)S(1)} %copy-done.31), channel_id=1, source_target_pairs={{0,8},{4,12},{8,0},{12,4},{16,24},{20,28},{24,16},{28,20},{1,9},{5... | collective-permute-start | bytes 442376 | tf_op jit(solution)/shard_map/ppermute | solution.py:683
  291.5 47.8 %collective-permute-start.40 = (bf16[576,1152]{1,0:T(8,128)(2,1)S(1)}, bf16[576,1152]{1,0:T(8,128)(2,1)S(1)}, u32[]{:S(2)}, u32[]{:S(2)}) collective-permute-start(bf16[576,1152]{1,0:T(8,128)(2,1)S(1)} %add_convert_fusion.1), channel_id=1, source_target_pairs={{0,2},{1,3},{2,0},{3,1},{4,6},{5,7},{6,4},{7,5},{8,10},{9,11},{10,... | collective-permute-start | bytes 3981320 | tf_op jit(solution)/shard_map/ppermute | solution.py:647
  299.5 23.4 %collective-permute-start.27 = (bf16[96,2304]{1,0:T(8,128)(2,1)S(1)}, bf16[96,2304]{1,0:T(8,128)(2,1)S(1)}, u32[]{:S(2)}, u32[]{:S(2)}) collective-permute-start(bf16[96,2304]{1,0:T(8,128)(2,1)S(1)} %broadcast_select_fusion.24.refs_2_), channel_id=1, source_target_pairs={{0,4},{4,0},{8,12},{12,8},{16,20},{20,16},{24,28},{28,24},{1,5},{5... | collective-permute-start | bytes 1327112 | tf_op jit(solution)/shard_map/ppermute | solution.py:521
  301.1 20.1 %collective-permute-start.28 = (bf16[96,2304]{1,0:T(8,128)(2,1)S(1)}, bf16[96,2304]{1,0:T(8,128)(2,1)S(1)}, u32[]{:S(2)}, u32[]{:S(2)}) collective-permute-start(bf16[96,2304]{1,0:T(8,128)(2,1)S(1)} %broadcast_select_fusion.26), channel_id=1, source_target_pairs={{0,8},{4,12},{8,0},{12,4},{16,24},{20,28},{24,16},{28,20},{1,9},{5... | collective-permute-start | bytes 1327112 | tf_op jit(solution)/shard_map/ppermute | solution.py:509
  328.0 31.2 %collective-permute-start.35 = (f32[288,128]{1,0:T(8,128)S(1)}, f32[288,128]{1,0:T(8,128)S(1)}, u32[]{:S(2)}, u32[]{:S(2)}) collective-permute-start(f32[288,128]{1,0:T(8,128)S(1)} %add.194), channel_id=1, source_target_pairs={{8,16},{12,20},{16,8},{20,12},{9,17},{13,21},{17,9},{21,13},{10,18... | collective-permute-start | bytes 442376 | tf_op jit(solution)/shard_map/ppermute | solution.py:683
  338.5 20.0 %collective-permute-start.36 = (bf16[96,2304]{1,0:T(8,128)(2,1)S(1)}, bf16[96,2304]{1,0:T(8,128)(2,1)S(1)}, u32[]{:S(2)}, u32[]{:S(2)}) collective-permute-start(bf16[96,2304]{1,0:T(8,128)(2,1)S(1)} %add_convert_fusion.21), channel_id=1, source_target_pairs={{8,16},{12,20},{16,8},{20,12},{9,17},{13,21},{17,9},{21,13},{10,18... | collective-permute-start | bytes 1327112 | tf_op jit(solution)/shard_map/ppermute | solution.py:517
  339.2 30.0 %collective-permute-start.45 = (bf16[96,2304]{1,0:T(8,128)(2,1)S(1)}, bf16[96,2304]{1,0:T(8,128)(2,1)S(1)}, u32[]{:S(2)}, u32[]{:S(2)}) collective-permute-start(bf16[96,2304]{1,0:T(8,128)(2,1)S(1)} %broadcast_select_fusion.18.refs_2_), channel_id=1, source_target_pairs={{0,4},{4,0},{8,12},{12,8},{16,20},{20,16},{24,28},{28,24},{1,5},{5... | collective-permute-start | bytes 1327112 | tf_op jit(solution)/shard_map/ppermute | solution.py:521
  350.3 17.0 %collective-permute-start.34 = (bf16[96,2304]{1,0:T(8,128)(2,1)S(1)}, bf16[96,2304]{1,0:T(8,128)(2,1)S(1)}, u32[]{:S(2)}, u32[]{:S(2)}) collective-permute-start(bf16[96,2304]{1,0:T(8,128)(2,1)S(1)} %get-tuple-element.805), channel_id=1, source_target_pairs={{0,8},{4,12},{8,0},{12,4},{16,24},{20,28},{24,16},{28,20},{1,9},{5... | collective-permute-start | bytes 1327112 | tf_op jit(solution)/shard_map/ppermute | solution.py:509
  358.6 17.7 %collective-permute-start.42 = (bf16[96,2304]{1,0:T(8,128)(2,1)S(1)}, bf16[96,2304]{1,0:T(8,128)(2,1)S(1)}, u32[]{:S(2)}, u32[]{:S(2)}) collective-permute-start(bf16[96,2304]{1,0:T(8,128)(2,1)S(1)} %broadcast_select_fusion.16.refs_0_), channel_id=1, source_target_pairs={{0,4},{4,0},{8,12},{12,8},{16,20},{20,16},{24,28},{28,24},{1,5},{5... | collective-permute-start | bytes 1327112 | tf_op jit(solution)/shard_map/ppermute | solution.py:521
  377.0 26.0 %collective-permute-start.53 = (bf16[96,2304]{1,0:T(8,128)(2,1)S(1)}, bf16[96,2304]{1,0:T(8,128)(2,1)S(1)}, u32[]{:S(2)}, u32[]{:S(2)}) collective-permute-start(bf16[96,2304]{1,0:T(8,128)(2,1)S(1)} %broadcast_select_fusion.13.refs_2_), channel_id=1, source_target_pairs={{0,4},{4,0},{8,12},{12,8},{16,20},{20,16},{24,28},{28,24},{1,5},{5... | collective-permute-start | bytes 1327112 | tf_op jit(solution)/shard_map/ppermute | solution.py:521
  390.8 20.2 %collective-permute-start.59 = (bf16[96,2304]{1,0:T(8,128)(2,1)S(1)}, bf16[96,2304]{1,0:T(8,128)(2,1)S(1)}, u32[]{:S(2)}, u32[]{:S(2)}) collective-permute-start(bf16[96,2304]{1,0:T(8,128)(2,1)S(1)} %broadcast_select_fusion.10.refs_0_), channel_id=1, source_target_pairs={{0,4},{4,0},{8,12},{12,8},{16,20},{20,16},{24,28},{28,24},{1,5},{5... | collective-permute-start | bytes 1327112 | tf_op jit(solution)/shard_map/ppermute | solution.py:521
  411.7 23.6 %collective-permute-start.61 = (bf16[96,2304]{1,0:T(8,128)(2,1)S(1)}, bf16[96,2304]{1,0:T(8,128)(2,1)S(1)}, u32[]{:S(2)}, u32[]{:S(2)}) collective-permute-start(bf16[96,2304]{1,0:T(8,128)(2,1)S(1)} %broadcast_select_fusion.6.refs_2_), channel_id=1, source_target_pairs={{0,4},{4,0},{8,12},{12,8},{16,20},{20,16},{24,28},{28,24},{1,5},{5... | collective-permute-start | bytes 1327112 | tf_op jit(solution)/shard_map/ppermute | solution.py:521
  424.9 18.4 %collective-permute-start.65 = (bf16[96,2304]{1,0:T(8,128)(2,1)S(1)}, bf16[96,2304]{1,0:T(8,128)(2,1)S(1)}, u32[]{:S(2)}, u32[]{:S(2)}) collective-permute-start(bf16[96,2304]{1,0:T(8,128)(2,1)S(1)} %broadcast_select_fusion.5.refs_0_), channel_id=1, source_target_pairs={{0,4},{4,0},{8,12},{12,8},{16,20},{20,16},{24,28},{28,24},{1,5},{5... | collective-permute-start | bytes 1327112 | tf_op jit(solution)/shard_map/ppermute | solution.py:521
  425.1 18.1 %collective-permute-start.66 = (bf16[96,2304]{1,0:T(8,128)(2,1)S(1)}, bf16[96,2304]{1,0:T(8,128)(2,1)S(1)}, u32[]{:S(2)}, u32[]{:S(2)}) collective-permute-start(bf16[96,2304]{1,0:T(8,128)(2,1)S(1)} %add_convert_fusion.8), channel_id=1, source_target_pairs={{0,8},{4,12},{8,0},{12,4},{16,24},{20,28},{24,16},{28,20},{1,9},{5... | collective-permute-start | bytes 1327112 | tf_op jit(solution)/shard_map/ppermute | solution.py:509
  443.2 19.3 %collective-permute-start.70 = (bf16[96,2304]{1,0:T(8,128)(2,1)S(1)}, bf16[96,2304]{1,0:T(8,128)(2,1)S(1)}, u32[]{:S(2)}, u32[]{:S(2)}) collective-permute-start(bf16[96,2304]{1,0:T(8,128)(2,1)S(1)} %broadcast_select_fusion.3.refs_2_), channel_id=1, source_target_pairs={{0,4},{4,0},{8,12},{12,8},{16,20},{20,16},{24,28},{28,24},{1,5},{5... | collective-permute-start | bytes 1327112 | tf_op jit(solution)/shard_map/ppermute | solution.py:521
  (85 other events, 921.5 us)

commit v3 on v2

--- a/solution.py
+++ b/solution.py
@@ -10,6 +10,7 @@
 LANES = 128
 ROWS = 16
 CHUNKS = 18
+PART = 96
 LAG = 4
 HIDDEN_COST = pl.CostEstimate(flops=1, bytes_accessed=1, transcendentals=0)
 
@@ -51,7 +52,7 @@
             live = is_live(j)
             cand = jnp.tanh(gates[0])
             forget = jax.nn.sigmoid(gates[1])
-            out_gate = jnp.where(live, jax.nn.sigmoid(gates[2]), 0.0)
+            out_gate = jnp.where(live, 0.5 * jnp.tanh(0.5 * gates[2]) + 0.5, 0.0)
             kept = jnp.where(live, 1.0 - forget, 0.0)
             decay = 1.0 - kept
             emitted = out_gate * grad_ref[rows, tile_of(j)].astype(jnp.float32)
@@ -208,9 +209,7 @@
     return pl.BlockSpec(shape, lambda *at: zeros, pipeline_mode=pl.Buffered(1))
 
 
-def gates_kernel(pick_ref, low_ref, high_ref, w_ref, *refs):
-    base_ref = refs[0] if len(refs) == 3 else None
-    out_ref, x_ref = refs[-2:]
+def gates_kernel(pick_ref, low_ref, high_ref, w_ref, out_ref, x_ref, *copy_refs):
     half_rows = low_ref.shape[0]
 
     @pl.when(pl.program_id(0) == 0)
@@ -223,102 +222,148 @@
     kinds, width = w_ref.shape[1:3]
     weights = w_ref[0].reshape(kinds * width, w_ref.shape[3])
     total = jnp.dot(weights, x_ref[...], preferred_element_type=jnp.float32)
-    total = total.reshape(out_ref.shape)
-    if base_ref is not None:
-        total = total + base_ref[...]
-    out_ref[...] = total
-
-
-def gates_step(pick, w_rows, own, sibling, base=None):
+    out_ref[...] = total.reshape(out_ref.shape)
+    for copy_ref in copy_refs:
+        copy_ref[...] = w_ref[...]
+
+
+def gates_step(pick, w_rows, own, sibling, copy):
     taps, kinds, width, depth = w_rows.shape
     rows, span = own.shape
-    block = lambda: pl.BlockSpec((1, kinds, width // 2, span), lambda g, p: (g, 0, 0, 0))
+    block = lambda last: pl.BlockSpec((1, kinds, width // 2, last), lambda g, p: (g, 0, 0, 0))
     specs = [
         once((rows, span)),
         once((rows, span)),
         pl.BlockSpec((1, kinds, width // 2, 2 * rows), lambda g, p: (g, 0, p[0], p[1])),
     ]
     operands = [own, sibling, w_rows]
-    if base is not None:
-        specs.append(block())
-        operands.append(base)
+    out_specs = [block(span), pl.BlockSpec((2 * rows, span), lambda g, p: (0, 0))]
+    out_shape = [
+        jax.ShapeDtypeStruct((taps, kinds, width // 2, span), jnp.float32),
+        jax.ShapeDtypeStruct((2 * rows, span), jnp.bfloat16),
+    ]
+    if copy:
+        out_specs.append(block(2 * rows))
+        out_shape.append(jax.ShapeDtypeStruct((taps, kinds, width // 2, 2 * rows), jnp.bfloat16))
     return pl.pallas_call(
         gates_kernel,
         grid_spec=pltpu.PrefetchScalarGridSpec(
             num_scalar_prefetch=1,
             grid=(taps,),
             in_specs=specs,
-            out_specs=[block(), pl.BlockSpec((2 * rows, span), lambda g, p: (0, 0))],
+            out_specs=out_specs,
         ),
-        out_shape=[
-            jax.ShapeDtypeStruct((taps, kinds, width // 2, span), jnp.float32),
-            jax.ShapeDtypeStruct((2 * rows, span), jnp.bfloat16),
-        ],
-        compiler_params=pltpu.CompilerParams(vmem_limit_bytes=48 * 2**20),
+        out_shape=out_shape,
+        compiler_params=pltpu.CompilerParams(vmem_limit_bytes=32 * 2**20),
         cost_estimate=HIDDEN_COST,
         name="gates_step",
     )(pick, *operands)
 
 
-def gates_both_kernel(pick_ref, near_ref, far_ref, w_near_ref, w_far_ref, out_ref):
-    kinds, width, rows = w_near_ref.shape[1:]
-
-    def product(w_ref, x_ref):
-        weights = w_ref[0].reshape(kinds * width, rows)
-        return jnp.dot(weights, x_ref[...], preferred_element_type=jnp.float32)
-
-    total = product(w_near_ref, near_ref) + product(w_far_ref, far_ref)
-    out_ref[...] = total.reshape(out_ref.shape)
-
-
-def gates_both(pick, w_rows, near, far):
+def gates_pool_kernel(pick_ref, length_ref, low_ref, high_ref, w_ref, base_ref, small_ref, grad_ref,
+                      hidden_ref, sums_ref, gg_ref, x_ref, *refs):
+    half_rows = low_ref.shape[0]
+
+    @pl.when(pl.program_id(0) == 0)
+    def _():
+        at = pl.multiple_of(pick_ref[2] * half_rows, 64)
+        x_ref[pl.ds(at, half_rows), :] = low_ref[...]
+        at = pl.multiple_of((1 - pick_ref[2]) * half_rows, 64)
+        x_ref[pl.ds(at, half_rows), :] = high_ref[...]
+
+    gates_ref = refs[-3]
+    for copy_ref in refs[:-3]:
+        copy_ref[...] = w_ref[...]
+    weights = w_ref[...].reshape(-1, w_ref.shape[3])
+    product = jnp.dot(weights, x_ref[...], preferred_element_type=jnp.float32)
+    gates_ref[...] = product.reshape(gates_ref.shape) + base_ref[...]
+    pool_kernel(length_ref, gates_ref, small_ref, grad_ref, hidden_ref, sums_ref, gg_ref, refs[-2:])
+
+
+def pool_shapes(width, span):
+    return [
+        jax.ShapeDtypeStruct((width, span), jnp.bfloat16),
+        jax.ShapeDtypeStruct((width, LANES), jnp.float32),
+        jax.ShapeDtypeStruct((2, 3, width, span), jnp.bfloat16),
+    ]
+
+
+def pool_scratch(part, span):
+    return [
+        pltpu.VMEM((2, 3, part, span), jnp.float32),
+        pltpu.VMEM((3, part, span), jnp.float32),
+        pltpu.VMEM((3, part, LANES), jnp.float32),
+    ]
+
+
+def gates_pool(pick, length, w_rows, own, sibling, base, small, grad, copy):
     taps, kinds, width, depth = w_rows.shape
-    rows, span = near.shape
+    rows, span = own.shape
+    width //= 2
+    part = PART
+    count = width // part
+    lines = lambda columns: pl.BlockSpec((part, columns), lambda i, p: (i, 0))
+    wide = pl.BlockSpec((taps, kinds, part, span), lambda i, p: (0, 0, i, 0))
+    copy_specs, copy_shapes = [], []
+    if copy:
+        copy_specs = [pl.BlockSpec((taps, kinds, part, 2 * rows), lambda i, p: (0, 0, i, 0))]
+        copy_shapes = [jax.ShapeDtypeStruct((taps, kinds, width, 2 * rows), jnp.bfloat16)]
     return pl.pallas_call(
-        gates_both_kernel,
+        gates_pool_kernel,
         grid_spec=pltpu.PrefetchScalarGridSpec(
             num_scalar_prefetch=1,
-            grid=(taps,),
+            grid=(count,),
             in_specs=[
+                pl.BlockSpec(memory_space=pltpu.SMEM),
                 once((rows, span)),
                 once((rows, span)),
-                pl.BlockSpec((1, kinds, width // 2, rows), lambda g, p: (g, 0, p[0], p[1])),
-                pl.BlockSpec((1, kinds, width // 2, rows), lambda g, p: (g, 0, p[0], 1 - p[1])),
+                pl.BlockSpec(
+                    (taps, kinds, part, 2 * rows), lambda i, p: (0, 0, p[0] * count + i, p[1])
+                ),
+                wide,
+                lines(LANES),
+                lines(span),
             ],
-            out_specs=pl.BlockSpec((1, kinds, width // 2, span), lambda g, p: (g, 0, 0, 0)),
+            out_specs=[
+                lines(span),
+                lines(LANES),
+                wide,
+                pl.BlockSpec((2 * rows, span), lambda i, p: (0, 0)),
+                *copy_specs,
+            ],
+            scratch_shapes=pool_scratch(part, span),
         ),
-        out_shape=jax.ShapeDtypeStruct((taps, kinds, width // 2, span), jnp.float32),
-        compiler_params=pltpu.CompilerParams(vmem_limit_bytes=48 * 2**20),
+        out_shape=pool_shapes(width, span)
+        + [jax.ShapeDtypeStruct((2 * rows, span), jnp.bfloat16)]
+        + copy_shapes,
+        compiler_params=pltpu.CompilerParams(vmem_limit_bytes=40 * 2**20),
         cost_estimate=HIDDEN_COST,
-        name="gates_both",
-    )(pick, near, far, w_rows, w_rows)
-
-
-def back_kernel(pick_ref, w_ref, mine_ref, other_ref, keep_ref, give_ref, total_ref):
+        name="gates_pool",
+    )(pick, length, own, sibling, w_rows, base, small, grad)
+
+
+def whole_kernel(function, count, *refs):
+    results = function(*[ref[...] for ref in refs[:count]])
+    for ref, result in zip(refs[count:], results):
+        ref[...] = result.astype(ref.dtype)
+
+
+def whole(function, outputs, *operands):
+    return pl.pallas_call(
+        functools.partial(whole_kernel, function, len(operands)),
+        out_shape=[jax.ShapeDtypeStruct(*output) for output in outputs],
+        compiler_params=pltpu.CompilerParams(vmem_limit_bytes=20 * 2**20),
+        cost_estimate=HIDDEN_COST,
+        name="whole",
+    )(*operands)
+
+
+def back_kernel(pick_ref, w_ref, gg_ref, keep_ref, give_ref, total_ref):
     step = pl.program_id(0)
-    kinds, width, columns = w_ref.shape[1:]
-    weights = w_ref[0].reshape(kinds * width, columns)
-
-    def add(grads):
-        product = lax.dot_general(
-            weights, grads, (((0,), (0,)), ((), ())), preferred_element_type=jnp.float32
-        )
-
-        @pl.when(step == 0)
-        def _():
-            total_ref[...] = product
-
-        @pl.when(step > 0)
-        def _():
-            total_ref[...] += product
-
-    @pl.when(step % 2 == 0)
-    def _():
-        add(mine_ref[0].reshape(kinds * width, mine_ref.shape[-1]))
-
-    @pl.when(step % 2 == 1)
-    def _():
-        add(other_ref[0].reshape(kinds * width, other_ref.shape[-1]))
+    columns = w_ref.shape[1]
+    total_ref[pl.ds(pl.multiple_of(step * columns, columns), columns), :] = lax.dot_general(
+        w_ref[...], gg_ref[...], (((0,), (0,)), ((), ())), preferred_element_type=jnp.float32
+    )
 
     @pl.when(step == pl.num_programs(0) - 1)
     def _():
@@ -329,23 +374,18 @@
         ].astype(jnp.bfloat16)
 
 
-def back_products(pick, w_rows, mine, other):
-    taps, kinds, width, depth = w_rows.shape
-    span = mine.shape[-1]
-    columns = depth // 2
-    grads = pl.BlockSpec((1, kinds, width // 2, span), lambda i, p: (i // 2, 0, 0, 0))
+def back_products(pick, weights, gg):
+    depth, columns = weights.shape
+    span = gg.shape[1]
+    part = 384
     return pl.pallas_call(
         back_kernel,
         grid_spec=pltpu.PrefetchScalarGridSpec(
             num_scalar_prefetch=1,
-            grid=(2 * taps,),
+            grid=(columns // part,),
             in_specs=[
-                pl.BlockSpec(
-                    (1, kinds, width // 2, columns),
-                    lambda i, p: (i // 2, 0, jnp.where(i % 2 == 0, p[0], 1 - p[0]), p[1]),
-                ),
-                grads,
-                grads,
+                pl.BlockSpec((depth, part), lambda i, p: (0, i)),
+                once((depth, span)),
             ],
             out_specs=[
                 pl.BlockSpec((columns // 2, span), lambda i, p: (0, 0)),
@@ -357,41 +397,65 @@
             jax.ShapeDtypeStruct((columns // 2, span), jnp.float32),
             jax.ShapeDtypeStruct((columns // 2, span), jnp.bfloat16),
         ],
-        compiler_params=pltpu.CompilerParams(vmem_limit_bytes=48 * 2**20),
+        compiler_params=pltpu.CompilerParams(vmem_limit_bytes=26 * 2**20),
         cost_estimate=HIDDEN_COST,
         name="back_products",
-    )(pick, w_rows, mine, other)
-
-
-def weight_kernel(mine_ref, pair_ref, near_ref, far_ref, pair_near_ref, pair_far_ref, out_ref):
-    def product(gg_ref, x_ref):
-        return lax.dot_general(
-            gg_ref[...], x_ref[...], (((1,), (1,)), ((), ())), preferred_element_type=jnp.float32
-        )
-
-    middle = near_ref.shape[0]
-    out_ref[:, :middle] = (
-        product(mine_ref, near_ref) + product(pair_ref, pair_near_ref)
-    ).astype(jnp.bfloat16)
-    out_ref[:, middle:] = (
-        product(mine_ref, far_ref) + product(pair_ref, pair_far_ref)
-    ).astype(jnp.bfloat16)
-
-
-def weight_products(gg_mine, gg_pair, near, far, pair_near, pair_far, block, first, last):
-    rows, span = gg_mine.shape
-    columns = near.shape[0]
-    grads = pl.BlockSpec((block, span), lambda i: (i + first, 0))
+    )(pick, weights, gg)
+
+
+def chunk_kernel(function, inputs, inner_ref, *refs):
+    function(inner_ref[0] == 1, *refs[:inputs], *refs[inputs:])
+
+
+def chunk_step(function, outputs, inner, size, *operands):
+    specs, arrays = [pl.BlockSpec(memory_space=pltpu.SMEM)], [inner]
+    for operand in operands:
+        array, at = operand if isinstance(operand, tuple) else (operand, 0)
+        specs.append(pl.BlockSpec((size, array.shape[1]), lambda i, at=at: (at, 0)))
+        arrays.append(array)
+    depth = arrays[1].shape[1]
     return pl.pallas_call(
-        weight_kernel,
-        grid=(last - first,),
-        in_specs=[grads, grads] + [once((columns, span))] * 4,
-        out_specs=pl.BlockSpec((block, 2 * columns), lambda i: (i, 0)),
-        out_shape=jax.ShapeDtypeStruct(((last - first) * block, 2 * columns), jnp.bfloat16),
-        compiler_params=pltpu.CompilerParams(vmem_limit_bytes=48 * 2**20),
+        functools.partial(chunk_kernel, function, len(operands)),
+        grid=(1,),
+        in_specs=specs,
+        out_specs=[pl.BlockSpec((size, depth), lambda i: (0, 0))] * outputs,
+        out_shape=[jax.ShapeDtypeStruct((size, depth), jnp.bfloat16)] * outputs,
+        compiler_params=pltpu.CompilerParams(vmem_limit_bytes=8 * 2**20),
         cost_estimate=HIDDEN_COST,
-        name="weight_products",
-    )(gg_mine, gg_pair, near, far, pair_near, pair_far)
+        name="chunk_step",
+    )(*arrays)
+
+
+def rounded_sum(left_ref, right_ref):
+    total = left_ref[...].astype(jnp.float32) + right_ref[...].astype(jnp.float32)
+    return total.astype(jnp.bfloat16)
+
+
+def take_chunk(inner, chunk_ref, out_ref):
+    out_ref[...] = chunk_ref[...]
+
+
+def sum_chunk(inner, chunk_ref, got_ref, sum_ref):
+    sum_ref[...] = rounded_sum(chunk_ref, got_ref)
+
+
+def sum_and_final(inner, chunk_ref, got_ref, total_ref, sum_ref, final_ref):
+    sum_ref[...] = rounded_sum(chunk_ref, got_ref)
+    final_ref[...] = jnp.where(inner, total_ref[...], got_ref[...])
+
+
+def total_and_next(inner, sum_ref, got_ref, chunk_ref, total_ref, next_ref):
+    total = rounded_sum(sum_ref, got_ref)
+    total_ref[...] = total
+    next_ref[...] = jnp.where(inner, total, chunk_ref[...])
+
+
+def final_chunk(inner, got_ref, total_ref, final_ref):
+    final_ref[...] = jnp.where(inner, total_ref[...], got_ref[...])
+
+
+def total_chunk(inner, sum_ref, got_ref, total_ref):
+    total_ref[...] = rounded_sum(sum_ref, got_ref)
 
 
 def even_odd(count):
@@ -470,7 +534,7 @@
         out_specs=pl.BlockSpec((count * size, depth), lambda i: (2 * group + i, 0)),
         out_shape=jax.ShapeDtypeStruct(shape, jnp.float32),
         input_output_aliases=aliases,
-        compiler_params=pltpu.CompilerParams(vmem_limit_bytes=40 * 2**20),
+        compiler_params=pltpu.CompilerParams(vmem_limit_bytes=16 * 2**20),
         cost_estimate=HIDDEN_COST,
         name="write_chunks",
     )(*operands)
@@ -487,45 +551,54 @@
 def piped_sums(order, chunks, pairs, fillers, arrived):
     position = lax.axis_index("dp") // 2
     inner = (position == 1) | (position == 2)
+    flag = inner.astype(jnp.int32).reshape(1)
     edge = line_pairs([(0, 1), (1, 0), (2, 3), (3, 2)])
     middle = line_pairs([(1, 2), (2, 1)])
-    sums, totals, finals, swapped = {}, {}, {}, {}
+    sums, totals, finals = {}, {}, {}
     got_edge, got_middle, got_pair = {}, {}, {}
+    size = chunks[0].shape[0]
+
+    def run(function, outputs, *operands):
+        return order(chunk_step(function, outputs, flag, size, *order(operands)))
+
+    payload = order(chunks[0])
+    got_edge[0] = lax.ppermute(payload, "dp", edge)
     for n in range(CHUNKS + LAG + 3):
-        k = n - 3
-        if 0 <= k < CHUNKS:
-            got = order(got_middle.pop(k))
-            totals[k] = order(add_rounded(sums.pop(k), got))
-        k = n - LAG
-        if n < CHUNKS and 0 <= k < CHUNKS:
-            payload = jnp.where(inner, totals[k], chunks[n])
-        elif n < CHUNKS:
-            payload = chunks[n]
-        elif 0 <= k < CHUNKS:
+        final = None
+        k = n - 1
+        if k in got_edge:
+            got = got_edge.pop(k)
+            if k < CHUNKS and k >= LAG:
+                sums[k], final = run(sum_and_final, 2, chunks[k], got, totals.pop(k - LAG))
+            elif k < CHUNKS:
+                (sums[k],) = run(sum_chunk, 1, chunks[k], got)
+            else:
+                (final,) = run(final_chunk, 1, got, totals.pop(k - LAG))
+            if k < CHUNKS:
+                got_middle[k] = lax.ppermute(sums[k], "dp", middle)
+        k = n - 2
+        payload = None
+        if k in got_middle:
+            got = got_middle.pop(k)
+            (totals[k],) = run(total_chunk, 1, sums.pop(k), got)
+        k = n + 1 - LAG
+        if k in totals and n + 1 < CHUNKS:
+            (payload,) = run(final_chunk, 1, chunks[n + 1], totals[k])
+        elif n + 1 < CHUNKS:
+            payload = order(chunks[n + 1])
+        elif k in totals:
             payload = totals[k]
-        else:
-            payload = None
         if payload is not None:
-            got_edge[n] = lax.ppermute(order(payload), "dp", edge)
+            got_edge[n + 1] = lax.ppermute(payload, "dp", edge)
+        k = n - 1 - LAG
+        if final is not None:
+            finals[k] = final
+            got_pair[k] = lax.ppermute(final, "dp", pairs)
+        k = k - 1
+        if k in got_pair:
+            arrived(k, finals, order(got_pair.pop(k)))
         if n in fillers:
             fillers[n]()
-        k = n - 1
-        if k in got_edge:
-            got = order(got_edge.pop(k))
-            if k < CHUNKS:
-                sums[k] = order(add_rounded(chunks.pop(k), got))
-                got_middle[k] = lax.ppermute(sums[k], "dp", middle)
-            k = k - LAG
-            if 0 <= k < CHUNKS:
-                finals[k] = order(jnp.where(inner, totals.pop(k), got))
-                got_pair[k] = lax.ppermute(finals[k], "dp", pairs)
-        k = n - LAG - 3
-        if 0 <= k < CHUNKS:
-            swapped[k] = order(got_pair.pop(k))
-            arrived(k, finals, swapped)
-    for k in sorted(got_pair):
-        swapped[k] = order(got_pair.pop(k))
-        arrived(k, finals, swapped)
 
 
 def on_device(line, channel_parts, inputs, lengths, start_cell, weight, bias, out_grad, cell_grad):
@@ -564,110 +637,158 @@
         def run(function, *operands):
             return done(function(*done(operands)))
 
-        pick_mine = jnp.stack([side, place // 2, place % 2]).astype(jnp.int32)
-        pick_mine_far = jnp.stack([side, 1 - place // 2, place % 2]).astype(jnp.int32)
-        pick_other = jnp.stack([other_side, place // 2, place % 2]).astype(jnp.int32)
+        pick_near = jnp.stack([side, place // 2, place % 2]).astype(jnp.int32)
+        pick_far = jnp.stack([side, 1 - place // 2, place % 2]).astype(jnp.int32)
+        small_pair = lax.ppermute(small_other, "dp", pairs)
         x_own = run(lambda x: mix(x.T, slots), inputs)
         far_got = lax.ppermute(x_own, "mp", chip_pairs)
         pair_got = lax.ppermute(x_own, "dp", pairs)
         near_got = lax.ppermute(x_own, "mp", core_pairs)
         grads = run(lambda g: mix(g.T, slots), out_grad)
         grads_mine, grads_other = done((half(grads, 0, side), half(grads, 0, other_side)))
-        gates, near = run(gates_step, pick_mine, w_rows, x_own, near_got)
+        gates, near, w_near = run(
+            lambda *given: gates_step(*given, True), pick_near, w_rows, x_own, near_got
+        )
+        cut = width * 2 // 3
         far_own = done(far_got)
         far_got = lax.ppermute(far_own, "mp", core_pairs)
-        x_pair = done(pair_got)
-        pair_far_got = lax.ppermute(x_pair, "mp", chip_pairs)
-        grads_pair = lax.ppermute(grads_other, "dp", pairs)
-        small_pair = lax.ppermute(small_other, "dp", pairs)
+        x_pair, small_pair = done((pair_got, small_pair))
+        relay = [
+            lax.ppermute(x_pair[:cut], "mp", chip_pairs),
+            lax.ppermute(far_own[cut:], "dp", pairs),
+        ]
         far_got = done(far_got)
         pair_near_got = lax.ppermute(done(x_pair), "mp", core_pairs)
-        gates, far = run(gates_step, pick_mine_far, w_rows, far_own, far_got, gates)
-        pair_gates, pair_near = run(gates_step, pick_mine, w_rows, x_pair, pair_near_got)
-        gates, grads_mine = done((gates, grads_mine))
-        hidden_mine, sums_mine, gg_mine = pooled(gates, lengths, done.token, grads_mine)
+        far_own, far_got, gates, grads_mine = done((far_own, far_got, gates, grads_mine))
+        hidden_mine, sums_mine, gg_mine, far, w_far = gates_pool(
+            pick_far, lengths, w_rows, far_own, far_got, gates, done.token, grads_mine, True
+        )
         done.token = sums_mine
-        gg_mine = done(gg_mine)
-        pair_far_own = done(pair_far_got)
+        gg_mine = done(gg_mine.reshape(rows, span))
+        pair_far_own = run(lambda a, b: jnp.concatenate([a, b], axis=0), *relay)
         pair_far_got = lax.ppermute(pair_far_own, "mp", core_pairs)
-        gates_other = run(gates_both, pick_other, w_rows, near, far)
-        pair_gates, pair_far = run(
-            gates_step, pick_mine_far, w_rows, pair_far_own, pair_far_got, pair_gates
+        grads_pair = lax.ppermute(done(grads_other), "dp", pairs)
+        kept = {}
+
+        own_shape, wide_type, sent_type = (width, span), jnp.float32, jnp.bfloat16
+
+        def add(left, right):
+            return (left + right.astype(jnp.float32),)
+
+        def add_both(left, right):
+            total = left + right.astype(jnp.float32)
+            return total, total
+
+        def fill_back(window, part):
+            keep, give = run(
+                back_products,
+                pick_near,
+                (w_near, w_far)[part].reshape(rows, depth // 2),
+                gg_mine if window == 0 else gg_pair,
+            )
+            kept["keep", window, part] = keep
+            kept["core", window, part] = lax.ppermute(give, "mp", core_pairs)
+
+        def fill_core(window, part):
+            kind = wide_type if part == 0 else sent_type
+            (kept["sum", window, part],) = run(
+                lambda *given: whole(add, [(own_shape, kind)], *given),
+                kept["keep", window, part],
+                kept["core", window, part],
+            )
+
+        def fill_cross(window):
+            kept["cross", window] = lax.ppermute(done(kept["sum", window, 1]), "mp", chip_pairs)
+
+        pair_gates, pair_near = run(
+            lambda *given: gates_step(*given, False), pick_near, w_rows, x_pair, pair_near_got
         )
         small_pair, grads_pair = done((small_pair, grads_pair))
         length_pair = small_pair[0, 5:6].astype(jnp.int32)
         small_pair = jnp.where(lane[:own] < 3, small_mine, small_pair)
-        _, sums_pair, gg_pair = run(pooled, pair_gates, length_pair, small_pair, grads_pair)
+        hidden_pair, sums_pair, gg_pair, pair_far = run(
+            lambda *given: gates_pool(*given, False),
+            pick_far,
+            length_pair,
+            w_rows,
+            pair_far_own,
+            pair_far_got,
+            pair_gates,
+            small_pair,
+            grads_pair,
+        )
+        gg_pair = gg_pair.reshape(rows, span)
 
         size = rows // CHUNKS
+        per = own // size
         chunks = {}
 
-        def products(first, last):
-            def fill():
-                part = run(
-                    lambda *at: weight_products(*at, own, first, last),
-                    gg_mine,
-                    gg_pair,
-                    near,
-                    far,
-                    pair_near,
-                    pair_far,
-                )
-                for k in range(first * per, last * per):
-                    at = (k - first * per) * size
-                    chunks[k] = part[at : at + size]
-
-            return fill
-
-        kept = {}
-
-        def fill_pool():
-            kept["pool"] = run(pooled, gates_other, lengths, small_other, grads_other)
-
-        def fill_back(part):
-            def stage():
-                keep, give = run(
-                    back_products,
-                    (pick_mine, pick_mine_far)[part],
-                    w_rows,
-                    gg_mine.reshape(2, 3, own, span),
-                    kept["pool"][2].reshape(2, 3, own, span),
-                )
-                kept["keep", part] = keep
-                kept["got", part] = lax.ppermute(give, "mp", core_pairs)
-
-            return stage
-
-        def fill_cross():
-            far_sum = run(
-                lambda a, b: (a + b.astype(jnp.float32)).astype(jnp.bfloat16),
-                kept["keep", 1],
-                kept["got", 1],
+        def products():
+            def more(total, gg, x):
+                return (total + cols_dot(gg, x)).astype(jnp.bfloat16)
+
+            own_near = run(cols_dot, gg_mine, near)
+            near_part = run(more, own_near, gg_pair, pair_near)
+            own_far = run(cols_dot, gg_mine, far)
+            far_part = run(more, own_far, gg_pair, pair_far)
+            for k in range(CHUNKS):
+                at = slice(k * size, (k + 1) * size)
+                chunks[k] = jnp.concatenate([near_part[at], far_part[at]], axis=1)
+
+        def fill_send():
+            (give,) = run(
+                lambda *given: whole(add, [(own_shape, sent_type)], *given),
+                kept["sum", 1, 0],
+                kept["cross", 1],
             )
-            kept["cross"] = lax.ppermute(far_sum, "mp", chip_pairs)
+            kept["pair"] = lax.ppermute(give, "dp", pairs)
+
+        def unmixed(total, slots):
+            return (
+                lax.dot_general(
+                    total, slots, (((1,), (1,)), ((), ())), preferred_element_type=jnp.float32
+                ),
+            )
+
+        def send(name, value):
+            kept[name] = lax.ppermute(done(value), "dp", pairs)
+
+        def receive(name):
+            kept[name] = done(kept[name])
 
         def fill_input():
-            def total(a, b, c):
-                total = a + b.astype(jnp.float32) + c.astype(jnp.float32)
-                return mix(total.astype(jnp.bfloat16), slots, back=True).T
-
-            kept["input"] = run(total, kept["keep", 0], kept["got", 0], kept["cross"])
+            def total(near_sum, cross, pair, slots):
+                total = near_sum + cross.astype(jnp.float32) + pair.astype(jnp.float32)
+                return unmixed(total.astype(jnp.bfloat16), slots)
+
+            (total,) = run(
+                lambda *given: whole(total, [(own_shape, sent_type)], *given),
+                kept["sum", 0, 0],
+                kept["cross", 0],
+                kept["pair"],
+                slots,
+            )
+            kept["input"] = total.T
 
         def fill_hidden():
-            def whole(mine, other):
-                return mix(join(is_low, mine, other, 0), slots, back=True).T
-
-            kept["hidden"] = run(whole, hidden_mine, kept["pool"][0])
-
-        per = own // size
-        bias_sums = run(jnp.add, sums_mine, sums_pair)
+            low, high = done((hidden_mine, kept["hidden"]))
+            low, high = jnp.where(is_low, low, high), jnp.where(is_low, high, low)
+
+            def both(low, high, slots):
+                return unmixed(jnp.concatenate([low, high], axis=0), slots)
+
+            (total,) = run(
+                lambda *given: whole(both, [(own_shape, sent_type)], *given), low, high, slots
+            )
+            kept["hidden out"] = total.T
+
         position = lax.axis_index("dp") // 2
         inner = (position == 1) | (position == 2)
 
         def fill_bias(stage):
             def run_stage():
                 if stage == 0:
-                    kept["bias"] = done(bias_sums)
+                    kept["bias"] = run(jnp.add, sums_mine, sums_pair)
                     moves = [(0, 1), (1, 0), (2, 3), (3, 2)]
                 elif stage == 1:
                     kept["bias"] = run(jnp.add, kept["bias"], kept["bias got"])
@@ -691,35 +812,54 @@
         flags = jnp.stack([side, place // 2]).astype(jnp.int32)
         kept["out"] = None
 
-        def arrived(k, finals, swapped):
+        swapped = {}
+
+        def arrived(k, finals, got):
+            swapped[k] = got
             group = k // per
             members = range(group * per, (group + 1) * per)
             if k == members[-1]:
                 parts = done(([finals[m] for m in members], [swapped[m] for m in members]))
                 kept["out"] = done(write_chunks(flags, *parts, group, kept["out"], (2 * rows, depth)))
 
-        products(0, 1)()
+        def fill(*steps):
+            def run_all():
+                for step, *given in steps:
+                    step(*given)
+
+            return run_all
+
+        fill_bias(0)()
+        send("hidden", hidden_pair)
+        fill_back(1, 1)
+        fill_back(1, 0)
+        fill_core(1, 1)
+        fill_cross(1)
+        fill_bias(1)()
+        fill_back(0, 1)
+        fill_core(1, 0)
+        fill_bias(2)()
+        fill_back(0, 0)
+        fill_core(0, 1)
+        fill_bias(3)()
+        products()
+        fill_core(0, 0)
+        receive("hidden")
+        fill_bias(4)()
         fillers = {
-            1: products(1, 3),
-            2: fill_pool,
-            3: fill_back(1),
-            4: products(3, 6),
-            5: fill_back(0),
-            6: fill_cross,
-            7: fill_bias(0),
-            8: fill_hidden,
-            9: fill_bias(1),
-            11: fill_input,
-            12: fill_bias(2),
-            14: fill_bias(3),
-            16: fill_bias(4),
+            0: fill((receive, ("cross", 1)), (fill_cross, 0)),
+            1: fill((fill_send,)),
+            3: fill((receive, ("cross", 0))),
+            4: fill((receive, "pair")),
+            CHUNKS - 1: fill((fill_hidden,)),
+            CHUNKS: fill((send, "sums", sums_pair)),
+            CHUNKS + 2: fill((receive, "sums"), (fill_input,)),
         }
         piped_sums(done, chunks, pairs, fillers, arrived)
-        hidden_other, sums_other, _ = kept["pool"]
-        input_grad, hidden = kept["input"], kept["hidden"]
+        input_grad, hidden = kept["input"], kept["hidden out"]
         wgrad = kept["out"].reshape(2, 3, width, depth)
         bias_grad = join(is_low, kept["bias"], kept["bias got"], 0)[:, 2:5].T
-        sums_mine = done.token
+        sums_mine, sums_other = done.token, kept["sums"]
     else:
         x_own = mix(inputs.T, slots)
         grads = mix(out_grad.T, slots)

time: 494 us -> 457 us (0.925)
  Pallas kernels: 185 us -> 132 us
  waiting for transfers between devices: 102 us -> 71.5 us
  matrix products: 15 us -> 41 us
  starting transfers between devices: 137 us -> 154 us
    dot_general x0 -> x4, matrix products: none -> 33.1 us  [cols_dot(): lax.dot_general(left, right, (((1,), (1,)), ((), ())), preferred_element_...]
    ppermute x45 -> x52, waiting for transfers between devices: 88.6 us -> 57 us  [the longest x21 23.1 us: piped_sums(): got_edge[n + 1] = lax.ppermute(payload, 'dp', edge)]
    pallas_call x4 -> x2, Pallas kernels: 46.1 us -> 17.8 us  [gates_step(): pl.pallas_call(gates_kernel, grid_spec=pltpu.PrefetchScalarGridSpec(num_s...]
    pallas_call x7 -> x63, Pallas kernels: 81.1 us -> 62.4 us  [the longest x2 38.9 us: gates_pool(): pl.pallas_call(gates_pool_kernel, grid_spec=pltpu.PrefetchScalarGridSpec(...]
    pallas_call x2 -> x4, Pallas kernels: 38.5 us -> 30.8 us  [back_products(): pl.pallas_call(back_kernel, grid_spec=pltpu.PrefetchScalarGridSpec(num_sc...]
    dot_general x4 -> x2, matrix products: 15 us -> 7.91 us  [mix(): lax.dot_general(block, order, dims, preferred_element_type=jnp.float32)]
    ppermute x3, starting transfers between devices: 4.41 us -> 10.4 us  [run_stage(): kept['bias got'] = lax.ppermute(kept['bias'], 'dp', line_pairs(moves))]
    ppermute x45 -> x52, starting transfers between devices: 114 us -> 120 us  [the longest x21 87.3 us: piped_sums(): got_edge[n + 1] = lax.ppermute(payload, 'dp', edge)]
  transfers between devices with their start and end apart: 74 -> 81, of which waited for: 21 -> 22; matrix products, arithmetic and copies ran while one was open for 4% -> 12% of each run, Pallas kernels for 34% -> 23%
where the time goes in v3:
time: 457 us; the launch traced here: 450 us
  starting transfers between devices  154 us (34%)
  Pallas kernels  132 us (29%)
  waiting for transfers between devices  71.5 us (16%)
  matrix products  41 us (9%)
  local copies, waits for them, and re-layouts  36.2 us (8%)
  other arithmetic  11.5 us (3%)
    ppermute x21, starting transfers between devices, piped_sums(): got_edge[n + 1] = lax.ppermute(payload, 'dp', edge)  87.3 us
    pallas_call x2, Pallas kernels, gates_pool(): pl.pallas_call(gates_pool_kernel, grid_spec=pltpu.PrefetchScalarGridSpec(...  38.9 us
    dot_general x4, matrix products, cols_dot(): lax.dot_general(left, right, (((1,), (1,)), ((), ())), preferred_element_...  33.1 us
    pallas_call x4, Pallas kernels, back_products(): pl.pallas_call(back_kernel, grid_spec=pltpu.PrefetchScalarGridSpec(num_sc...  30.8 us
    unnamed x191, local copies, waits for them, and re-layouts  27 us
    ppermute x18, starting transfers between devices, piped_sums(): got_pair[k] = lax.ppermute(final, 'dp', pairs)  24 us
    ppermute x21, waiting for transfers between devices, piped_sums(): got_edge[n + 1] = lax.ppermute(payload, 'dp', edge)  23.1 us
    pallas_call x6, Pallas kernels, write_chunks(): pl.pallas_call(functools.partial(write_kernel, count), grid=(2,), in_spec...  20.5 us
  transfers between devices with their start and end apart: 81, of which 22 were waited for; matrix products, arithmetic and copies ran while one was open for 12% of the time, Pallas kernels for 23%

profile of v3, /device:TPU:0, one launch (start us, length us, event | category | flops | bytes accessed | tf_op | source)
XLA Modules:
  0.0 449.8 jit_solution(14087590203532679958)
XLA Ops:
  17.3 9.4 %gates_step.2 = (f32[2,3,288,1152]{3,2,1,0:T(8,128)S(1)}, bf16[1152,1152]{1,0:T(8,128)(2,1)S(1)}, bf16[2,3,288,1152]{3,2,1,0:T(8,128)(2,1)S(1)}) custom-call(s32[3]{0:T(128)S(1)} %add_add_fusion.1.pick_ref, bf16[576,1152]{1,0:T(8,128)(2,1)} %convolution_convert_fusion.1.low_ref, bf16[576,1152]{1,0:T(8,128)(2,1)} %collective-permute-done.1.high_ref, ...), custom_call_target="tpu_custom_call" | custom-call | flops 1 | bytes 1 | tf_op jit(solution)/shard_map/gates_step/pallas_call | solution.py:248
  33.5 7.2 %collective-permute-done.low_ref = bf16[576,1152]{1,0:T(8,128)(2,1)S(1)} collective-permute-done((bf16[576,1152]{1,0:T(8,128)(2,1)}, bf16[576,1152]{1,0:T(8,128)(2,1)S(1)}, u32[]{:S(2)}, u32[]{:S(2)}) %collective-permute-start) | collective-permute-done | bytes 1327136 | tf_op jit(solution)/shard_map/ppermute | solution.py:644
  42.4 4.5 %collective-permute-done.4 = f32[288,128]{1,0:T(8,128)S(1)} collective-permute-done((f32[288,128]{1,0:T(8,128)S(1)}, f32[288,128]{1,0:T(8,128)S(1)}, u32[]{:S(2)}, u32[]{:S(2)}) %collective-permute-start.4) | collective-permute-done | bytes 147488 | tf_op jit(solution)/shard_map/ppermute | solution.py:642
  52.7 19.9 %gates_pool.2 = (bf16[288,1152]{1,0:T(8,128)(2,1)S(1)}, f32[288,128]{1,0:T(8,128)S(1)}, bf16[2,3,288,1152]{3,2,1,0:T(8,128)(2,1)S(1)}, bf16[1152,1152]{1,0:T(8,128)(2,1)S(1)}, bf16[2,3,288,1152]{3,2,1,0:T(8,128)(2,1)}) custom-call(s32[3]{0:T(128)S(1)} %add_add_fusion.pick_ref, s32[1]{0:T(128)S(6)} %copy.33.length_ref, ...), custom_call_target="tpu_custom_call" | custom-call | flops 1 | bytes 1 | tf_op jit(solution)/shard_map/gates_pool/pallas_call | solution.py:311
  77.7 8.3 %gates_step.3 = (f32[2,3,288,1152]{3,2,1,0:T(8,128)S(1)}, bf16[1152,1152]{1,0:T(8,128)(2,1)S(1)}) custom-call(s32[3]{0:T(128)S(1)} %add_add_fusion.1.pick_ref, bf16[576,1152]{1,0:T(8,128)(2,1)S(1)} %collective-permute-done.3.low_ref, bf16[576,1152]{1,0:T(8,128)(2,1)S(1)} %collective-permute-done.8.high_ref, bf16[2,3,576,2304]{3,2,1,0:T(8,128)(2,1)} %bitcast.45), custom_call_target="tpu_custom_call" | custom-call | flops 1 | bytes 1 | tf_op jit(solution)/shard_map/gates_step/pallas_call | solution.py:248
  95.7 19.0 %gates_pool.3 = (bf16[288,1152]{1,0:T(8,128)(2,1)}, f32[288,128]{1,0:T(8,128)S(1)}, bf16[2,3,288,1152]{3,2,1,0:T(8,128)(2,1)S(1)}, bf16[1152,1152]{1,0:T(8,128)(2,1)S(1)}) custom-call(s32[3]{0:T(128)S(1)} %add_add_fusion.pick_ref, s32[1]{0:T(128)} %bitcast.8.length_ref, bf16[576,1152]{1,0:T(8,128)(2,1)S(1)} %pad_maximum_fusion.low_ref, ...), custom_call_target="tpu_custom_call" | custom-call | flops 1 | bytes 1 | tf_op jit(solution)/shard_map/gates_pool/pallas_call | solution.py:311
  114.8 7.7 %back_products.4 = (f32[576,1152]{1,0:T(8,128)S(1)}, bf16[576,1152]{1,0:T(8,128)(2,1)S(1)}) custom-call(s32[3]{0:T(128)S(1)} %add_add_fusion.1.pick_ref, bf16[1728,1152]{1,0:T(8,128)(2,1)S(1)} %bitcast.40, bf16[1728,1152]{1,0:T(8,128)(2,1)S(1)} %bitcast.36), custom_call_target="tpu_custom_call" | custom-call | flops 1 | bytes 1 | tf_op jit(solution)/shard_map/back_products/pallas_call | solution.py:381
  124.3 7.3 %back_products.5 = (f32[576,1152]{1,0:T(8,128)S(1)}, bf16[576,1152]{1,0:T(8,128)(2,1)S(1)}) custom-call(s32[3]{0:T(128)S(1)} %add_add_fusion.1.pick_ref, bf16[1728,1152]{1,0:T(8,128)(2,1)S(1)} %bitcast.30, bf16[1728,1152]{1,0:T(8,128)(2,1)S(1)} %bitcast.37), custom_call_target="tpu_custom_call" | custom-call | flops 1 | bytes 1 | tf_op jit(solution)/shard_map/back_products/pallas_call | solution.py:381
  133.2 8.4 %back_products.6 = (f32[576,1152]{1,0:T(8,128)S(1)}, bf16[576,1152]{1,0:T(8,128)(2,1)}) custom-call(s32[3]{0:T(128)S(1)} %add_add_fusion.1.pick_ref, bf16[1728,1152]{1,0:T(8,128)(2,1)S(1)} %bitcast.41, bf16[1728,1152]{1,0:T(8,128)(2,1)S(1)} %bitcast.32), custom_call_target="tpu_custom_call" | custom-call | flops 1 | bytes 1 | tf_op jit(solution)/shard_map/back_products/pallas_call | solution.py:381
  143.1 8.1 %collective-permute-start.16 = (f32[288,128]{1,0:T(8,128)S(1)}, f32[288,128]{1,0:T(8,128)S(1)}, u32[]{:S(2)}, u32[]{:S(2)}) collective-permute-start(f32[288,128]{1,0:T(8,128)S(1)} %add.67), channel_id=1, source_target_pairs={{8,0},{12,4},{16,24},{20,28},{0,8},{4,12},{24,16},{28,20},{9,1},{1... | collective-permute-start | bytes 442376 | tf_op jit(solution)/shard_map/ppermute | solution.py:804
  156.5 7.4 %back_products.7 = (f32[576,1152]{1,0:T(8,128)S(1)}, bf16[576,1152]{1,0:T(8,128)(2,1)S(1)}) custom-call(s32[3]{0:T(128)S(1)} %add_add_fusion.1.pick_ref, bf16[1728,1152]{1,0:T(8,128)(2,1)S(1)} %bitcast.31, bf16[1728,1152]{1,0:T(8,128)(2,1)S(1)} %bitcast.33), custom_call_target="tpu_custom_call" | custom-call | flops 1 | bytes 1 | tf_op jit(solution)/shard_map/back_products/pallas_call | solution.py:381
  166.9 8.0 %fusion.13 = f32[1728,1152]{1,0:T(8,128)} fusion(bf16[1728,1152]{1,0:T(8,128)(2,1)S(1)} %bitcast.34, bf16[1152,1152]{1,0:T(8,128)(2,1)S(1)} %copy-done.40), kind=kOutput, calls=%fused_computation.61 | convolution fusion | flops 4586471424 | bytes 14598144 | tf_op jit(solution)/shard_map/dot_general | solution.py:204
  175.0 8.5 %fusion = bf16[1728,1152]{1,0:T(8,128)(2,1)S(1)} fusion(f32[1728,1152]{1,0:T(8,128)} %fusion.13, bf16[1728,1152]{1,0:T(8,128)(2,1)S(1)} %bitcast.38, bf16[1152,1152]{1,0:T(8,128)(2,1)S(1)} %copy-done.44), kind=kOutput, calls=%fused_computation.2 | convolution fusion | flops 4590452736 | bytes 18579456 | tf_op jit(solution)/shard_map/dot_general | solution.py:204
  183.5 8.0 %fusion.14 = f32[1728,1152]{1,0:T(8,128)} fusion(bf16[1728,1152]{1,0:T(8,128)(2,1)S(1)} %bitcast.35, bf16[1152,1152]{1,0:T(8,128)(2,1)S(1)} %copy-done.42), kind=kOutput, calls=%fused_computation.62 | convolution fusion | flops 4586471424 | bytes 14598144 | tf_op jit(solution)/shard_map/dot_general | solution.py:204
  191.5 8.5 %fusion.1 = bf16[1728,1152]{1,0:T(8,128)(2,1)S(1)} fusion(f32[1728,1152]{1,0:T(8,128)} %fusion.14, bf16[1728,1152]{1,0:T(8,128)(2,1)S(1)} %bitcast.39, bf16[1152,1152]{1,0:T(8,128)(2,1)S(1)} %copy-done.46), kind=kOutput, calls=%fused_computation.3 | convolution fusion | flops 4590452736 | bytes 18579456 | tf_op jit(solution)/shard_map/dot_general | solution.py:204
  215.4 7.5 %collective-permute-done.21.refs_1_ = bf16[96,2304]{1,0:T(8,128)(2,1)} collective-permute-done((bf16[96,2304]{1,0:T(8,128)(2,1)S(1)}, bf16[96,2304]{1,0:T(8,128)(2,1)}, u32[]{:S(2)}, u32[]{:S(2)}) %collective-permute-start.21) | collective-permute-done | bytes 442400 | tf_op jit(solution)/shard_map/ppermute | solution.py:565
  233.3 6.8 %collective-permute-start.26 = (bf16[96,2304]{1,0:T(8,128)(2,1)S(1)}, bf16[96,2304]{1,0:T(8,128)(2,1)S(1)}, u32[]{:S(2)}, u32[]{:S(2)}) collective-permute-start(bf16[96,2304]{1,0:T(8,128)(2,1)S(1)} %pad_maximum_fusion.7.refs_0_), channel_id=1, source_target_pairs={{0,8},{4,12},{8,0},{12,4},{16,24},{20,28},{24,16},{28,20},{1,9},{5... | collective-permute-start | bytes 1327112 | tf_op jit(solution)/shard_map/ppermute | solution.py:592
  243.0 6.4 %collective-permute-start.30 = (bf16[96,2304]{1,0:T(8,128)(2,1)S(1)}, bf16[96,2304]{1,0:T(8,128)(2,1)S(1)}, u32[]{:S(2)}, u32[]{:S(2)}) collective-permute-start(bf16[96,2304]{1,0:T(8,128)(2,1)S(1)} %chunk_step.59), channel_id=1, source_target_pairs={{0,8},{4,12},{8,0},{12,4},{16,24},{20,28},{24,16},{28,20},{1,9},{5... | collective-permute-start | bytes 1327112 | tf_op jit(solution)/shard_map/ppermute | solution.py:592
  252.4 6.5 %collective-permute-start.28 = (bf16[96,2304]{1,0:T(8,128)(2,1)S(1)}, bf16[96,2304]{1,0:T(8,128)(2,1)S(1)}, u32[]{:S(2)}, u32[]{:S(2)}) collective-permute-start(bf16[96,2304]{1,0:T(8,128)(2,1)S(1)} %chunk_step.62), channel_id=1, source_target_pairs={{0,8},{4,12},{8,0},{12,4},{16,24},{20,28},{24,16},{28,20},{1,9},{5... | collective-permute-start | bytes 1327112 | tf_op jit(solution)/shard_map/ppermute | solution.py:592
  263.6 4.8 %collective-permute-start.33 = (bf16[96,2304]{1,0:T(8,128)(2,1)S(1)}, bf16[96,2304]{1,0:T(8,128)(2,1)S(1)}, u32[]{:S(2)}, u32[]{:S(2)}) collective-permute-start(bf16[96,2304]{1,0:T(8,128)(2,1)S(1)} %chunk_step.65), channel_id=1, source_target_pairs={{0,8},{4,12},{8,0},{12,4},{16,24},{20,28},{24,16},{28,20},{1,9},{5... | collective-permute-start | bytes 1327112 | tf_op jit(solution)/shard_map/ppermute | solution.py:592
  273.1 4.8 %collective-permute-start.37 = (bf16[96,2304]{1,0:T(8,128)(2,1)S(1)}, bf16[96,2304]{1,0:T(8,128)(2,1)S(1)}, u32[]{:S(2)}, u32[]{:S(2)}) collective-permute-start(bf16[96,2304]{1,0:T(8,128)(2,1)S(1)} %chunk_step.68), channel_id=1, source_target_pairs={{0,8},{4,12},{8,0},{12,4},{16,24},{20,28},{24,16},{28,20},{1,9},{5... | collective-permute-start | bytes 1327112 | tf_op jit(solution)/shard_map/ppermute | solution.py:592
  282.4 5.0 %collective-permute-start.42 = (bf16[96,2304]{1,0:T(8,128)(2,1)S(1)}, bf16[96,2304]{1,0:T(8,128)(2,1)S(1)}, u32[]{:S(2)}, u32[]{:S(2)}) collective-permute-start(bf16[96,2304]{1,0:T(8,128)(2,1)S(1)} %chunk_step.71), channel_id=1, source_target_pairs={{0,8},{4,12},{8,0},{12,4},{16,24},{20,28},{24,16},{28,20},{1,9},{5... | collective-permute-start | bytes 1327112 | tf_op jit(solution)/shard_map/ppermute | solution.py:592
  291.8 5.0 %collective-permute-start.39 = (bf16[96,2304]{1,0:T(8,128)(2,1)S(1)}, bf16[96,2304]{1,0:T(8,128)(2,1)S(1)}, u32[]{:S(2)}, u32[]{:S(2)}) collective-permute-start(bf16[96,2304]{1,0:T(8,128)(2,1)S(1)} %chunk_step.74), channel_id=1, source_target_pairs={{0,8},{4,12},{8,0},{12,4},{16,24},{20,28},{24,16},{28,20},{1,9},{5... | collective-permute-start | bytes 1327112 | tf_op jit(solution)/shard_map/ppermute | solution.py:592
  301.7 6.1 %collective-permute-start.45 = (bf16[96,2304]{1,0:T(8,128)(2,1)S(1)}, bf16[96,2304]{1,0:T(8,128)(2,1)S(1)}, u32[]{:S(2)}, u32[]{:S(2)}) collective-permute-start(bf16[96,2304]{1,0:T(8,128)(2,1)S(1)} %chunk_step.77), channel_id=1, source_target_pairs={{0,8},{4,12},{8,0},{12,4},{16,24},{20,28},{24,16},{28,20},{1,9},{5... | collective-permute-start | bytes 1327112 | tf_op jit(solution)/shard_map/ppermute | solution.py:592
  311.2 6.9 %collective-permute-start.49 = (bf16[96,2304]{1,0:T(8,128)(2,1)S(1)}, bf16[96,2304]{1,0:T(8,128)(2,1)S(1)}, u32[]{:S(2)}, u32[]{:S(2)}) collective-permute-start(bf16[96,2304]{1,0:T(8,128)(2,1)S(1)} %chunk_step.80), channel_id=1, source_target_pairs={{0,8},{4,12},{8,0},{12,4},{16,24},{20,28},{24,16},{28,20},{1,9},{5... | collective-permute-start | bytes 1327112 | tf_op jit(solution)/shard_map/ppermute | solution.py:592
  322.0 8.0 %collective-permute-start.54 = (bf16[96,2304]{1,0:T(8,128)(2,1)S(1)}, bf16[96,2304]{1,0:T(8,128)(2,1)S(1)}, u32[]{:S(2)}, u32[]{:S(2)}) collective-permute-start(bf16[96,2304]{1,0:T(8,128)(2,1)S(1)} %chunk_step.83), channel_id=1, source_target_pairs={{0,8},{4,12},{8,0},{12,4},{16,24},{20,28},{24,16},{28,20},{1,9},{5... | collective-permute-start | bytes 1327112 | tf_op jit(solution)/shard_map/ppermute | solution.py:592
  341.0 5.9 %collective-permute-done.52.refs_4_ = bf16[96,2304]{1,0:T(8,128)(2,1)S(1)} collective-permute-done((bf16[96,2304]{1,0:T(8,128)(2,1)S(1)}, bf16[96,2304]{1,0:T(8,128)(2,1)S(1)}, u32[]{:S(2)}, u32[]{:S(2)}) %collective-permute-start.52) | collective-permute-done | bytes 442400 | tf_op jit(solution)/shard_map/ppermute | solution.py:596
  351.8 4.8 %collective-permute-start.59 = (bf16[96,2304]{1,0:T(8,128)(2,1)S(1)}, bf16[96,2304]{1,0:T(8,128)(2,1)S(1)}, u32[]{:S(2)}, u32[]{:S(2)}) collective-permute-start(bf16[96,2304]{1,0:T(8,128)(2,1)S(1)} %chunk_step.92), channel_id=1, source_target_pairs={{0,8},{4,12},{8,0},{12,4},{16,24},{20,28},{24,16},{28,20},{1,9},{5... | collective-permute-start | bytes 1327112 | tf_op jit(solution)/shard_map/ppermute | solution.py:592
  394.8 6.5 %collective-permute-start.67 = (bf16[96,2304]{1,0:T(8,128)(2,1)S(1)}, bf16[96,2304]{1,0:T(8,128)(2,1)S(1)}, u32[]{:S(2)}, u32[]{:S(2)}) collective-permute-start(bf16[96,2304]{1,0:T(8,128)(2,1)S(1)} %chunk_step.100.refs_1_), channel_id=1, source_target_pairs={{0,8},{4,12},{8,0},{12,4},{16,24},{20,28},{24,16},{28,20},{1,9},{5... | collective-permute-start | bytes 1327112 | tf_op jit(solution)/shard_map/ppermute | solution.py:592
  406.4 5.6 %collective-permute-done.67.refs_0_ = bf16[96,2304]{1,0:T(8,128)(2,1)S(1)} collective-permute-done((bf16[96,2304]{1,0:T(8,128)(2,1)S(1)}, bf16[96,2304]{1,0:T(8,128)(2,1)S(1)}, u32[]{:S(2)}, u32[]{:S(2)}) %collective-permute-start.67) | collective-permute-done | bytes 442400 | tf_op jit(solution)/shard_map/ppermute | solution.py:592
  422.7 4.5 whole.13
  430.4 5.8 %collective-permute-done.79.refs_4_ = bf16[96,2304]{1,0:T(8,128)(2,1)S(1)} collective-permute-done((bf16[96,2304]{1,0:T(8,128)(2,1)S(1)}, bf16[96,2304]{1,0:T(8,128)(2,1)S(1)}, u32[]{:S(2)}, u32[]{:S(2)}) %collective-permute-start.79) | collective-permute-done | bytes 442400 | tf_op jit(solution)/shard_map/ppermute | solution.py:596
  (452 shorter events, 204.5 us)
Async XLA Ops:
  8.1 32.5 %collective-permute-start = (bf16[576,1152]{1,0:T(8,128)(2,1)}, bf16[576,1152]{1,0:T(8,128)(2,1)S(1)}, u32[]{:S(2)}, u32[]{:S(2)}) collective-permute-start(bf16[576,1152]{1,0:T(8,128)(2,1)} %convolution_convert_fusion.1.low_ref), channel_id=1, source_target_pairs={{0,2},{1,3},{2,0},{3,1},{4,6},{5,7},{6,4},{7,5},{8,10},{9,11},{10,... | collective-permute-start | bytes 3981320 | tf_op jit(solution)/shard_map/ppermute | solution.py:644
  10.6 36.3 %collective-permute-start.3 = (bf16[576,1152]{1,0:T(8,128)(2,1)}, bf16[576,1152]{1,0:T(8,128)(2,1)S(1)}, u32[]{:S(2)}, u32[]{:S(2)}) collective-permute-start(bf16[576,1152]{1,0:T(8,128)(2,1)} %convolution_convert_fusion.1.low_ref), channel_id=1, source_target_pairs={{0,4},{4,0},{8,12},{12,8},{16,20},{20,16},{24,28},{28,24},{1,5},{5... | collective-permute-start | bytes 3981320 | tf_op jit(solution)/shard_map/ppermute | solution.py:645
  48.6 25.6 %collective-permute-start.5 = (bf16[384,1152]{1,0:T(8,128)(2,1)}, bf16[384,1152]{1,0:T(8,128)(2,1)}, u32[]{:S(2)}, u32[]{:S(2)}) collective-permute-start(bf16[384,1152]{1,0:T(8,128)(2,1)} %slice.129), channel_id=1, source_target_pairs={{0,2},{1,3},{2,0},{3,1},{4,6},{5,7},{6,4},{7,5},{8,10},{9,11},{10,... | collective-permute-start | bytes 2654216 | tf_op jit(solution)/shard_map/ppermute | solution.py:657
  51.1 23.0 %collective-permute-start.6 = (bf16[192,1152]{1,0:T(8,128)(2,1)}, bf16[192,1152]{1,0:T(8,128)(2,1)}, u32[]{:S(2)}, u32[]{:S(2)}) collective-permute-start(bf16[192,1152]{1,0:T(8,128)(2,1)} %slice.130), channel_id=1, source_target_pairs={{0,4},{4,0},{8,12},{12,8},{16,20},{20,16},{24,28},{28,24},{1,5},{5... | collective-permute-start | bytes 1327112 | tf_op jit(solution)/shard_map/ppermute | solution.py:658
  77.0 18.7 %collective-permute-start.9 = (bf16[576,1152]{1,0:T(8,128)(2,1)S(1)}, bf16[576,1152]{1,0:T(8,128)(2,1)S(1)}, u32[]{:S(2)}, u32[]{:S(2)}) collective-permute-start(bf16[576,1152]{1,0:T(8,128)(2,1)S(1)} %pad_maximum_fusion.low_ref), channel_id=1, source_target_pairs={{0,1},{1,0},{2,3},{3,2},{4,5},{5,4},{6,7},{7,6},{8,9},{9,8},{10,11... | collective-permute-start | bytes 3981320 | tf_op jit(solution)/shard_map/ppermute | solution.py:669
  77.2 17.2 %collective-permute-start.7 = (bf16[288,1152]{1,0:T(8,128)(2,1)S(1)}, bf16[288,1152]{1,0:T(8,128)(2,1)S(1)}, u32[]{:S(2)}, u32[]{:S(2)}) collective-permute-start(bf16[288,1152]{1,0:T(8,128)(2,1)S(1)} %copy-done.75), channel_id=1, source_target_pairs={{0,4},{4,0},{8,12},{12,8},{16,20},{20,16},{24,28},{28,24},{1,5},{5... | collective-permute-start | bytes 1990664 | tf_op jit(solution)/shard_map/ppermute | solution.py:670
  141.5 22.4 %collective-permute-start.17 = (bf16[576,1152]{1,0:T(8,128)(2,1)}, bf16[576,1152]{1,0:T(8,128)(2,1)}, u32[]{:S(2)}, u32[]{:S(2)}) collective-permute-start(bf16[576,1152]{1,0:T(8,128)(2,1)} %get-tuple-element.788), channel_id=1, source_target_pairs={{0,1},{1,0},{2,3},{3,2},{4,5},{5,4},{6,7},{7,6},{8,9},{9,8},{10,11... | collective-permute-start | bytes 3981320 | tf_op jit(solution)/shard_map/ppermute | solution.py:690
  143.1 23.8 %collective-permute-start.16 = (f32[288,128]{1,0:T(8,128)S(1)}, f32[288,128]{1,0:T(8,128)S(1)}, u32[]{:S(2)}, u32[]{:S(2)}) collective-permute-start(f32[288,128]{1,0:T(8,128)S(1)} %add.67), channel_id=1, source_target_pairs={{8,0},{12,4},{16,24},{20,28},{0,8},{4,12},{24,16},{28,20},{9,1},{1... | collective-permute-start | bytes 442376 | tf_op jit(solution)/shard_map/ppermute | solution.py:804
  151.2 55.7 %collective-permute-start.10 = (bf16[288,1152]{1,0:T(8,128)(2,1)}, bf16[288,1152]{1,0:T(8,128)(2,1)}, u32[]{:S(2)}, u32[]{:S(2)}) collective-permute-start(bf16[288,1152]{1,0:T(8,128)(2,1)} %get-tuple-element.727), channel_id=1, source_target_pairs={{0,4},{4,0},{8,12},{12,8},{16,20},{20,16},{24,28},{28,24},{1,5},{5... | collective-permute-start | bytes 1990664 | tf_op jit(solution)/shard_map/ppermute | solution.py:754
  151.7 58.1 %collective-permute-start.20 = (bf16[576,1152]{1,0:T(8,128)(2,1)}, bf16[576,1152]{1,0:T(8,128)(2,1)S(1)}, u32[]{:S(2)}, u32[]{:S(2)}) collective-permute-start(bf16[576,1152]{1,0:T(8,128)(2,1)} %copy-done.21), channel_id=1, source_target_pairs={{0,2},{1,3},{2,0},{3,1},{4,6},{5,7},{6,4},{7,5},{8,10},{9,11},{10,... | collective-permute-start | bytes 3981320 | tf_op jit(solution)/shard_map/ppermute | solution.py:701
  163.9 41.3 %collective-permute-start.15 = (bf16[576,1152]{1,0:T(8,128)(2,1)S(1)}, bf16[576,1152]{1,0:T(8,128)(2,1)S(1)}, u32[]{:S(2)}, u32[]{:S(2)}) collective-permute-start(bf16[576,1152]{1,0:T(8,128)(2,1)S(1)} %get-tuple-element.783), channel_id=1, source_target_pairs={{0,1},{1,0},{2,3},{3,2},{4,5},{5,4},{6,7},{7,6},{8,9},{9,8},{10,11... | collective-permute-start | bytes 3981320 | tf_op jit(solution)/shard_map/ppermute | solution.py:690
  211.4 38.0 %collective-permute-start.27 = (bf16[576,1152]{1,0:T(8,128)(2,1)}, bf16[576,1152]{1,0:T(8,128)(2,1)}, u32[]{:S(2)}, u32[]{:S(2)}) collective-permute-start(bf16[576,1152]{1,0:T(8,128)(2,1)} %whole.9), channel_id=1, source_target_pairs={{0,2},{1,3},{2,0},{3,1},{4,6},{5,7},{6,4},{7,5},{8,10},{9,11},{10,... | collective-permute-start | bytes 3981320 | tf_op jit(solution)/shard_map/ppermute | solution.py:701
  212.9 19.3 %collective-permute-start.19 = (bf16[96,2304]{1,0:T(8,128)(2,1)S(1)}, bf16[96,2304]{1,0:T(8,128)(2,1)S(1)}, u32[]{:S(2)}, u32[]{:S(2)}) collective-permute-start(bf16[96,2304]{1,0:T(8,128)(2,1)S(1)} %pad_maximum_fusion.4.refs_0_), channel_id=1, source_target_pairs={{0,8},{4,12},{8,0},{12,4},{16,24},{20,28},{24,16},{28,20},{1,9},{5... | collective-permute-start | bytes 1327112 | tf_op jit(solution)/shard_map/ppermute | solution.py:592
  224.3 34.6 %collective-permute-start.31 = (bf16[576,1152]{1,0:T(8,128)(2,1)S(1)}, bf16[576,1152]{1,0:T(8,128)(2,1)S(1)}, u32[]{:S(2)}, u32[]{:S(2)}) collective-permute-start(bf16[576,1152]{1,0:T(8,128)(2,1)S(1)} %whole.11), channel_id=1, source_target_pairs={{0,4},{4,0},{8,12},{12,8},{16,20},{20,16},{24,28},{28,24},{1,5},{5... | collective-permute-start | bytes 3981320 | tf_op jit(solution)/shard_map/ppermute | solution.py:744
  233.3 18.0 %collective-permute-start.26 = (bf16[96,2304]{1,0:T(8,128)(2,1)S(1)}, bf16[96,2304]{1,0:T(8,128)(2,1)S(1)}, u32[]{:S(2)}, u32[]{:S(2)}) collective-permute-start(bf16[96,2304]{1,0:T(8,128)(2,1)S(1)} %pad_maximum_fusion.7.refs_0_), channel_id=1, source_target_pairs={{0,8},{4,12},{8,0},{12,4},{16,24},{20,28},{24,16},{28,20},{1,9},{5... | collective-permute-start | bytes 1327112 | tf_op jit(solution)/shard_map/ppermute | solution.py:592
  243.0 17.7 %collective-permute-start.30 = (bf16[96,2304]{1,0:T(8,128)(2,1)S(1)}, bf16[96,2304]{1,0:T(8,128)(2,1)S(1)}, u32[]{:S(2)}, u32[]{:S(2)}) collective-permute-start(bf16[96,2304]{1,0:T(8,128)(2,1)S(1)} %chunk_step.59), channel_id=1, source_target_pairs={{0,8},{4,12},{8,0},{12,4},{16,24},{20,28},{24,16},{28,20},{1,9},{5... | collective-permute-start | bytes 1327112 | tf_op jit(solution)/shard_map/ppermute | solution.py:592
  252.4 17.8 %collective-permute-start.28 = (bf16[96,2304]{1,0:T(8,128)(2,1)S(1)}, bf16[96,2304]{1,0:T(8,128)(2,1)S(1)}, u32[]{:S(2)}, u32[]{:S(2)}) collective-permute-start(bf16[96,2304]{1,0:T(8,128)(2,1)S(1)} %chunk_step.62), channel_id=1, source_target_pairs={{0,8},{4,12},{8,0},{12,4},{16,24},{20,28},{24,16},{28,20},{1,9},{5... | collective-permute-start | bytes 1327112 | tf_op jit(solution)/shard_map/ppermute | solution.py:592
  271.3 16.2 %collective-permute-start.38 = (bf16[96,2304]{1,0:T(8,128)(2,1)S(1)}, bf16[96,2304]{1,0:T(8,128)(2,1)S(1)}, u32[]{:S(2)}, u32[]{:S(2)}) collective-permute-start(bf16[96,2304]{1,0:T(8,128)(2,1)S(1)} %get-tuple-element.980.refs_1_), channel_id=1, source_target_pairs={{0,4},{4,0},{8,12},{12,8},{16,20},{20,16},{24,28},{28,24},{1,5},{5... | collective-permute-start | bytes 1327112 | tf_op jit(solution)/shard_map/ppermute | solution.py:596
  282.4 17.8 %collective-permute-start.42 = (bf16[96,2304]{1,0:T(8,128)(2,1)S(1)}, bf16[96,2304]{1,0:T(8,128)(2,1)S(1)}, u32[]{:S(2)}, u32[]{:S(2)}) collective-permute-start(bf16[96,2304]{1,0:T(8,128)(2,1)S(1)} %chunk_step.71), channel_id=1, source_target_pairs={{0,8},{4,12},{8,0},{12,4},{16,24},{20,28},{24,16},{28,20},{1,9},{5... | collective-permute-start | bytes 1327112 | tf_op jit(solution)/shard_map/ppermute | solution.py:592
  290.0 17.8 %collective-permute-start.40 = (bf16[96,2304]{1,0:T(8,128)(2,1)S(1)}, bf16[96,2304]{1,0:T(8,128)(2,1)S(1)}, u32[]{:S(2)}, u32[]{:S(2)}) collective-permute-start(bf16[96,2304]{1,0:T(8,128)(2,1)S(1)} %get-tuple-element.1048.refs_0_), channel_id=1, source_target_pairs={{0,4},{4,0},{8,12},{12,8},{16,20},{20,16},{24,28},{28,24},{1,5},{5... | collective-permute-start | bytes 1327112 | tf_op jit(solution)/shard_map/ppermute | solution.py:596
  291.8 16.3 %collective-permute-start.39 = (bf16[96,2304]{1,0:T(8,128)(2,1)S(1)}, bf16[96,2304]{1,0:T(8,128)(2,1)S(1)}, u32[]{:S(2)}, u32[]{:S(2)}) collective-permute-start(bf16[96,2304]{1,0:T(8,128)(2,1)S(1)} %chunk_step.74), channel_id=1, source_target_pairs={{0,8},{4,12},{8,0},{12,4},{16,24},{20,28},{24,16},{28,20},{1,9},{5... | collective-permute-start | bytes 1327112 | tf_op jit(solution)/shard_map/ppermute | solution.py:592
  301.2 16.9 %collective-permute-start.46 = (bf16[96,2304]{1,0:T(8,128)(2,1)S(1)}, bf16[96,2304]{1,0:T(8,128)(2,1)S(1)}, u32[]{:S(2)}, u32[]{:S(2)}) collective-permute-start(bf16[96,2304]{1,0:T(8,128)(2,1)S(1)} %get-tuple-element.1049.refs_1_), channel_id=1, source_target_pairs={{0,4},{4,0},{8,12},{12,8},{16,20},{20,16},{24,28},{28,24},{1,5},{5... | collective-permute-start | bytes 1327112 | tf_op jit(solution)/shard_map/ppermute | solution.py:596
  301.7 17.1 %collective-permute-start.45 = (bf16[96,2304]{1,0:T(8,128)(2,1)S(1)}, bf16[96,2304]{1,0:T(8,128)(2,1)S(1)}, u32[]{:S(2)}, u32[]{:S(2)}) collective-permute-start(bf16[96,2304]{1,0:T(8,128)(2,1)S(1)} %chunk_step.77), channel_id=1, source_target_pairs={{0,8},{4,12},{8,0},{12,4},{16,24},{20,28},{24,16},{28,20},{1,9},{5... | collective-permute-start | bytes 1327112 | tf_op jit(solution)/shard_map/ppermute | solution.py:592
  311.2 22.1 %collective-permute-start.49 = (bf16[96,2304]{1,0:T(8,128)(2,1)S(1)}, bf16[96,2304]{1,0:T(8,128)(2,1)S(1)}, u32[]{:S(2)}, u32[]{:S(2)}) collective-permute-start(bf16[96,2304]{1,0:T(8,128)(2,1)S(1)} %chunk_step.80), channel_id=1, source_target_pairs={{0,8},{4,12},{8,0},{12,4},{16,24},{20,28},{24,16},{28,20},{1,9},{5... | collective-permute-start | bytes 1327112 | tf_op jit(solution)/shard_map/ppermute | solution.py:592
  319.8 17.0 %collective-permute-start.55 = (bf16[96,2304]{1,0:T(8,128)(2,1)S(1)}, bf16[96,2304]{1,0:T(8,128)(2,1)S(1)}, u32[]{:S(2)}, u32[]{:S(2)}) collective-permute-start(bf16[96,2304]{1,0:T(8,128)(2,1)S(1)} %get-tuple-element.1119.refs_0_), channel_id=1, source_target_pairs={{0,4},{4,0},{8,12},{12,8},{16,20},{20,16},{24,28},{28,24},{1,5},{5... | collective-permute-start | bytes 1327112 | tf_op jit(solution)/shard_map/ppermute | solution.py:596
  322.0 17.7 %collective-permute-start.54 = (bf16[96,2304]{1,0:T(8,128)(2,1)S(1)}, bf16[96,2304]{1,0:T(8,128)(2,1)S(1)}, u32[]{:S(2)}, u32[]{:S(2)}) collective-permute-start(bf16[96,2304]{1,0:T(8,128)(2,1)S(1)} %chunk_step.83), channel_id=1, source_target_pairs={{0,8},{4,12},{8,0},{12,4},{16,24},{20,28},{24,16},{28,20},{1,9},{5... | collective-permute-start | bytes 1327112 | tf_op jit(solution)/shard_map/ppermute | solution.py:592
  376.4 16.5 %collective-permute-start.68 = (bf16[96,2304]{1,0:T(8,128)(2,1)S(1)}, bf16[96,2304]{1,0:T(8,128)(2,1)S(1)}, u32[]{:S(2)}, u32[]{:S(2)}) collective-permute-start(bf16[96,2304]{1,0:T(8,128)(2,1)S(1)} %chunk_step.98), channel_id=1, source_target_pairs={{0,8},{4,12},{8,0},{12,4},{16,24},{20,28},{24,16},{28,20},{1,9},{5... | collective-permute-start | bytes 1327112 | tf_op jit(solution)/shard_map/ppermute | solution.py:592
  379.0 22.4 %collective-permute-start.71 = (bf16[96,2304]{1,0:T(8,128)(2,1)S(1)}, bf16[96,2304]{1,0:T(8,128)(2,1)S(1)}, u32[]{:S(2)}, u32[]{:S(2)}) collective-permute-start(bf16[96,2304]{1,0:T(8,128)(2,1)S(1)} %chunk_step.97.refs_1_), channel_id=1, source_target_pairs={{0,8},{4,12},{8,0},{12,4},{16,24},{20,28},{24,16},{28,20},{1,9},{5... | collective-permute-start | bytes 1327112 | tf_op jit(solution)/shard_map/ppermute | solution.py:592
  381.0 20.5 %collective-permute-start.72 = (bf16[96,2304]{1,0:T(8,128)(2,1)S(1)}, bf16[96,2304]{1,0:T(8,128)(2,1)S(1)}, u32[]{:S(2)}, u32[]{:S(2)}) collective-permute-start(bf16[96,2304]{1,0:T(8,128)(2,1)S(1)} %get-tuple-element.1246.refs_0_), channel_id=1, source_target_pairs={{0,4},{4,0},{8,12},{12,8},{16,20},{20,16},{24,28},{28,24},{1,5},{5... | collective-permute-start | bytes 1327112 | tf_op jit(solution)/shard_map/ppermute | solution.py:596
  394.8 17.3 %collective-permute-start.67 = (bf16[96,2304]{1,0:T(8,128)(2,1)S(1)}, bf16[96,2304]{1,0:T(8,128)(2,1)S(1)}, u32[]{:S(2)}, u32[]{:S(2)}) collective-permute-start(bf16[96,2304]{1,0:T(8,128)(2,1)S(1)} %chunk_step.100.refs_1_), channel_id=1, source_target_pairs={{0,8},{4,12},{8,0},{12,4},{16,24},{20,28},{24,16},{28,20},{1,9},{5... | collective-permute-start | bytes 1327112 | tf_op jit(solution)/shard_map/ppermute | solution.py:592
  402.7 24.5 %collective-permute-start.74 = (bf16[96,2304]{1,0:T(8,128)(2,1)S(1)}, bf16[96,2304]{1,0:T(8,128)(2,1)S(1)}, u32[]{:S(2)}, u32[]{:S(2)}) collective-permute-start(bf16[96,2304]{1,0:T(8,128)(2,1)S(1)} %chunk_step.102.refs_1_), channel_id=1, source_target_pairs={{0,8},{4,12},{8,0},{12,4},{16,24},{20,28},{24,16},{28,20},{1,9},{5... | collective-permute-start | bytes 1327112 | tf_op jit(solution)/shard_map/ppermute | solution.py:592
  412.1 16.6 %collective-permute-start.78 = (bf16[96,2304]{1,0:T(8,128)(2,1)S(1)}, bf16[96,2304]{1,0:T(8,128)(2,1)S(1)}, u32[]{:S(2)}, u32[]{:S(2)}) collective-permute-start(bf16[96,2304]{1,0:T(8,128)(2,1)S(1)} %chunk_step.105.refs_0_), channel_id=1, source_target_pairs={{0,4},{4,0},{8,12},{12,8},{16,20},{20,16},{24,28},{28,24},{1,5},{5... | collective-permute-start | bytes 1327112 | tf_op jit(solution)/shard_map/ppermute | solution.py:596
  (144 other events, 1473.5 us)

commit v4 on v3

--- a/solution.py
+++ b/solution.py
@@ -10,7 +10,7 @@
 LANES = 128
 ROWS = 16
 CHUNKS = 18
-PART = 96
+PART = 144
 LAG = 4
 HIDDEN_COST = pl.CostEstimate(flops=1, bytes_accessed=1, transcendentals=0)
 
@@ -632,18 +632,18 @@
         return hidden, sums, gg.reshape(rows, span)
 
     if line == 4 and channel_parts == 4:
-        done = Order(small_mine)
+        done = Order(out_grad)
 
         def run(function, *operands):
             return done(function(*done(operands)))
 
         pick_near = jnp.stack([side, place // 2, place % 2]).astype(jnp.int32)
         pick_far = jnp.stack([side, 1 - place // 2, place % 2]).astype(jnp.int32)
-        small_pair = lax.ppermute(small_other, "dp", pairs)
         x_own = run(lambda x: mix(x.T, slots), inputs)
         far_got = lax.ppermute(x_own, "mp", chip_pairs)
         pair_got = lax.ppermute(x_own, "dp", pairs)
         near_got = lax.ppermute(x_own, "mp", core_pairs)
+        out_grad, done.token = done.token, small_mine
         grads = run(lambda g: mix(g.T, slots), out_grad)
         grads_mine, grads_other = done((half(grads, 0, side), half(grads, 0, other_side)))
         gates, near, w_near = run(
@@ -652,10 +652,10 @@
         cut = width * 2 // 3
         far_own = done(far_got)
         far_got = lax.ppermute(far_own, "mp", core_pairs)
-        x_pair, small_pair = done((pair_got, small_pair))
+        x_pair = done(pair_got)
         relay = [
             lax.ppermute(x_pair[:cut], "mp", chip_pairs),
-            lax.ppermute(far_own[cut:], "dp", pairs),
+            lax.ppermute(jnp.concatenate([far_own[cut:], grads_other], axis=0), "dp", pairs),
         ]
         far_got = done(far_got)
         pair_near_got = lax.ppermute(done(x_pair), "mp", core_pairs)
@@ -665,9 +665,11 @@
         )
         done.token = sums_mine
         gg_mine = done(gg_mine.reshape(rows, span))
-        pair_far_own = run(lambda a, b: jnp.concatenate([a, b], axis=0), *relay)
+        pair_far_own, grads_pair = run(
+            lambda a, b: (jnp.concatenate([a, b[: width - cut]], axis=0), b[width - cut :]), *relay
+        )
         pair_far_got = lax.ppermute(pair_far_own, "mp", core_pairs)
-        grads_pair = lax.ppermute(done(grads_other), "dp", pairs)
+        small_pair = lax.ppermute(done(small_other), "dp", pairs)
         kept = {}
 
         own_shape, wide_type, sent_type = (width, span), jnp.float32, jnp.bfloat16
@@ -830,6 +832,9 @@
             return run_all
 
         fill_bias(0)()
+        fill_bias(0)()
+        fill_bias(0)()
+        fill_bias(0)()
         send("hidden", hidden_pair)
         fill_back(1, 1)
         fill_back(1, 0)
@@ -838,16 +843,15 @@
         fill_bias(1)()
         fill_back(0, 1)
         fill_core(1, 0)
+        fill_back(0, 0)
         fill_bias(2)()
-        fill_back(0, 0)
         fill_core(0, 1)
-        fill_bias(3)()
         products()
         fill_core(0, 0)
         receive("hidden")
-        fill_bias(4)()
+        fill_bias(3)()
         fillers = {
-            0: fill((receive, ("cross", 1)), (fill_cross, 0)),
+            0: fill((receive, ("cross", 1)), (fill_cross, 0), (fill_bias(4),)),
             1: fill((fill_send,)),
             3: fill((receive, ("cross", 0))),
             4: fill((receive, "pair")),

time: 457 us -> 447 us (0.978)
  starting transfers between devices: 154 us -> 146 us
    ppermute x3 -> x2, waiting for transfers between devices: 8.09 us -> 2.29 us  [the longest x1 2.29 us: on_device(): lax.ppermute(jnp.concatenate([far_own[cut:], grads_other], axis=0), 'dp',...]
    ppermute x21, waiting for transfers between devices: 23.1 us -> 27.9 us  [piped_sums(): got_edge[n + 1] = lax.ppermute(payload, 'dp', edge)]
    unnamed x191 -> x199, local copies, waits for them, and re-layouts: 27 us -> 28.1 us
  transfers between devices with their start and end apart: 81 -> 80, of which waited for: 22 -> 26; matrix products, arithmetic and copies ran while one was open for 12% -> 13% of each run, Pallas kernels for 23% -> 23%
where the time goes in v4:
time: 447 us; the launch traced here: 439 us
  starting transfers between devices  146 us (33%)
  Pallas kernels  130 us (29%)
  waiting for transfers between devices  68.1 us (15%)
  matrix products  41 us (9%)
  local copies, waits for them, and re-layouts  38.9 us (9%)
  other arithmetic  11.2 us (3%)
    ppermute x21, starting transfers between devices, piped_sums(): got_edge[n + 1] = lax.ppermute(payload, 'dp', edge)  84.5 us
    pallas_call x2, Pallas kernels, gates_pool(): pl.pallas_call(gates_pool_kernel, grid_spec=pltpu.PrefetchScalarGridSpec(...  37.6 us
    dot_general x4, matrix products, cols_dot(): lax.dot_general(left, right, (((1,), (1,)), ((), ())), preferred_element_...  33.1 us
    pallas_call x4, Pallas kernels, back_products(): pl.pallas_call(back_kernel, grid_spec=pltpu.PrefetchScalarGridSpec(num_sc...  30.6 us
    unnamed x199, local copies, waits for them, and re-layouts  28.1 us
    ppermute x21, waiting for transfers between devices, piped_sums(): got_edge[n + 1] = lax.ppermute(payload, 'dp', edge)  27.9 us
    ppermute x18, starting transfers between devices, piped_sums(): got_pair[k] = lax.ppermute(final, 'dp', pairs)  22.6 us
    pallas_call x6, Pallas kernels, write_chunks(): pl.pallas_call(functools.partial(write_kernel, count), grid=(2,), in_spec...  20.5 us
  transfers between devices with their start and end apart: 80, of which 26 were waited for; matrix products, arithmetic and copies ran while one was open for 13% of the time, Pallas kernels for 23%

profile of v4, /device:TPU:0, one launch (start us, length us, event | category | flops | bytes accessed | tf_op | source)
XLA Modules:
  0.0 439.1 jit_solution(4006127972838461493)
XLA Ops:
  17.1 9.6 %gates_step.2 = (f32[2,3,288,1152]{3,2,1,0:T(8,128)S(1)}, bf16[1152,1152]{1,0:T(8,128)(2,1)S(1)}, bf16[2,3,288,1152]{3,2,1,0:T(8,128)(2,1)S(1)}) custom-call(s32[3]{0:T(128)S(1)} %add_add_fusion.1.pick_ref, bf16[576,1152]{1,0:T(8,128)(2,1)} %convolution_convert_fusion.1.low_ref, bf16[576,1152]{1,0:T(8,128)(2,1)} %collective-permute-done.1.high_ref, ...), custom_call_target="tpu_custom_call" | custom-call | flops 1 | bytes 1 | tf_op jit(solution)/shard_map/gates_step/pallas_call | solution.py:248
  31.8 7.0 %collective-permute-done.low_ref = bf16[576,1152]{1,0:T(8,128)(2,1)S(1)} collective-permute-done((bf16[576,1152]{1,0:T(8,128)(2,1)}, bf16[576,1152]{1,0:T(8,128)(2,1)S(1)}, u32[]{:S(2)}, u32[]{:S(2)}) %collective-permute-start) | collective-permute-done | bytes 1327136 | tf_op jit(solution)/shard_map/ppermute | solution.py:643
  44.2 19.4 %gates_pool.2 = (bf16[288,1152]{1,0:T(8,128)(2,1)S(1)}, f32[288,128]{1,0:T(8,128)S(1)}, bf16[2,3,288,1152]{3,2,1,0:T(8,128)(2,1)S(1)}, bf16[1152,1152]{1,0:T(8,128)(2,1)S(1)}, bf16[2,3,288,1152]{3,2,1,0:T(8,128)(2,1)}) custom-call(s32[3]{0:T(128)S(1)} %add_add_fusion.pick_ref, s32[1]{0:T(128)S(6)} %copy.33.length_ref, ...), custom_call_target="tpu_custom_call" | custom-call | flops 1 | bytes 1 | tf_op jit(solution)/shard_map/gates_pool/pallas_call | solution.py:311
  72.9 8.3 %gates_step.3 = (f32[2,3,288,1152]{3,2,1,0:T(8,128)S(1)}, bf16[1152,1152]{1,0:T(8,128)(2,1)S(1)}) custom-call(s32[3]{0:T(128)S(1)} %add_add_fusion.1.pick_ref, bf16[576,1152]{1,0:T(8,128)(2,1)S(1)} %collective-permute-done.3.low_ref, bf16[576,1152]{1,0:T(8,128)(2,1)S(1)} %collective-permute-done.7.high_ref, bf16[2,3,576,2304]{3,2,1,0:T(8,128)(2,1)} %bitcast.45), custom_call_target="tpu_custom_call" | custom-call | flops 1 | bytes 1 | tf_op jit(solution)/shard_map/gates_step/pallas_call | solution.py:248
  87.3 18.1 %gates_pool.3 = (bf16[288,1152]{1,0:T(8,128)(2,1)S(1)}, f32[288,128]{1,0:T(8,128)S(1)}, bf16[2,3,288,1152]{3,2,1,0:T(8,128)(2,1)S(1)}, bf16[1152,1152]{1,0:T(8,128)(2,1)S(1)}) custom-call(s32[3]{0:T(128)S(1)} %add_add_fusion.pick_ref, s32[1]{0:T(128)} %bitcast.8.length_ref, bf16[576,1152]{1,0:T(8,128)(2,1)S(1)} %pad_maximum_fusion.low_ref, ...), custom_call_target="tpu_custom_call" | custom-call | flops 1 | bytes 1 | tf_op jit(solution)/shard_map/gates_pool/pallas_call | solution.py:311
  105.6 7.3 %back_products.4 = (f32[576,1152]{1,0:T(8,128)S(1)}, bf16[576,1152]{1,0:T(8,128)(2,1)S(1)}) custom-call(s32[3]{0:T(128)S(1)} %add_add_fusion.1.pick_ref, bf16[1728,1152]{1,0:T(8,128)(2,1)S(1)} %bitcast.40, bf16[1728,1152]{1,0:T(8,128)(2,1)S(1)} %bitcast.36), custom_call_target="tpu_custom_call" | custom-call | flops 1 | bytes 1 | tf_op jit(solution)/shard_map/back_products/pallas_call | solution.py:381
  114.6 7.3 %back_products.5 = (f32[576,1152]{1,0:T(8,128)S(1)}, bf16[576,1152]{1,0:T(8,128)(2,1)S(1)}) custom-call(s32[3]{0:T(128)S(1)} %add_add_fusion.1.pick_ref, bf16[1728,1152]{1,0:T(8,128)(2,1)S(1)} %bitcast.30, bf16[1728,1152]{1,0:T(8,128)(2,1)S(1)} %bitcast.37), custom_call_target="tpu_custom_call" | custom-call | flops 1 | bytes 1 | tf_op jit(solution)/shard_map/back_products/pallas_call | solution.py:381
  124.5 8.4 %back_products.6 = (f32[576,1152]{1,0:T(8,128)S(1)}, bf16[576,1152]{1,0:T(8,128)(2,1)}) custom-call(s32[3]{0:T(128)S(1)} %add_add_fusion.1.pick_ref, bf16[1728,1152]{1,0:T(8,128)(2,1)S(1)} %bitcast.41, bf16[1728,1152]{1,0:T(8,128)(2,1)S(1)} %bitcast.32), custom_call_target="tpu_custom_call" | custom-call | flops 1 | bytes 1 | tf_op jit(solution)/shard_map/back_products/pallas_call | solution.py:381
  143.5 7.5 %back_products.7 = (f32[576,1152]{1,0:T(8,128)S(1)}, bf16[576,1152]{1,0:T(8,128)(2,1)S(1)}) custom-call(s32[3]{0:T(128)S(1)} %add_add_fusion.1.pick_ref, bf16[1728,1152]{1,0:T(8,128)(2,1)S(1)} %bitcast.31, bf16[1728,1152]{1,0:T(8,128)(2,1)S(1)} %bitcast.33), custom_call_target="tpu_custom_call" | custom-call | flops 1 | bytes 1 | tf_op jit(solution)/shard_map/back_products/pallas_call | solution.py:381
  160.3 8.0 %fusion.13 = f32[1728,1152]{1,0:T(8,128)} fusion(bf16[1728,1152]{1,0:T(8,128)(2,1)S(1)} %bitcast.34, bf16[1152,1152]{1,0:T(8,128)(2,1)S(1)} %copy-done.44), kind=kOutput, calls=%fused_computation.62 | convolution fusion | flops 4586471424 | bytes 14598144 | tf_op jit(solution)/shard_map/dot_general | solution.py:204
  168.3 8.5 %fusion = bf16[1728,1152]{1,0:T(8,128)(2,1)S(1)} fusion(f32[1728,1152]{1,0:T(8,128)} %fusion.13, bf16[1728,1152]{1,0:T(8,128)(2,1)S(1)} %bitcast.38, bf16[1152,1152]{1,0:T(8,128)(2,1)S(1)} %copy-done.48), kind=kOutput, calls=%fused_computation.2 | convolution fusion | flops 4590452736 | bytes 18579456 | tf_op jit(solution)/shard_map/dot_general | solution.py:204
  176.8 8.0 %fusion.14 = f32[1728,1152]{1,0:T(8,128)} fusion(bf16[1728,1152]{1,0:T(8,128)(2,1)S(1)} %bitcast.35, bf16[1152,1152]{1,0:T(8,128)(2,1)S(1)} %copy-done.46), kind=kOutput, calls=%fused_computation.63 | convolution fusion | flops 4586471424 | bytes 14598144 | tf_op jit(solution)/shard_map/dot_general | solution.py:204
  184.9 8.5 %fusion.1 = bf16[1728,1152]{1,0:T(8,128)(2,1)S(1)} fusion(f32[1728,1152]{1,0:T(8,128)} %fusion.14, bf16[1728,1152]{1,0:T(8,128)(2,1)S(1)} %bitcast.39, bf16[1152,1152]{1,0:T(8,128)(2,1)S(1)} %copy-done.50), kind=kOutput, calls=%fused_computation.3 | convolution fusion | flops 4590452736 | bytes 18579456 | tf_op jit(solution)/shard_map/dot_general | solution.py:204
  207.1 5.7 %collective-permute-done.19.refs_1_ = bf16[96,2304]{1,0:T(8,128)(2,1)} collective-permute-done((bf16[96,2304]{1,0:T(8,128)(2,1)S(1)}, bf16[96,2304]{1,0:T(8,128)(2,1)}, u32[]{:S(2)}, u32[]{:S(2)}) %collective-permute-start.19) | collective-permute-done | bytes 442400 | tf_op jit(solution)/shard_map/ppermute | solution.py:565
  217.3 4.9 %collective-permute-done.17.refs_1_ = bf16[96,2304]{1,0:T(8,128)(2,1)S(1)} collective-permute-done((bf16[96,2304]{1,0:T(8,128)(2,1)S(1)}, bf16[96,2304]{1,0:T(8,128)(2,1)S(1)}, u32[]{:S(2)}, u32[]{:S(2)}) %collective-permute-start.17) | collective-permute-done | bytes 442400 | tf_op jit(solution)/shard_map/ppermute | solution.py:592
  223.2 6.4 %collective-permute-start.25 = (bf16[96,2304]{1,0:T(8,128)(2,1)S(1)}, bf16[96,2304]{1,0:T(8,128)(2,1)S(1)}, u32[]{:S(2)}, u32[]{:S(2)}) collective-permute-start(bf16[96,2304]{1,0:T(8,128)(2,1)S(1)} %pad_maximum_fusion.8.refs_0_), channel_id=1, source_target_pairs={{0,8},{4,12},{8,0},{12,4},{16,24},{20,28},{24,16},{28,20},{1,9},{5... | collective-permute-start | bytes 1327112 | tf_op jit(solution)/shard_map/ppermute | solution.py:592
  232.9 6.1 %collective-permute-start.29 = (bf16[96,2304]{1,0:T(8,128)(2,1)S(1)}, bf16[96,2304]{1,0:T(8,128)(2,1)S(1)}, u32[]{:S(2)}, u32[]{:S(2)}) collective-permute-start(bf16[96,2304]{1,0:T(8,128)(2,1)S(1)} %chunk_step.59), channel_id=1, source_target_pairs={{0,8},{4,12},{8,0},{12,4},{16,24},{20,28},{24,16},{28,20},{1,9},{5... | collective-permute-start | bytes 1327112 | tf_op jit(solution)/shard_map/ppermute | solution.py:592
  242.3 6.1 %collective-permute-start.27 = (bf16[96,2304]{1,0:T(8,128)(2,1)S(1)}, bf16[96,2304]{1,0:T(8,128)(2,1)S(1)}, u32[]{:S(2)}, u32[]{:S(2)}) collective-permute-start(bf16[96,2304]{1,0:T(8,128)(2,1)S(1)} %chunk_step.62), channel_id=1, source_target_pairs={{0,8},{4,12},{8,0},{12,4},{16,24},{20,28},{24,16},{28,20},{1,9},{5... | collective-permute-start | bytes 1327112 | tf_op jit(solution)/shard_map/ppermute | solution.py:592
  252.9 5.3 %collective-permute-start.32 = (bf16[96,2304]{1,0:T(8,128)(2,1)S(1)}, bf16[96,2304]{1,0:T(8,128)(2,1)S(1)}, u32[]{:S(2)}, u32[]{:S(2)}) collective-permute-start(bf16[96,2304]{1,0:T(8,128)(2,1)S(1)} %chunk_step.65), channel_id=1, source_target_pairs={{0,8},{4,12},{8,0},{12,4},{16,24},{20,28},{24,16},{28,20},{1,9},{5... | collective-permute-start | bytes 1327112 | tf_op jit(solution)/shard_map/ppermute | solution.py:592
  262.4 5.3 %collective-permute-start.36 = (bf16[96,2304]{1,0:T(8,128)(2,1)S(1)}, bf16[96,2304]{1,0:T(8,128)(2,1)S(1)}, u32[]{:S(2)}, u32[]{:S(2)}) collective-permute-start(bf16[96,2304]{1,0:T(8,128)(2,1)S(1)} %chunk_step.68), channel_id=1, source_target_pairs={{0,8},{4,12},{8,0},{12,4},{16,24},{20,28},{24,16},{28,20},{1,9},{5... | collective-permute-start | bytes 1327112 | tf_op jit(solution)/shard_map/ppermute | solution.py:592
  271.7 6.6 %collective-permute-start.41 = (bf16[96,2304]{1,0:T(8,128)(2,1)S(1)}, bf16[96,2304]{1,0:T(8,128)(2,1)S(1)}, u32[]{:S(2)}, u32[]{:S(2)}) collective-permute-start(bf16[96,2304]{1,0:T(8,128)(2,1)S(1)} %chunk_step.71), channel_id=1, source_target_pairs={{0,8},{4,12},{8,0},{12,4},{16,24},{20,28},{24,16},{28,20},{1,9},{5... | collective-permute-start | bytes 1327112 | tf_op jit(solution)/shard_map/ppermute | solution.py:592
  281.1 5.5 %collective-permute-start.38 = (bf16[96,2304]{1,0:T(8,128)(2,1)S(1)}, bf16[96,2304]{1,0:T(8,128)(2,1)S(1)}, u32[]{:S(2)}, u32[]{:S(2)}) collective-permute-start(bf16[96,2304]{1,0:T(8,128)(2,1)S(1)} %chunk_step.74), channel_id=1, source_target_pairs={{0,8},{4,12},{8,0},{12,4},{16,24},{20,28},{24,16},{28,20},{1,9},{5... | collective-permute-start | bytes 1327112 | tf_op jit(solution)/shard_map/ppermute | solution.py:592
  292.4 4.6 %collective-permute-start.44 = (bf16[96,2304]{1,0:T(8,128)(2,1)S(1)}, bf16[96,2304]{1,0:T(8,128)(2,1)S(1)}, u32[]{:S(2)}, u32[]{:S(2)}) collective-permute-start(bf16[96,2304]{1,0:T(8,128)(2,1)S(1)} %chunk_step.77), channel_id=1, source_target_pairs={{0,8},{4,12},{8,0},{12,4},{16,24},{20,28},{24,16},{28,20},{1,9},{5... | collective-permute-start | bytes 1327112 | tf_op jit(solution)/shard_map/ppermute | solution.py:592
  301.0 6.3 %collective-permute-start.48 = (bf16[96,2304]{1,0:T(8,128)(2,1)S(1)}, bf16[96,2304]{1,0:T(8,128)(2,1)S(1)}, u32[]{:S(2)}, u32[]{:S(2)}) collective-permute-start(bf16[96,2304]{1,0:T(8,128)(2,1)S(1)} %chunk_step.80), channel_id=1, source_target_pairs={{0,8},{4,12},{8,0},{12,4},{16,24},{20,28},{24,16},{28,20},{1,9},{5... | collective-permute-start | bytes 1327112 | tf_op jit(solution)/shard_map/ppermute | solution.py:592
  310.8 7.1 %collective-permute-start.53 = (bf16[96,2304]{1,0:T(8,128)(2,1)S(1)}, bf16[96,2304]{1,0:T(8,128)(2,1)S(1)}, u32[]{:S(2)}, u32[]{:S(2)}) collective-permute-start(bf16[96,2304]{1,0:T(8,128)(2,1)S(1)} %chunk_step.83), channel_id=1, source_target_pairs={{0,8},{4,12},{8,0},{12,4},{16,24},{20,28},{24,16},{28,20},{1,9},{5... | collective-permute-start | bytes 1327112 | tf_op jit(solution)/shard_map/ppermute | solution.py:592
  330.2 4.8 %collective-permute-done.51.refs_4_ = bf16[96,2304]{1,0:T(8,128)(2,1)S(1)} collective-permute-done((bf16[96,2304]{1,0:T(8,128)(2,1)S(1)}, bf16[96,2304]{1,0:T(8,128)(2,1)S(1)}, u32[]{:S(2)}, u32[]{:S(2)}) %collective-permute-start.51) | collective-permute-done | bytes 442400 | tf_op jit(solution)/shard_map/ppermute | solution.py:596
  341.1 5.1 %collective-permute-start.58 = (bf16[96,2304]{1,0:T(8,128)(2,1)S(1)}, bf16[96,2304]{1,0:T(8,128)(2,1)S(1)}, u32[]{:S(2)}, u32[]{:S(2)}) collective-permute-start(bf16[96,2304]{1,0:T(8,128)(2,1)S(1)} %chunk_step.92), channel_id=1, source_target_pairs={{0,8},{4,12},{8,0},{12,4},{16,24},{20,28},{24,16},{28,20},{1,9},{5... | collective-permute-start | bytes 1327112 | tf_op jit(solution)/shard_map/ppermute | solution.py:592
  373.3 4.2 write_chunks.9.refs_6_
  384.1 5.9 %collective-permute-start.66 = (bf16[96,2304]{1,0:T(8,128)(2,1)S(1)}, bf16[96,2304]{1,0:T(8,128)(2,1)S(1)}, u32[]{:S(2)}, u32[]{:S(2)}) collective-permute-start(bf16[96,2304]{1,0:T(8,128)(2,1)S(1)} %chunk_step.100.refs_1_), channel_id=1, source_target_pairs={{0,8},{4,12},{8,0},{12,4},{16,24},{20,28},{24,16},{28,20},{1,9},{5... | collective-permute-start | bytes 1327112 | tf_op jit(solution)/shard_map/ppermute | solution.py:592
  395.8 5.4 %collective-permute-done.66.refs_0_ = bf16[96,2304]{1,0:T(8,128)(2,1)S(1)} collective-permute-done((bf16[96,2304]{1,0:T(8,128)(2,1)S(1)}, bf16[96,2304]{1,0:T(8,128)(2,1)S(1)}, u32[]{:S(2)}, u32[]{:S(2)}) %collective-permute-start.66) | collective-permute-done | bytes 442400 | tf_op jit(solution)/shard_map/ppermute | solution.py:592
  412.1 4.5 %whole.13 = bf16[576,1152]{1,0:T(8,128)(2,1)} custom-call(f32[576,1152]{1,0:T(8,128)S(1)} %copy-done.12, bf16[576,1152]{1,0:T(8,128)(2,1)} %collective-permute-done.26.refs_1_, bf16[576,1152]{1,0:T(8,128)(2,1)S(1)} %copy-done.22, bf16[1152,1152]{1,0:T(8,128)(2,1)S(1)} %fusion.10.refs_2_.refs_3_), custom_call_target="tpu_custom_call" | custom-call | flops 1 | bytes 1 | tf_op jit(solution)/shard_map/whole/pallas_call | solution.py:352
  419.8 5.6 %collective-permute-done.78.refs_4_ = bf16[96,2304]{1,0:T(8,128)(2,1)S(1)} collective-permute-done((bf16[96,2304]{1,0:T(8,128)(2,1)S(1)}, bf16[96,2304]{1,0:T(8,128)(2,1)S(1)}, u32[]{:S(2)}, u32[]{:S(2)}) %collective-permute-start.78) | collective-permute-done | bytes 442400 | tf_op jit(solution)/shard_map/ppermute | solution.py:596
  (461 shorter events, 203.7 us)
Async XLA Ops:
  6.3 32.5 %collective-permute-start = (bf16[576,1152]{1,0:T(8,128)(2,1)}, bf16[576,1152]{1,0:T(8,128)(2,1)S(1)}, u32[]{:S(2)}, u32[]{:S(2)}) collective-permute-start(bf16[576,1152]{1,0:T(8,128)(2,1)} %convolution_convert_fusion.1.low_ref), channel_id=1, source_target_pairs={{0,2},{1,3},{2,0},{3,1},{4,6},{5,7},{6,4},{7,5},{8,10},{9,11},{10,... | collective-permute-start | bytes 3981320 | tf_op jit(solution)/shard_map/ppermute | solution.py:643
  8.8 32.9 %collective-permute-start.3 = (bf16[576,1152]{1,0:T(8,128)(2,1)}, bf16[576,1152]{1,0:T(8,128)(2,1)S(1)}, u32[]{:S(2)}, u32[]{:S(2)}) collective-permute-start(bf16[576,1152]{1,0:T(8,128)(2,1)} %convolution_convert_fusion.1.low_ref), channel_id=1, source_target_pairs={{0,4},{4,0},{8,12},{12,8},{16,20},{20,16},{24,28},{28,24},{1,5},{5... | collective-permute-start | bytes 3981320 | tf_op jit(solution)/shard_map/ppermute | solution.py:644
  39.9 27.1 %collective-permute-start.5 = (bf16[480,1152]{1,0:T(8,128)(2,1)}, bf16[480,1152]{1,0:T(8,128)(2,1)}, u32[]{:S(2)}, u32[]{:S(2)}) collective-permute-start(bf16[480,1152]{1,0:T(8,128)(2,1)} %pad_maximum_fusion.1), channel_id=1, source_target_pairs={{0,4},{4,0},{8,12},{12,8},{16,20},{20,16},{24,28},{28,24},{1,5},{5... | collective-permute-start | bytes 3317768 | tf_op jit(solution)/shard_map/ppermute | solution.py:658
  42.7 22.1 %collective-permute-start.4 = (bf16[384,1152]{1,0:T(8,128)(2,1)}, bf16[384,1152]{1,0:T(8,128)(2,1)}, u32[]{:S(2)}, u32[]{:S(2)}) collective-permute-start(bf16[384,1152]{1,0:T(8,128)(2,1)} %slice.135), channel_id=1, source_target_pairs={{0,2},{1,3},{2,0},{3,1},{4,6},{5,7},{6,4},{7,5},{8,10},{9,11},{10,... | collective-permute-start | bytes 2654216 | tf_op jit(solution)/shard_map/ppermute | solution.py:657
  70.6 16.7 %collective-permute-start.8 = (bf16[576,1152]{1,0:T(8,128)(2,1)S(1)}, bf16[576,1152]{1,0:T(8,128)(2,1)S(1)}, u32[]{:S(2)}, u32[]{:S(2)}) collective-permute-start(bf16[576,1152]{1,0:T(8,128)(2,1)S(1)} %pad_maximum_fusion.low_ref), channel_id=1, source_target_pairs={{0,1},{1,0},{2,3},{3,2},{4,5},{5,4},{6,7},{7,6},{8,9},{9,8},{10,11... | collective-permute-start | bytes 3981320 | tf_op jit(solution)/shard_map/ppermute | solution.py:671
  134.4 23.2 %collective-permute-start.14 = (bf16[576,1152]{1,0:T(8,128)(2,1)}, bf16[576,1152]{1,0:T(8,128)(2,1)}, u32[]{:S(2)}, u32[]{:S(2)}) collective-permute-start(bf16[576,1152]{1,0:T(8,128)(2,1)} %get-tuple-element.788), channel_id=1, source_target_pairs={{0,1},{1,0},{2,3},{3,2},{4,5},{5,4},{6,7},{7,6},{8,9},{9,8},{10,11... | collective-permute-start | bytes 3981320 | tf_op jit(solution)/shard_map/ppermute | solution.py:692
  134.6 18.3 %collective-permute-start.15 = (f32[288,128]{1,0:T(8,128)S(1)}, f32[288,128]{1,0:T(8,128)}, u32[]{:S(2)}, u32[]{:S(2)}) collective-permute-start(f32[288,128]{1,0:T(8,128)S(1)} %add.69), channel_id=1, source_target_pairs={{8,16},{12,20},{16,8},{20,12},{9,17},{13,21},{17,9},{21,13},{10,18... | collective-permute-start | bytes 442376 | tf_op jit(solution)/shard_map/ppermute | solution.py:806
  135.9 61.1 %collective-permute-start.9 = (bf16[288,1152]{1,0:T(8,128)(2,1)S(1)}, bf16[288,1152]{1,0:T(8,128)(2,1)}, u32[]{:S(2)}, u32[]{:S(2)}) collective-permute-start(bf16[288,1152]{1,0:T(8,128)(2,1)S(1)} %get-tuple-element.733), channel_id=1, source_target_pairs={{0,4},{4,0},{8,12},{12,8},{16,20},{20,16},{24,28},{28,24},{1,5},{5... | collective-permute-start | bytes 1990664 | tf_op jit(solution)/shard_map/ppermute | solution.py:756
  151.1 44.2 %collective-permute-start.13 = (bf16[576,1152]{1,0:T(8,128)(2,1)S(1)}, bf16[576,1152]{1,0:T(8,128)(2,1)S(1)}, u32[]{:S(2)}, u32[]{:S(2)}) collective-permute-start(bf16[576,1152]{1,0:T(8,128)(2,1)S(1)} %get-tuple-element.784), channel_id=1, source_target_pairs={{0,1},{1,0},{2,3},{3,2},{4,5},{5,4},{6,7},{7,6},{8,9},{9,8},{10,11... | collective-permute-start | bytes 3981320 | tf_op jit(solution)/shard_map/ppermute | solution.py:692
  151.3 48.5 %collective-permute-start.18 = (bf16[576,1152]{1,0:T(8,128)(2,1)S(1)}, bf16[576,1152]{1,0:T(8,128)(2,1)S(1)}, u32[]{:S(2)}, u32[]{:S(2)}) collective-permute-start(bf16[576,1152]{1,0:T(8,128)(2,1)S(1)} %copy-done.26), channel_id=1, source_target_pairs={{0,2},{1,3},{2,0},{3,1},{4,6},{5,7},{6,4},{7,5},{8,10},{9,11},{10,... | collective-permute-start | bytes 3981320 | tf_op jit(solution)/shard_map/ppermute | solution.py:703
  153.8 43.2 %collective-permute-start.16 = (f32[288,128]{1,0:T(8,128)S(1)}, f32[288,128]{1,0:T(8,128)S(1)}, u32[]{:S(2)}, u32[]{:S(2)}) collective-permute-start(f32[288,128]{1,0:T(8,128)S(1)} %add.70), channel_id=1, source_target_pairs={{8,0},{12,4},{16,24},{20,28},{0,8},{4,12},{24,16},{28,20},{9,1},{1... | collective-permute-start | bytes 442376 | tf_op jit(solution)/shard_map/ppermute | solution.py:806
  200.9 38.0 %collective-permute-start.26 = (bf16[576,1152]{1,0:T(8,128)(2,1)}, bf16[576,1152]{1,0:T(8,128)(2,1)}, u32[]{:S(2)}, u32[]{:S(2)}) collective-permute-start(bf16[576,1152]{1,0:T(8,128)(2,1)} %whole.9), channel_id=1, source_target_pairs={{0,2},{1,3},{2,0},{3,1},{4,6},{5,7},{6,4},{7,5},{8,10},{9,11},{10,... | collective-permute-start | bytes 3981320 | tf_op jit(solution)/shard_map/ppermute | solution.py:703
  202.3 19.8 %collective-permute-start.17 = (bf16[96,2304]{1,0:T(8,128)(2,1)S(1)}, bf16[96,2304]{1,0:T(8,128)(2,1)S(1)}, u32[]{:S(2)}, u32[]{:S(2)}) collective-permute-start(bf16[96,2304]{1,0:T(8,128)(2,1)S(1)} %pad_maximum_fusion.5.refs_0_), channel_id=1, source_target_pairs={{0,8},{4,12},{8,0},{12,4},{16,24},{20,28},{24,16},{28,20},{1,9},{5... | collective-permute-start | bytes 1327112 | tf_op jit(solution)/shard_map/ppermute | solution.py:592
  214.2 34.2 %collective-permute-start.30 = (bf16[576,1152]{1,0:T(8,128)(2,1)S(1)}, bf16[576,1152]{1,0:T(8,128)(2,1)S(1)}, u32[]{:S(2)}, u32[]{:S(2)}) collective-permute-start(bf16[576,1152]{1,0:T(8,128)(2,1)S(1)} %whole.11), channel_id=1, source_target_pairs={{0,4},{4,0},{8,12},{12,8},{16,20},{20,16},{24,28},{28,24},{1,5},{5... | collective-permute-start | bytes 3981320 | tf_op jit(solution)/shard_map/ppermute | solution.py:746
  223.2 18.0 %collective-permute-start.25 = (bf16[96,2304]{1,0:T(8,128)(2,1)S(1)}, bf16[96,2304]{1,0:T(8,128)(2,1)S(1)}, u32[]{:S(2)}, u32[]{:S(2)}) collective-permute-start(bf16[96,2304]{1,0:T(8,128)(2,1)S(1)} %pad_maximum_fusion.8.refs_0_), channel_id=1, source_target_pairs={{0,8},{4,12},{8,0},{12,4},{16,24},{20,28},{24,16},{28,20},{1,9},{5... | collective-permute-start | bytes 1327112 | tf_op jit(solution)/shard_map/ppermute | solution.py:592
  232.9 17.7 %collective-permute-start.29 = (bf16[96,2304]{1,0:T(8,128)(2,1)S(1)}, bf16[96,2304]{1,0:T(8,128)(2,1)S(1)}, u32[]{:S(2)}, u32[]{:S(2)}) collective-permute-start(bf16[96,2304]{1,0:T(8,128)(2,1)S(1)} %chunk_step.59), channel_id=1, source_target_pairs={{0,8},{4,12},{8,0},{12,4},{16,24},{20,28},{24,16},{28,20},{1,9},{5... | collective-permute-start | bytes 1327112 | tf_op jit(solution)/shard_map/ppermute | solution.py:592
  242.3 17.8 %collective-permute-start.27 = (bf16[96,2304]{1,0:T(8,128)(2,1)S(1)}, bf16[96,2304]{1,0:T(8,128)(2,1)S(1)}, u32[]{:S(2)}, u32[]{:S(2)}) collective-permute-start(bf16[96,2304]{1,0:T(8,128)(2,1)S(1)} %chunk_step.62), channel_id=1, source_target_pairs={{0,8},{4,12},{8,0},{12,4},{16,24},{20,28},{24,16},{28,20},{1,9},{5... | collective-permute-start | bytes 1327112 | tf_op jit(solution)/shard_map/ppermute | solution.py:592
  252.9 16.7 %collective-permute-start.32 = (bf16[96,2304]{1,0:T(8,128)(2,1)S(1)}, bf16[96,2304]{1,0:T(8,128)(2,1)S(1)}, u32[]{:S(2)}, u32[]{:S(2)}) collective-permute-start(bf16[96,2304]{1,0:T(8,128)(2,1)S(1)} %chunk_step.65), channel_id=1, source_target_pairs={{0,8},{4,12},{8,0},{12,4},{16,24},{20,28},{24,16},{28,20},{1,9},{5... | collective-permute-start | bytes 1327112 | tf_op jit(solution)/shard_map/ppermute | solution.py:592
  261.2 17.2 %collective-permute-start.37 = (bf16[96,2304]{1,0:T(8,128)(2,1)S(1)}, bf16[96,2304]{1,0:T(8,128)(2,1)S(1)}, u32[]{:S(2)}, u32[]{:S(2)}) collective-permute-start(bf16[96,2304]{1,0:T(8,128)(2,1)S(1)} %get-tuple-element.986.refs_1_), channel_id=1, source_target_pairs={{0,4},{4,0},{8,12},{12,8},{16,20},{20,16},{24,28},{28,24},{1,5},{5... | collective-permute-start | bytes 1327112 | tf_op jit(solution)/shard_map/ppermute | solution.py:596
  262.4 16.7 %collective-permute-start.36 = (bf16[96,2304]{1,0:T(8,128)(2,1)S(1)}, bf16[96,2304]{1,0:T(8,128)(2,1)S(1)}, u32[]{:S(2)}, u32[]{:S(2)}) collective-permute-start(bf16[96,2304]{1,0:T(8,128)(2,1)S(1)} %chunk_step.68), channel_id=1, source_target_pairs={{0,8},{4,12},{8,0},{12,4},{16,24},{20,28},{24,16},{28,20},{1,9},{5... | collective-permute-start | bytes 1327112 | tf_op jit(solution)/shard_map/ppermute | solution.py:592
  271.7 18.3 %collective-permute-start.41 = (bf16[96,2304]{1,0:T(8,128)(2,1)S(1)}, bf16[96,2304]{1,0:T(8,128)(2,1)S(1)}, u32[]{:S(2)}, u32[]{:S(2)}) collective-permute-start(bf16[96,2304]{1,0:T(8,128)(2,1)S(1)} %chunk_step.71), channel_id=1, source_target_pairs={{0,8},{4,12},{8,0},{12,4},{16,24},{20,28},{24,16},{28,20},{1,9},{5... | collective-permute-start | bytes 1327112 | tf_op jit(solution)/shard_map/ppermute | solution.py:592
  279.9 17.1 %collective-permute-start.39 = (bf16[96,2304]{1,0:T(8,128)(2,1)S(1)}, bf16[96,2304]{1,0:T(8,128)(2,1)S(1)}, u32[]{:S(2)}, u32[]{:S(2)}) collective-permute-start(bf16[96,2304]{1,0:T(8,128)(2,1)S(1)} %get-tuple-element.1054.refs_0_), channel_id=1, source_target_pairs={{0,4},{4,0},{8,12},{12,8},{16,20},{20,16},{24,28},{28,24},{1,5},{5... | collective-permute-start | bytes 1327112 | tf_op jit(solution)/shard_map/ppermute | solution.py:596
  281.1 17.8 %collective-permute-start.38 = (bf16[96,2304]{1,0:T(8,128)(2,1)S(1)}, bf16[96,2304]{1,0:T(8,128)(2,1)S(1)}, u32[]{:S(2)}, u32[]{:S(2)}) collective-permute-start(bf16[96,2304]{1,0:T(8,128)(2,1)S(1)} %chunk_step.74), channel_id=1, source_target_pairs={{0,8},{4,12},{8,0},{12,4},{16,24},{20,28},{24,16},{28,20},{1,9},{5... | collective-permute-start | bytes 1327112 | tf_op jit(solution)/shard_map/ppermute | solution.py:592
  301.0 20.1 %collective-permute-start.48 = (bf16[96,2304]{1,0:T(8,128)(2,1)S(1)}, bf16[96,2304]{1,0:T(8,128)(2,1)S(1)}, u32[]{:S(2)}, u32[]{:S(2)}) collective-permute-start(bf16[96,2304]{1,0:T(8,128)(2,1)S(1)} %chunk_step.80), channel_id=1, source_target_pairs={{0,8},{4,12},{8,0},{12,4},{16,24},{20,28},{24,16},{28,20},{1,9},{5... | collective-permute-start | bytes 1327112 | tf_op jit(solution)/shard_map/ppermute | solution.py:592
  309.2 17.9 %collective-permute-start.54 = (bf16[96,2304]{1,0:T(8,128)(2,1)S(1)}, bf16[96,2304]{1,0:T(8,128)(2,1)S(1)}, u32[]{:S(2)}, u32[]{:S(2)}) collective-permute-start(bf16[96,2304]{1,0:T(8,128)(2,1)S(1)} %get-tuple-element.1125.refs_0_), channel_id=1, source_target_pairs={{0,4},{4,0},{8,12},{12,8},{16,20},{20,16},{24,28},{28,24},{1,5},{5... | collective-permute-start | bytes 1327112 | tf_op jit(solution)/shard_map/ppermute | solution.py:596
  310.8 18.2 %collective-permute-start.53 = (bf16[96,2304]{1,0:T(8,128)(2,1)S(1)}, bf16[96,2304]{1,0:T(8,128)(2,1)S(1)}, u32[]{:S(2)}, u32[]{:S(2)}) collective-permute-start(bf16[96,2304]{1,0:T(8,128)(2,1)S(1)} %chunk_step.83), channel_id=1, source_target_pairs={{0,8},{4,12},{8,0},{12,4},{16,24},{20,28},{24,16},{28,20},{1,9},{5... | collective-permute-start | bytes 1327112 | tf_op jit(solution)/shard_map/ppermute | solution.py:592
  341.1 17.5 %collective-permute-start.58 = (bf16[96,2304]{1,0:T(8,128)(2,1)S(1)}, bf16[96,2304]{1,0:T(8,128)(2,1)S(1)}, u32[]{:S(2)}, u32[]{:S(2)}) collective-permute-start(bf16[96,2304]{1,0:T(8,128)(2,1)S(1)} %chunk_step.92), channel_id=1, source_target_pairs={{0,8},{4,12},{8,0},{12,4},{16,24},{20,28},{24,16},{28,20},{1,9},{5... | collective-permute-start | bytes 1327112 | tf_op jit(solution)/shard_map/ppermute | solution.py:592
  367.7 22.5 %collective-permute-start.70 = (bf16[96,2304]{1,0:T(8,128)(2,1)S(1)}, bf16[96,2304]{1,0:T(8,128)(2,1)S(1)}, u32[]{:S(2)}, u32[]{:S(2)}) collective-permute-start(bf16[96,2304]{1,0:T(8,128)(2,1)S(1)} %chunk_step.97.refs_1_), channel_id=1, source_target_pairs={{0,8},{4,12},{8,0},{12,4},{16,24},{20,28},{24,16},{28,20},{1,9},{5... | collective-permute-start | bytes 1327112 | tf_op jit(solution)/shard_map/ppermute | solution.py:592
  370.5 19.7 %collective-permute-start.71 = (bf16[96,2304]{1,0:T(8,128)(2,1)S(1)}, bf16[96,2304]{1,0:T(8,128)(2,1)S(1)}, u32[]{:S(2)}, u32[]{:S(2)}) collective-permute-start(bf16[96,2304]{1,0:T(8,128)(2,1)S(1)} %get-tuple-element.1252.refs_0_), channel_id=1, source_target_pairs={{0,4},{4,0},{8,12},{12,8},{16,20},{20,16},{24,28},{28,24},{1,5},{5... | collective-permute-start | bytes 1327112 | tf_op jit(solution)/shard_map/ppermute | solution.py:596
  384.1 17.0 %collective-permute-start.66 = (bf16[96,2304]{1,0:T(8,128)(2,1)S(1)}, bf16[96,2304]{1,0:T(8,128)(2,1)S(1)}, u32[]{:S(2)}, u32[]{:S(2)}) collective-permute-start(bf16[96,2304]{1,0:T(8,128)(2,1)S(1)} %chunk_step.100.refs_1_), channel_id=1, source_target_pairs={{0,8},{4,12},{8,0},{12,4},{16,24},{20,28},{24,16},{28,20},{1,9},{5... | collective-permute-start | bytes 1327112 | tf_op jit(solution)/shard_map/ppermute | solution.py:592
  391.8 24.8 %collective-permute-start.73 = (bf16[96,2304]{1,0:T(8,128)(2,1)S(1)}, bf16[96,2304]{1,0:T(8,128)(2,1)S(1)}, u32[]{:S(2)}, u32[]{:S(2)}) collective-permute-start(bf16[96,2304]{1,0:T(8,128)(2,1)S(1)} %chunk_step.102.refs_1_), channel_id=1, source_target_pairs={{0,8},{4,12},{8,0},{12,4},{16,24},{20,28},{24,16},{28,20},{1,9},{5... | collective-permute-start | bytes 1327112 | tf_op jit(solution)/shard_map/ppermute | solution.py:592
  401.2 16.9 %collective-permute-start.77 = (bf16[96,2304]{1,0:T(8,128)(2,1)S(1)}, bf16[96,2304]{1,0:T(8,128)(2,1)S(1)}, u32[]{:S(2)}, u32[]{:S(2)}) collective-permute-start(bf16[96,2304]{1,0:T(8,128)(2,1)S(1)} %chunk_step.105.refs_0_), channel_id=1, source_target_pairs={{0,4},{4,0},{8,12},{12,8},{16,20},{20,16},{24,28},{28,24},{1,5},{5... | collective-permute-start | bytes 1327112 | tf_op jit(solution)/shard_map/ppermute | solution.py:596
  (147 other events, 1539.4 us)

commit v5 on v4

--- a/solution.py
+++ b/solution.py
@@ -209,7 +209,8 @@
     return pl.BlockSpec(shape, lambda *at: zeros, pipeline_mode=pl.Buffered(1))
 
 
-def gates_kernel(pick_ref, low_ref, high_ref, w_ref, out_ref, x_ref, *copy_refs):
+def gates_kernel(skip, pick_ref, low_ref, high_ref, w_ref, *refs):
+    out_ref, x_ref, *copy_refs = refs[skip:]
     half_rows = low_ref.shape[0]
 
     @pl.when(pl.program_id(0) == 0)
@@ -227,7 +228,7 @@
         copy_ref[...] = w_ref[...]
 
 
-def gates_step(pick, w_rows, own, sibling, copy):
+def gates_step(pick, w_rows, own, sibling, copy, window, held):
     taps, kinds, width, depth = w_rows.shape
     rows, span = own.shape
     block = lambda last: pl.BlockSpec((1, kinds, width // 2, last), lambda g, p: (g, 0, 0, 0))
@@ -237,16 +238,21 @@
         pl.BlockSpec((1, kinds, width // 2, 2 * rows), lambda g, p: (g, 0, p[0], p[1])),
     ]
     operands = [own, sibling, w_rows]
-    out_specs = [block(span), pl.BlockSpec((2 * rows, span), lambda g, p: (0, 0))]
+    aliases = {}
+    if held is not None:
+        specs.append(pl.BlockSpec(memory_space=pltpu.HBM))
+        operands.append(held)
+        aliases = {len(operands): 1}
+    out_specs = [block(span), pl.BlockSpec((2 * rows, span), lambda g, p: (0, window))]
     out_shape = [
         jax.ShapeDtypeStruct((taps, kinds, width // 2, span), jnp.float32),
-        jax.ShapeDtypeStruct((2 * rows, span), jnp.bfloat16),
+        jax.ShapeDtypeStruct((depth, 2 * span), jnp.bfloat16),
     ]
     if copy:
         out_specs.append(block(2 * rows))
         out_shape.append(jax.ShapeDtypeStruct((taps, kinds, width // 2, 2 * rows), jnp.bfloat16))
     return pl.pallas_call(
-        gates_kernel,
+        functools.partial(gates_kernel, 0 if held is None else 1),
         grid_spec=pltpu.PrefetchScalarGridSpec(
             num_scalar_prefetch=1,
             grid=(taps,),
@@ -254,14 +260,16 @@
             out_specs=out_specs,
         ),
         out_shape=out_shape,
-        compiler_params=pltpu.CompilerParams(vmem_limit_bytes=32 * 2**20),
+        input_output_aliases=aliases,
+        compiler_params=pltpu.CompilerParams(vmem_limit_bytes=50 * 2**20),
         cost_estimate=HIDDEN_COST,
         name="gates_step",
     )(pick, *operands)
 
 
-def gates_pool_kernel(pick_ref, length_ref, low_ref, high_ref, w_ref, base_ref, small_ref, grad_ref,
-                      hidden_ref, sums_ref, gg_ref, x_ref, *refs):
+def gates_pool_kernel(skip, pick_ref, length_ref, low_ref, high_ref, w_ref, base_ref, small_ref,
+                      grad_ref, *refs):
+    hidden_ref, sums_ref, gg_ref, x_ref, *refs = refs[skip:]
     half_rows = low_ref.shape[0]
 
     @pl.when(pl.program_id(0) == 0)
@@ -296,7 +304,7 @@
     ]
 
 
-def gates_pool(pick, length, w_rows, own, sibling, base, small, grad, copy):
+def gates_pool(pick, length, w_rows, own, sibling, base, small, grad, held, copy, window, before):
     taps, kinds, width, depth = w_rows.shape
     rows, span = own.shape
     width //= 2
@@ -309,7 +317,7 @@
         copy_specs = [pl.BlockSpec((taps, kinds, part, 2 * rows), lambda i, p: (0, 0, i, 0))]
         copy_shapes = [jax.ShapeDtypeStruct((taps, kinds, width, 2 * rows), jnp.bfloat16)]
     return pl.pallas_call(
-        gates_pool_kernel,
+        functools.partial(gates_pool_kernel, 1 + len(before)),
         grid_spec=pltpu.PrefetchScalarGridSpec(
             num_scalar_prefetch=1,
             grid=(count,),
@@ -323,23 +331,28 @@
                 wide,
                 lines(LANES),
                 lines(span),
-            ],
+            ]
+            + [pl.BlockSpec(memory_space=pltpu.HBM)] * (1 + len(before)),
             out_specs=[
                 lines(span),
                 lines(LANES),
-                wide,
-                pl.BlockSpec((2 * rows, span), lambda i, p: (0, 0)),
+                pl.BlockSpec((taps, kinds, part, span), lambda i, p: (0, 0, i, window)),
+                pl.BlockSpec((2 * rows, span), lambda i, p: (1, window)),
                 *copy_specs,
             ],
             scratch_shapes=pool_scratch(part, span),
         ),
-        out_shape=pool_shapes(width, span)
-        + [jax.ShapeDtypeStruct((2 * rows, span), jnp.bfloat16)]
+        out_shape=pool_shapes(width, span)[:2]
+        + [
+            jax.ShapeDtypeStruct((taps, kinds, width, 2 * span), jnp.bfloat16),
+            jax.ShapeDtypeStruct((depth, 2 * span), jnp.bfloat16),
+        ]
         + copy_shapes,
-        compiler_params=pltpu.CompilerParams(vmem_limit_bytes=40 * 2**20),
+        input_output_aliases={8: 3, **({9: 2} if before else {})},
+        compiler_params=pltpu.CompilerParams(vmem_limit_bytes=50 * 2**20),
         cost_estimate=HIDDEN_COST,
         name="gates_pool",
-    )(pick, length, own, sibling, w_rows, base, small, grad)
+    )(pick, length, own, sibling, w_rows, base, small, grad, held, *before)
 
 
 def whole_kernel(function, count, *refs):
@@ -374,9 +387,9 @@
         ].astype(jnp.bfloat16)
 
 
-def back_products(pick, weights, gg):
+def back_products(pick, weights, gg, window):
     depth, columns = weights.shape
-    span = gg.shape[1]
+    span = gg.shape[1] // 2
     part = 384
     return pl.pallas_call(
         back_kernel,
@@ -385,7 +398,9 @@
             grid=(columns // part,),
             in_specs=[
                 pl.BlockSpec((depth, part), lambda i, p: (0, i)),
-                once((depth, span)),
+                pl.BlockSpec(
+                    (depth, span), lambda i, p: (0, window), pipeline_mode=pl.Buffered(1)
+                ),
             ],
             out_specs=[
                 pl.BlockSpec((columns // 2, span), lambda i, p: (0, 0)),
@@ -556,12 +571,16 @@
     middle = line_pairs([(1, 2), (2, 1)])
     sums, totals, finals = {}, {}, {}
     got_edge, got_middle, got_pair = {}, {}, {}
-    size = chunks[0].shape[0]
+    size = chunks.shape[0] // CHUNKS
 
     def run(function, outputs, *operands):
-        return order(chunk_step(function, outputs, flag, size, *order(operands)))
-
-    payload = order(chunks[0])
+        arrays = order(tuple(o[0] if isinstance(o, tuple) else o for o in operands))
+        operands = [
+            (array, o[1]) if isinstance(o, tuple) else array for array, o in zip(arrays, operands)
+        ]
+        return order(chunk_step(function, outputs, flag, size, *operands))
+
+    (payload,) = run(take_chunk, 1, (chunks, 0))
     got_edge[0] = lax.ppermute(payload, "dp", edge)
     for n in range(CHUNKS + LAG + 3):
         final = None
@@ -569,9 +588,9 @@
         if k in got_edge:
             got = got_edge.pop(k)
             if k < CHUNKS and k >= LAG:
-                sums[k], final = run(sum_and_final, 2, chunks[k], got, totals.pop(k - LAG))
+                sums[k], final = run(sum_and_final, 2, (chunks, k), got, totals.pop(k - LAG))
             elif k < CHUNKS:
-                (sums[k],) = run(sum_chunk, 1, chunks[k], got)
+                (sums[k],) = run(sum_chunk, 1, (chunks, k), got)
             else:
                 (final,) = run(final_chunk, 1, got, totals.pop(k - LAG))
             if k < CHUNKS:
@@ -583,9 +602,9 @@
             (totals[k],) = run(total_chunk, 1, sums.pop(k), got)
         k = n + 1 - LAG
         if k in totals and n + 1 < CHUNKS:
-            (payload,) = run(final_chunk, 1, chunks[n + 1], totals[k])
+            (payload,) = run(final_chunk, 1, (chunks, n + 1), totals[k])
         elif n + 1 < CHUNKS:
-            payload = order(chunks[n + 1])
+            (payload,) = run(take_chunk, 1, (chunks, n + 1))
         elif k in totals:
             payload = totals[k]
         if payload is not None:
@@ -646,8 +665,8 @@
         out_grad, done.token = done.token, small_mine
         grads = run(lambda g: mix(g.T, slots), out_grad)
         grads_mine, grads_other = done((half(grads, 0, side), half(grads, 0, other_side)))
-        gates, near, w_near = run(
-            lambda *given: gates_step(*given, True), pick_near, w_rows, x_own, near_got
+        gates, held, w_near = run(
+            lambda *given: gates_step(*given, True, 0, None), pick_near, w_rows, x_own, near_got
         )
         cut = width * 2 // 3
         far_own = done(far_got)
@@ -660,11 +679,23 @@
         far_got = done(far_got)
         pair_near_got = lax.ppermute(done(x_pair), "mp", core_pairs)
         far_own, far_got, gates, grads_mine = done((far_own, far_got, gates, grads_mine))
-        hidden_mine, sums_mine, gg_mine, far, w_far = gates_pool(
-            pick_far, lengths, w_rows, far_own, far_got, gates, done.token, grads_mine, True
+        held = done(held)
+        hidden_mine, sums_mine, gg, held, w_far = gates_pool(
+            pick_far,
+            lengths,
+            w_rows,
+            far_own,
+            far_got,
+            gates,
+            done.token,
+            grads_mine,
+            held,
+            True,
+            0,
+            (),
         )
         done.token = sums_mine
-        gg_mine = done(gg_mine.reshape(rows, span))
+        gg, held = done((gg, held))
         pair_far_own, grads_pair = run(
             lambda a, b: (jnp.concatenate([a, b[: width - cut]], axis=0), b[width - cut :]), *relay
         )
@@ -683,10 +714,10 @@
 
         def fill_back(window, part):
             keep, give = run(
-                back_products,
+                lambda *given: back_products(*given, window),
                 pick_near,
                 (w_near, w_far)[part].reshape(rows, depth // 2),
-                gg_mine if window == 0 else gg_pair,
+                gg.reshape(rows, 2 * span),
             )
             kept["keep", window, part] = keep
             kept["core", window, part] = lax.ppermute(give, "mp", core_pairs)
@@ -702,14 +733,19 @@
         def fill_cross(window):
             kept["cross", window] = lax.ppermute(done(kept["sum", window, 1]), "mp", chip_pairs)
 
-        pair_gates, pair_near = run(
-            lambda *given: gates_step(*given, False), pick_near, w_rows, x_pair, pair_near_got
+        pair_gates, held = run(
+            lambda *given: gates_step(*given[:4], False, 1, given[4]),
+            pick_near,
+            w_rows,
+            x_pair,
+            pair_near_got,
+            held,
         )
         small_pair, grads_pair = done((small_pair, grads_pair))
         length_pair = small_pair[0, 5:6].astype(jnp.int32)
         small_pair = jnp.where(lane[:own] < 3, small_mine, small_pair)
-        hidden_pair, sums_pair, gg_pair, pair_far = run(
-            lambda *given: gates_pool(*given, False),
+        hidden_pair, sums_pair, gg, held = run(
+            lambda *given: gates_pool(*given[:9], False, 1, given[9:]),
             pick_far,
             length_pair,
             w_rows,
@@ -718,24 +754,17 @@
             pair_gates,
             small_pair,
             grads_pair,
+            held,
+            gg,
         )
-        gg_pair = gg_pair.reshape(rows, span)
 
         size = rows // CHUNKS
         per = own // size
-        chunks = {}
 
         def products():
-            def more(total, gg, x):
-                return (total + cols_dot(gg, x)).astype(jnp.bfloat16)
-
-            own_near = run(cols_dot, gg_mine, near)
-            near_part = run(more, own_near, gg_pair, pair_near)
-            own_far = run(cols_dot, gg_mine, far)
-            far_part = run(more, own_far, gg_pair, pair_far)
-            for k in range(CHUNKS):
-                at = slice(k * size, (k + 1) * size)
-                chunks[k] = jnp.concatenate([near_part[at], far_part[at]], axis=1)
+            return run(
+                lambda gg, x: cols_dot(gg.reshape(rows, 2 * span), x).astype(jnp.bfloat16), gg, held
+            )
 
         def fill_send():
             (give,) = run(
@@ -846,7 +875,7 @@
         fill_back(0, 0)
         fill_bias(2)()
         fill_core(0, 1)
-        products()
+        chunks = products()
         fill_core(0, 0)
         receive("hidden")
         fill_bias(3)()
@@ -855,9 +884,10 @@
             1: fill((fill_send,)),
             3: fill((receive, ("cross", 0))),
             4: fill((receive, "pair")),
-            CHUNKS - 1: fill((fill_hidden,)),
             CHUNKS: fill((send, "sums", sums_pair)),
-            CHUNKS + 2: fill((receive, "sums"), (fill_input,)),
+            CHUNKS + 2: fill((fill_hidden,)),
+            CHUNKS + 3: fill((fill_input,)),
+            CHUNKS + 4: fill((receive, "sums")),
         }
         piped_sums(done, chunks, pairs, fillers, arrived)
         input_grad, hidden = kept["input"], kept["hidden out"]

time: 447 us -> 429 us (0.960)
  waiting for transfers between devices: 68.1 us -> 95.9 us
  starting transfers between devices: 146 us -> 124 us
  local copies, waits for them, and re-layouts: 38.9 us -> 28.3 us
  matrix products: 41 us -> 31.5 us
    ppermute x21, waiting for transfers between devices: 27.9 us -> 65.7 us  [piped_sums(): got_edge[n + 1] = lax.ppermute(payload, 'dp', edge)]
    ppermute x21, starting transfers between devices: 84.5 us -> 65.7 us  [piped_sums(): got_edge[n + 1] = lax.ppermute(payload, 'dp', edge)]
    ppermute x18, waiting for transfers between devices: 18.4 us -> 2.62 us  [piped_sums(): got_pair[k] = lax.ppermute(final, 'dp', pairs)]
    dot_general x4 -> x1, matrix products: 33.1 us -> 23.6 us  [cols_dot(): lax.dot_general(left, right, (((1,), (1,)), ((), ())), preferred_element_...]
    pallas_call x4, Pallas kernels: 55.4 us -> 64.1 us  [the longest x2 41.2 us: gates_pool(): pl.pallas_call(functools.partial(gates_pool_kernel, 1 + len(before)), gri...]
    unnamed x199 -> x117, local copies, waits for them, and re-layouts: 28.1 us -> 20.2 us
    ppermute x2, waiting for transfers between devices: 3.81 us -> 10.7 us  [send(): kept[name] = lax.ppermute(done(value), 'dp', pairs)]
    pallas_call x54 -> x58, Pallas kernels: 12.2 us -> 6.54 us  [chunk_step(): pl.pallas_call(functools.partial(chunk_kernel, function, len(operands)),...]
  transfers between devices with their start and end apart: 80 -> 80, of which waited for: 26 -> 26; matrix products, arithmetic and copies ran while one was open for 13% -> 10% of each run, Pallas kernels for 23% -> 24%
where the time goes in v5:
time: 429 us; the launch traced here: 423 us
  Pallas kernels  132 us (31%)
  starting transfers between devices  124 us (29%)
  waiting for transfers between devices  95.9 us (22%)
  matrix products  31.5 us (7%)
  local copies, waits for them, and re-layouts  28.3 us (7%)
  other arithmetic  7.7 us (2%)
    ppermute x21, waiting for transfers between devices, piped_sums(): got_edge[n + 1] = lax.ppermute(payload, 'dp', edge)  65.7 us
    ppermute x21, starting transfers between devices, piped_sums(): got_edge[n + 1] = lax.ppermute(payload, 'dp', edge)  65.7 us
    pallas_call x2, Pallas kernels, gates_pool(): pl.pallas_call(functools.partial(gates_pool_kernel, 1 + len(before)), gri...  41.2 us
    pallas_call x4, Pallas kernels, back_products(): pl.pallas_call(back_kernel, grid_spec=pltpu.PrefetchScalarGridSpec(num_sc...  32.7 us
    dot_general x1, matrix products, cols_dot(): lax.dot_general(left, right, (((1,), (1,)), ((), ())), preferred_element_...  23.6 us
    pallas_call x2, Pallas kernels, gates_step(): pl.pallas_call(functools.partial(gates_kernel, 0 if held is None else 1),...  22.8 us
    ppermute x18, starting transfers between devices, piped_sums(): got_pair[k] = lax.ppermute(final, 'dp', pairs)  21.2 us
    pallas_call x6, Pallas kernels, write_chunks(): pl.pallas_call(functools.partial(write_kernel, count), grid=(2,), in_spec...  20.2 us
  transfers between devices with their start and end apart: 80, of which 26 were waited for; matrix products, arithmetic and copies ran while one was open for 10% of the time, Pallas kernels for 24%

profile of v5, /device:TPU:0, one launch (start us, length us, event | category | flops | bytes accessed | tf_op | source)
XLA Modules:
  0.0 422.9 jit_solution(7092215113850910479)
XLA Ops:
  11.9 4.1 convolution_convert_fusion.1
  19.5 11.8 %gates_step.2 = (f32[2,3,288,1152]{3,2,1,0:T(8,128)}, bf16[2304,2304]{1,0:T(8,128)(2,1)}, bf16[2,3,288,1152]{3,2,1,0:T(8,128)(2,1)}) custom-call(s32[3]{0:T(128)S(1)} %add_add_fusion.1.pick_ref, bf16[576,1152]{1,0:T(8,128)(2,1)} %convolution_convert_fusion.2.low_ref, bf16[576,1152]{1,0:T(8,128)(2,1)S(1)} %copy-done.21, bf16[2,3,576,2304]{3,2,1,0:T(8,128)(2,1)} %bitcast.34), custom_call_target="tpu_custom_call" | custom-call | flops 1 | bytes 1 | tf_op jit(solution)/shard_map/gates_step/pallas_call | solution.py:254
  31.3 7.6 %collective-permute-done.low_ref = bf16[576,1152]{1,0:T(8,128)(2,1)} collective-permute-done((bf16[576,1152]{1,0:T(8,128)(2,1)}, bf16[576,1152]{1,0:T(8,128)(2,1)}, u32[]{:S(2)}, u32[]{:S(2)}) %collective-permute-start) | collective-permute-done | bytes 1327136 | tf_op jit(solution)/shard_map/ppermute | solution.py:662
  45.3 21.0 %gates_pool.2 = (bf16[288,1152]{1,0:T(8,128)(2,1)S(1)}, f32[288,128]{1,0:T(8,128)S(1)}, bf16[2,3,288,2304]{3,2,1,0:T(8,128)(2,1)}, bf16[2304,2304]{1,0:T(8,128)(2,1)}, bf16[2,3,288,1152]{3,2,1,0:T(8,128)(2,1)}) custom-call(s32[3]{0:T(128)S(1)} %add_add_fusion.pick_ref, s32[1]{0:T(128)S(6)} %copy.41.length_ref, ...), custom_call_target="tpu_custom_call", output_to_operand_aliasing={{3}: (8, {})} | custom-call | flops 1 | bytes 1 | tf_op jit(solution)/shard_map/gates_pool/pallas_call | solution.py:319
  74.0 11.0 %gates_step.3 = (f32[2,3,288,1152]{3,2,1,0:T(8,128)}, bf16[2304,2304]{1,0:T(8,128)(2,1)}) custom-call(s32[3]{0:T(128)S(1)} %add_add_fusion.1.pick_ref, bf16[576,1152]{1,0:T(8,128)(2,1)S(1)} %collective-permute-done.3.low_ref, bf16[576,1152]{1,0:T(8,128)(2,1)S(1)} %collective-permute-done.7.high_ref, ...), custom_call_target="tpu_custom_call", output_to_operand_aliasing={{1}: (4, {})} | custom-call | flops 1 | bytes 1 | tf_op jit(solution)/shard_map/gates_step/pallas_call | solution.py:254
  87.4 20.2 %gates_pool.3 = (bf16[288,1152]{1,0:T(8,128)(2,1)S(1)}, f32[288,128]{1,0:T(8,128)S(1)}, bf16[2,3,288,2304]{3,2,1,0:T(8,128)(2,1)}, bf16[2304,2304]{1,0:T(8,128)(2,1)}) custom-call(s32[3]{0:T(128)S(1)} %add_add_fusion.pick_ref, s32[1]{0:T(128)} %bitcast.7.length_ref, ...), custom_call_target="tpu_custom_call", output_to_operand_aliasing={{3}: (8, {}), {2}: (9, {})} | custom-call | flops 1 | bytes 1 | tf_op jit(solution)/shard_map/gates_pool/pallas_call | solution.py:319
  110.9 7.6 %back_products.4 = (f32[576,1152]{1,0:T(8,128)S(1)}, bf16[576,1152]{1,0:T(8,128)(2,1)S(1)}) custom-call(s32[3]{0:T(128)S(1)} %add_add_fusion.1.pick_ref, bf16[1728,1152]{1,0:T(8,128)(2,1)S(1)} %bitcast.31, bf16[1728,2304]{1,0:T(8,128)(2,1)S(1)} %bitcast.25), custom_call_target="tpu_custom_call" | custom-call | flops 1 | bytes 1 | tf_op jit(solution)/shard_map/back_products/pallas_call | solution.py:394
  120.3 8.6 %back_products.5 = (f32[576,1152]{1,0:T(8,128)S(1)}, bf16[576,1152]{1,0:T(8,128)(2,1)}) custom-call(s32[3]{0:T(128)S(1)} %add_add_fusion.1.pick_ref, bf16[1728,1152]{1,0:T(8,128)(2,1)S(1)} %bitcast.29, bf16[1728,2304]{1,0:T(8,128)(2,1)S(1)} %bitcast.26), custom_call_target="tpu_custom_call" | custom-call | flops 1 | bytes 1 | tf_op jit(solution)/shard_map/back_products/pallas_call | solution.py:394
  130.5 8.7 %back_products.6 = (f32[576,1152]{1,0:T(8,128)S(1)}, bf16[576,1152]{1,0:T(8,128)(2,1)}) custom-call(s32[3]{0:T(128)S(1)} %add_add_fusion.1.pick_ref, bf16[1728,1152]{1,0:T(8,128)(2,1)S(1)} %bitcast.32, bf16[1728,2304]{1,0:T(8,128)(2,1)S(1)} %bitcast.27), custom_call_target="tpu_custom_call" | custom-call | flops 1 | bytes 1 | tf_op jit(solution)/shard_map/back_products/pallas_call | solution.py:394
  148.0 7.8 %back_products.7 = (f32[576,1152]{1,0:T(8,128)S(1)}, bf16[576,1152]{1,0:T(8,128)(2,1)S(1)}) custom-call(s32[3]{0:T(128)S(1)} %add_add_fusion.1.pick_ref, bf16[1728,1152]{1,0:T(8,128)(2,1)S(1)} %bitcast.30, bf16[1728,2304]{1,0:T(8,128)(2,1)S(1)} %bitcast.28), custom_call_target="tpu_custom_call" | custom-call | flops 1 | bytes 1 | tf_op jit(solution)/shard_map/back_products/pallas_call | solution.py:394
  157.7 4.3 %collective-permute-start.16 = (f32[288,128]{1,0:T(8,128)S(1)}, f32[288,128]{1,0:T(8,128)S(1)}, u32[]{:S(2)}, u32[]{:S(2)}) collective-permute-start(f32[288,128]{1,0:T(8,128)S(1)} %add.64), channel_id=1, source_target_pairs={{8,0},{12,4},{16,24},{20,28},{0,8},{4,12},{24,16},{28,20},{9,1},{1... | collective-permute-start | bytes 442376 | tf_op jit(solution)/shard_map/ppermute | solution.py:835
  163.5 23.6 %convolution_convert_fusion.refs_0_ = bf16[1728,2304]{1,0:T(8,128)(2,1)S(1)} fusion(bf16[1728,2304]{1,0:T(8,128)(2,1)} %bitcast.24, bf16[2304,2304]{1,0:T(8,128)(2,1)} %get-tuple-element.805), kind=kOutput, calls=%fused_computation | convolution fusion | flops 18349867008 | bytes 26542080 | tf_op jit(solution)/shard_map/dot_general | solution.py:204
  194.9 7.0 %collective-permute-done.17.refs_1_ = bf16[96,2304]{1,0:T(8,128)(2,1)S(1)} collective-permute-done((bf16[96,2304]{1,0:T(8,128)(2,1)S(1)}, bf16[96,2304]{1,0:T(8,128)(2,1)S(1)}, u32[]{:S(2)}, u32[]{:S(2)}) %collective-permute-start.17) | collective-permute-done | bytes 442400 | tf_op jit(solution)/shard_map/ppermute | solution.py:584
  205.6 5.8 %collective-permute-done.21.refs_1_ = bf16[96,2304]{1,0:T(8,128)(2,1)S(1)} collective-permute-done((bf16[96,2304]{1,0:T(8,128)(2,1)S(1)}, bf16[96,2304]{1,0:T(8,128)(2,1)S(1)}, u32[]{:S(2)}, u32[]{:S(2)}) %collective-permute-start.21) | collective-permute-done | bytes 442400 | tf_op jit(solution)/shard_map/ppermute | solution.py:611
  212.4 4.7 %collective-permute-start.27 = (bf16[96,2304]{1,0:T(8,128)(2,1)S(1)}, bf16[96,2304]{1,0:T(8,128)(2,1)S(1)}, u32[]{:S(2)}, u32[]{:S(2)}) collective-permute-start(bf16[96,2304]{1,0:T(8,128)(2,1)S(1)} %chunk_step.64), channel_id=1, source_target_pairs={{0,8},{4,12},{8,0},{12,4},{16,24},{20,28},{24,16},{28,20},{1,9},{5... | collective-permute-start | bytes 1327112 | tf_op jit(solution)/shard_map/ppermute | solution.py:611
  217.1 3.8 collective-permute-done.23.refs_1_
  221.9 4.7 %collective-permute-start.24 = (bf16[96,2304]{1,0:T(8,128)(2,1)S(1)}, bf16[96,2304]{1,0:T(8,128)(2,1)S(1)}, u32[]{:S(2)}, u32[]{:S(2)}) collective-permute-start(bf16[96,2304]{1,0:T(8,128)(2,1)S(1)} %chunk_step.67), channel_id=1, source_target_pairs={{0,8},{4,12},{8,0},{12,4},{16,24},{20,28},{24,16},{28,20},{1,9},{5... | collective-permute-start | bytes 1327112 | tf_op jit(solution)/shard_map/ppermute | solution.py:611
  231.4 4.6 %collective-permute-start.30 = (bf16[96,2304]{1,0:T(8,128)(2,1)S(1)}, bf16[96,2304]{1,0:T(8,128)(2,1)S(1)}, u32[]{:S(2)}, u32[]{:S(2)}) collective-permute-start(bf16[96,2304]{1,0:T(8,128)(2,1)S(1)} %chunk_step.70), channel_id=1, source_target_pairs={{0,8},{4,12},{8,0},{12,4},{16,24},{20,28},{24,16},{28,20},{1,9},{5... | collective-permute-start | bytes 1327112 | tf_op jit(solution)/shard_map/ppermute | solution.py:611
  236.0 3.8 collective-permute-done.24.refs_1_
  245.4 3.9 collective-permute-done.30.refs_1_
  254.9 3.9 collective-permute-done.33.refs_1_
  264.4 3.9 collective-permute-done.39.refs_1_
  283.4 3.9 collective-permute-done.41.refs_1_
  292.9 3.9 collective-permute-done.45.refs_1_
  311.8 3.9 collective-permute-done.47.refs_1_
  321.3 3.9 collective-permute-done.53.refs_1_
  340.3 3.9 collective-permute-done.62.refs_1_
  349.7 3.9 collective-permute-done.59.refs_1_
  368.4 4.2 collective-permute-done.67.refs_0_
  377.3 4.8 %collective-permute-done.73.refs_0_ = bf16[96,2304]{1,0:T(8,128)(2,1)} collective-permute-done((bf16[96,2304]{1,0:T(8,128)(2,1)S(1)}, bf16[96,2304]{1,0:T(8,128)(2,1)}, u32[]{:S(2)}, u32[]{:S(2)}) %collective-permute-start.73) | collective-permute-done | bytes 442400 | tf_op jit(solution)/shard_map/ppermute | solution.py:611
  384.4 3.9 write_chunks.10.refs_6_
  405.6 10.7 %collective-permute-done.79 = f32[288,128]{1,0:T(8,128)S(1)} collective-permute-done((f32[288,128]{1,0:T(8,128)S(1)}, f32[288,128]{1,0:T(8,128)S(1)}, u32[]{:S(2)}, u32[]{:S(2)}) %collective-permute-start.79) | collective-permute-done | bytes 147488 | tf_op jit(solution)/shard_map/ppermute | solution.py:785
  (360 shorter events, 190.4 us)
Async XLA Ops:
  6.3 32.6 %collective-permute-start = (bf16[576,1152]{1,0:T(8,128)(2,1)}, bf16[576,1152]{1,0:T(8,128)(2,1)}, u32[]{:S(2)}, u32[]{:S(2)}) collective-permute-start(bf16[576,1152]{1,0:T(8,128)(2,1)} %convolution_convert_fusion.2.low_ref), channel_id=1, source_target_pairs={{0,2},{1,3},{2,0},{3,1},{4,6},{5,7},{6,4},{7,5},{8,10},{9,11},{10,... | collective-permute-start | bytes 3981320 | tf_op jit(solution)/shard_map/ppermute | solution.py:662
  8.8 34.0 %collective-permute-start.3 = (bf16[576,1152]{1,0:T(8,128)(2,1)}, bf16[576,1152]{1,0:T(8,128)(2,1)S(1)}, u32[]{:S(2)}, u32[]{:S(2)}) collective-permute-start(bf16[576,1152]{1,0:T(8,128)(2,1)} %convolution_convert_fusion.2.low_ref), channel_id=1, source_target_pairs={{0,4},{4,0},{8,12},{12,8},{16,20},{20,16},{24,28},{28,24},{1,5},{5... | collective-permute-start | bytes 3981320 | tf_op jit(solution)/shard_map/ppermute | solution.py:663
  41.0 27.1 %collective-permute-start.5 = (bf16[480,1152]{1,0:T(8,128)(2,1)}, bf16[480,1152]{1,0:T(8,128)(2,1)}, u32[]{:S(2)}, u32[]{:S(2)}) collective-permute-start(bf16[480,1152]{1,0:T(8,128)(2,1)} %pad_maximum_fusion.1), channel_id=1, source_target_pairs={{0,4},{4,0},{8,12},{12,8},{16,20},{20,16},{24,28},{28,24},{1,5},{5... | collective-permute-start | bytes 3317768 | tf_op jit(solution)/shard_map/ppermute | solution.py:677
  43.8 22.6 %collective-permute-start.4 = (bf16[384,1152]{1,0:T(8,128)(2,1)}, bf16[384,1152]{1,0:T(8,128)(2,1)}, u32[]{:S(2)}, u32[]{:S(2)}) collective-permute-start(bf16[384,1152]{1,0:T(8,128)(2,1)} %slice.27), channel_id=1, source_target_pairs={{0,2},{1,3},{2,0},{3,1},{4,6},{5,7},{6,4},{7,5},{8,10},{9,11},{10,... | collective-permute-start | bytes 2654216 | tf_op jit(solution)/shard_map/ppermute | solution.py:676
  140.6 21.3 %collective-permute-start.14 = (bf16[576,1152]{1,0:T(8,128)(2,1)}, bf16[576,1152]{1,0:T(8,128)(2,1)}, u32[]{:S(2)}, u32[]{:S(2)}) collective-permute-start(bf16[576,1152]{1,0:T(8,128)(2,1)} %get-tuple-element.793), channel_id=1, source_target_pairs={{0,1},{1,0},{2,3},{3,2},{4,5},{5,4},{6,7},{7,6},{8,9},{9,8},{10,11... | collective-permute-start | bytes 3981320 | tf_op jit(solution)/shard_map/ppermute | solution.py:723
  140.8 16.9 %collective-permute-start.15 = (f32[288,128]{1,0:T(8,128)S(1)}, f32[288,128]{1,0:T(8,128)S(1)}, u32[]{:S(2)}, u32[]{:S(2)}) collective-permute-start(f32[288,128]{1,0:T(8,128)S(1)} %add.63), channel_id=1, source_target_pairs={{8,16},{12,20},{16,8},{20,12},{9,17},{13,21},{17,9},{21,13},{10,18... | collective-permute-start | bytes 442376 | tf_op jit(solution)/shard_map/ppermute | solution.py:835
  141.5 45.9 %collective-permute-start.9 = (bf16[288,1152]{1,0:T(8,128)(2,1)S(1)}, bf16[288,1152]{1,0:T(8,128)(2,1)}, u32[]{:S(2)}, u32[]{:S(2)}) collective-permute-start(bf16[288,1152]{1,0:T(8,128)(2,1)S(1)} %get-tuple-element.740), channel_id=1, source_target_pairs={{0,4},{4,0},{8,12},{12,8},{16,20},{20,16},{24,28},{28,24},{1,5},{5... | collective-permute-start | bytes 1990664 | tf_op jit(solution)/shard_map/ppermute | solution.py:785
  155.8 31.3 %collective-permute-start.13 = (bf16[576,1152]{1,0:T(8,128)(2,1)S(1)}, bf16[576,1152]{1,0:T(8,128)(2,1)S(1)}, u32[]{:S(2)}, u32[]{:S(2)}) collective-permute-start(bf16[576,1152]{1,0:T(8,128)(2,1)S(1)} %get-tuple-element.790), channel_id=1, source_target_pairs={{0,1},{1,0},{2,3},{3,2},{4,5},{5,4},{6,7},{7,6},{8,9},{9,8},{10,11... | collective-permute-start | bytes 3981320 | tf_op jit(solution)/shard_map/ppermute | solution.py:723
  156.2 32.8 %collective-permute-start.19 = (bf16[576,1152]{1,0:T(8,128)(2,1)S(1)}, bf16[576,1152]{1,0:T(8,128)(2,1)S(1)}, u32[]{:S(2)}, u32[]{:S(2)}) collective-permute-start(bf16[576,1152]{1,0:T(8,128)(2,1)S(1)} %copy-done.19), channel_id=1, source_target_pairs={{0,2},{1,3},{2,0},{3,1},{4,6},{5,7},{6,4},{7,5},{8,10},{9,11},{10,... | collective-permute-start | bytes 3981320 | tf_op jit(solution)/shard_map/ppermute | solution.py:734
  157.7 29.7 %collective-permute-start.16 = (f32[288,128]{1,0:T(8,128)S(1)}, f32[288,128]{1,0:T(8,128)S(1)}, u32[]{:S(2)}, u32[]{:S(2)}) collective-permute-start(f32[288,128]{1,0:T(8,128)S(1)} %add.64), channel_id=1, source_target_pairs={{8,0},{12,4},{16,24},{20,28},{0,8},{4,12},{24,16},{28,20},{9,1},{1... | collective-permute-start | bytes 442376 | tf_op jit(solution)/shard_map/ppermute | solution.py:835
  189.0 37.6 %collective-permute-start.28 = (bf16[576,1152]{1,0:T(8,128)(2,1)S(1)}, bf16[576,1152]{1,0:T(8,128)(2,1)S(1)}, u32[]{:S(2)}, u32[]{:S(2)}) collective-permute-start(bf16[576,1152]{1,0:T(8,128)(2,1)S(1)} %whole.9), channel_id=1, source_target_pairs={{0,2},{1,3},{2,0},{3,1},{4,6},{5,7},{6,4},{7,5},{8,10},{9,11},{10,... | collective-permute-start | bytes 3981320 | tf_op jit(solution)/shard_map/ppermute | solution.py:734
  190.7 20.7 %collective-permute-start.21 = (bf16[96,2304]{1,0:T(8,128)(2,1)S(1)}, bf16[96,2304]{1,0:T(8,128)(2,1)S(1)}, u32[]{:S(2)}, u32[]{:S(2)}) collective-permute-start(bf16[96,2304]{1,0:T(8,128)(2,1)S(1)} %chunk_step.59), channel_id=1, source_target_pairs={{0,8},{4,12},{8,0},{12,4},{16,24},{20,28},{24,16},{28,20},{1,9},{5... | collective-permute-start | bytes 1327112 | tf_op jit(solution)/shard_map/ppermute | solution.py:611
  202.3 33.7 %collective-permute-start.25 = (bf16[576,1152]{1,0:T(8,128)(2,1)S(1)}, bf16[576,1152]{1,0:T(8,128)(2,1)S(1)}, u32[]{:S(2)}, u32[]{:S(2)}) collective-permute-start(bf16[576,1152]{1,0:T(8,128)(2,1)S(1)} %whole.11), channel_id=1, source_target_pairs={{0,4},{4,0},{8,12},{12,8},{16,20},{20,16},{24,28},{28,24},{1,5},{5... | collective-permute-start | bytes 3981320 | tf_op jit(solution)/shard_map/ppermute | solution.py:775
  204.2 16.7 %collective-permute-start.23 = (bf16[96,2304]{1,0:T(8,128)(2,1)S(1)}, bf16[96,2304]{1,0:T(8,128)(2,1)S(1)}, u32[]{:S(2)}, u32[]{:S(2)}) collective-permute-start(bf16[96,2304]{1,0:T(8,128)(2,1)S(1)} %chunk_step.61), channel_id=1, source_target_pairs={{0,8},{4,12},{8,0},{12,4},{16,24},{20,28},{24,16},{28,20},{1,9},{5... | collective-permute-start | bytes 1327112 | tf_op jit(solution)/shard_map/ppermute | solution.py:611
  212.4 18.0 %collective-permute-start.27 = (bf16[96,2304]{1,0:T(8,128)(2,1)S(1)}, bf16[96,2304]{1,0:T(8,128)(2,1)S(1)}, u32[]{:S(2)}, u32[]{:S(2)}) collective-permute-start(bf16[96,2304]{1,0:T(8,128)(2,1)S(1)} %chunk_step.64), channel_id=1, source_target_pairs={{0,8},{4,12},{8,0},{12,4},{16,24},{20,28},{24,16},{28,20},{1,9},{5... | collective-permute-start | bytes 1327112 | tf_op jit(solution)/shard_map/ppermute | solution.py:611
  221.9 18.0 %collective-permute-start.24 = (bf16[96,2304]{1,0:T(8,128)(2,1)S(1)}, bf16[96,2304]{1,0:T(8,128)(2,1)S(1)}, u32[]{:S(2)}, u32[]{:S(2)}) collective-permute-start(bf16[96,2304]{1,0:T(8,128)(2,1)S(1)} %chunk_step.67), channel_id=1, source_target_pairs={{0,8},{4,12},{8,0},{12,4},{16,24},{20,28},{24,16},{28,20},{1,9},{5... | collective-permute-start | bytes 1327112 | tf_op jit(solution)/shard_map/ppermute | solution.py:611
  231.4 18.0 %collective-permute-start.30 = (bf16[96,2304]{1,0:T(8,128)(2,1)S(1)}, bf16[96,2304]{1,0:T(8,128)(2,1)S(1)}, u32[]{:S(2)}, u32[]{:S(2)}) collective-permute-start(bf16[96,2304]{1,0:T(8,128)(2,1)S(1)} %chunk_step.70), channel_id=1, source_target_pairs={{0,8},{4,12},{8,0},{12,4},{16,24},{20,28},{24,16},{28,20},{1,9},{5... | collective-permute-start | bytes 1327112 | tf_op jit(solution)/shard_map/ppermute | solution.py:611
  242.1 16.7 %collective-permute-start.33 = (bf16[96,2304]{1,0:T(8,128)(2,1)S(1)}, bf16[96,2304]{1,0:T(8,128)(2,1)S(1)}, u32[]{:S(2)}, u32[]{:S(2)}) collective-permute-start(bf16[96,2304]{1,0:T(8,128)(2,1)S(1)} %chunk_step.73), channel_id=1, source_target_pairs={{0,8},{4,12},{8,0},{12,4},{16,24},{20,28},{24,16},{28,20},{1,9},{5... | collective-permute-start | bytes 1327112 | tf_op jit(solution)/shard_map/ppermute | solution.py:611
  251.5 16.7 %collective-permute-start.39 = (bf16[96,2304]{1,0:T(8,128)(2,1)S(1)}, bf16[96,2304]{1,0:T(8,128)(2,1)S(1)}, u32[]{:S(2)}, u32[]{:S(2)}) collective-permute-start(bf16[96,2304]{1,0:T(8,128)(2,1)S(1)} %chunk_step.76), channel_id=1, source_target_pairs={{0,8},{4,12},{8,0},{12,4},{16,24},{20,28},{24,16},{28,20},{1,9},{5... | collective-permute-start | bytes 1327112 | tf_op jit(solution)/shard_map/ppermute | solution.py:611
  261.4 16.4 %collective-permute-start.35 = (bf16[96,2304]{1,0:T(8,128)(2,1)S(1)}, bf16[96,2304]{1,0:T(8,128)(2,1)S(1)}, u32[]{:S(2)}, u32[]{:S(2)}) collective-permute-start(bf16[96,2304]{1,0:T(8,128)(2,1)S(1)} %chunk_step.79), channel_id=1, source_target_pairs={{0,8},{4,12},{8,0},{12,4},{16,24},{20,28},{24,16},{28,20},{1,9},{5... | collective-permute-start | bytes 1327112 | tf_op jit(solution)/shard_map/ppermute | solution.py:611
  270.5 16.8 %collective-permute-start.41 = (bf16[96,2304]{1,0:T(8,128)(2,1)S(1)}, bf16[96,2304]{1,0:T(8,128)(2,1)S(1)}, u32[]{:S(2)}, u32[]{:S(2)}) collective-permute-start(bf16[96,2304]{1,0:T(8,128)(2,1)S(1)} %chunk_step.82), channel_id=1, source_target_pairs={{0,8},{4,12},{8,0},{12,4},{16,24},{20,28},{24,16},{28,20},{1,9},{5... | collective-permute-start | bytes 1327112 | tf_op jit(solution)/shard_map/ppermute | solution.py:611
  280.0 16.8 %collective-permute-start.45 = (bf16[96,2304]{1,0:T(8,128)(2,1)S(1)}, bf16[96,2304]{1,0:T(8,128)(2,1)S(1)}, u32[]{:S(2)}, u32[]{:S(2)}) collective-permute-start(bf16[96,2304]{1,0:T(8,128)(2,1)S(1)} %chunk_step.85), channel_id=1, source_target_pairs={{0,8},{4,12},{8,0},{12,4},{16,24},{20,28},{24,16},{28,20},{1,9},{5... | collective-permute-start | bytes 1327112 | tf_op jit(solution)/shard_map/ppermute | solution.py:611
  289.4 16.8 %collective-permute-start.50 = (bf16[96,2304]{1,0:T(8,128)(2,1)S(1)}, bf16[96,2304]{1,0:T(8,128)(2,1)S(1)}, u32[]{:S(2)}, u32[]{:S(2)}) collective-permute-start(bf16[96,2304]{1,0:T(8,128)(2,1)S(1)} %chunk_step.88), channel_id=1, source_target_pairs={{0,8},{4,12},{8,0},{12,4},{16,24},{20,28},{24,16},{28,20},{1,9},{5... | collective-permute-start | bytes 1327112 | tf_op jit(solution)/shard_map/ppermute | solution.py:611
  298.9 16.8 %collective-permute-start.47 = (bf16[96,2304]{1,0:T(8,128)(2,1)S(1)}, bf16[96,2304]{1,0:T(8,128)(2,1)S(1)}, u32[]{:S(2)}, u32[]{:S(2)}) collective-permute-start(bf16[96,2304]{1,0:T(8,128)(2,1)S(1)} %chunk_step.91), channel_id=1, source_target_pairs={{0,8},{4,12},{8,0},{12,4},{16,24},{20,28},{24,16},{28,20},{1,9},{5... | collective-permute-start | bytes 1327112 | tf_op jit(solution)/shard_map/ppermute | solution.py:611
  308.4 16.7 %collective-permute-start.53 = (bf16[96,2304]{1,0:T(8,128)(2,1)S(1)}, bf16[96,2304]{1,0:T(8,128)(2,1)S(1)}, u32[]{:S(2)}, u32[]{:S(2)}) collective-permute-start(bf16[96,2304]{1,0:T(8,128)(2,1)S(1)} %chunk_step.94), channel_id=1, source_target_pairs={{0,8},{4,12},{8,0},{12,4},{16,24},{20,28},{24,16},{28,20},{1,9},{5... | collective-permute-start | bytes 1327112 | tf_op jit(solution)/shard_map/ppermute | solution.py:611
  317.9 16.8 %collective-permute-start.57 = (bf16[96,2304]{1,0:T(8,128)(2,1)S(1)}, bf16[96,2304]{1,0:T(8,128)(2,1)S(1)}, u32[]{:S(2)}, u32[]{:S(2)}) collective-permute-start(bf16[96,2304]{1,0:T(8,128)(2,1)S(1)} %chunk_step.97), channel_id=1, source_target_pairs={{0,8},{4,12},{8,0},{12,4},{16,24},{20,28},{24,16},{28,20},{1,9},{5... | collective-permute-start | bytes 1327112 | tf_op jit(solution)/shard_map/ppermute | solution.py:611
  327.4 16.8 %collective-permute-start.62 = (bf16[96,2304]{1,0:T(8,128)(2,1)S(1)}, bf16[96,2304]{1,0:T(8,128)(2,1)S(1)}, u32[]{:S(2)}, u32[]{:S(2)}) collective-permute-start(bf16[96,2304]{1,0:T(8,128)(2,1)S(1)} %chunk_step.100), channel_id=1, source_target_pairs={{0,8},{4,12},{8,0},{12,4},{16,24},{20,28},{24,16},{28,20},{1,9},{5... | collective-permute-start | bytes 1327112 | tf_op jit(solution)/shard_map/ppermute | solution.py:611
  336.9 16.7 %collective-permute-start.59 = (bf16[96,2304]{1,0:T(8,128)(2,1)S(1)}, bf16[96,2304]{1,0:T(8,128)(2,1)S(1)}, u32[]{:S(2)}, u32[]{:S(2)}) collective-permute-start(bf16[96,2304]{1,0:T(8,128)(2,1)S(1)} %chunk_step.103), channel_id=1, source_target_pairs={{0,8},{4,12},{8,0},{12,4},{16,24},{20,28},{24,16},{28,20},{1,9},{5... | collective-permute-start | bytes 1327112 | tf_op jit(solution)/shard_map/ppermute | solution.py:611
  346.3 16.7 %collective-permute-start.64 = (bf16[96,2304]{1,0:T(8,128)(2,1)S(1)}, bf16[96,2304]{1,0:T(8,128)(2,1)S(1)}, u32[]{:S(2)}, u32[]{:S(2)}) collective-permute-start(bf16[96,2304]{1,0:T(8,128)(2,1)S(1)} %chunk_step.106), channel_id=1, source_target_pairs={{0,8},{4,12},{8,0},{12,4},{16,24},{20,28},{24,16},{28,20},{1,9},{5... | collective-permute-start | bytes 1327112 | tf_op jit(solution)/shard_map/ppermute | solution.py:611
  355.7 16.9 %collective-permute-start.67 = (bf16[96,2304]{1,0:T(8,128)(2,1)S(1)}, bf16[96,2304]{1,0:T(8,128)(2,1)S(1)}, u32[]{:S(2)}, u32[]{:S(2)}) collective-permute-start(bf16[96,2304]{1,0:T(8,128)(2,1)S(1)} %chunk_step.105.refs_1_), channel_id=1, source_target_pairs={{0,8},{4,12},{8,0},{12,4},{16,24},{20,28},{24,16},{28,20},{1,9},{5... | collective-permute-start | bytes 1327112 | tf_op jit(solution)/shard_map/ppermute | solution.py:611
  365.5 16.6 %collective-permute-start.73 = (bf16[96,2304]{1,0:T(8,128)(2,1)S(1)}, bf16[96,2304]{1,0:T(8,128)(2,1)}, u32[]{:S(2)}, u32[]{:S(2)}) collective-permute-start(bf16[96,2304]{1,0:T(8,128)(2,1)S(1)} %chunk_step.108.refs_1_), channel_id=1, source_target_pairs={{0,8},{4,12},{8,0},{12,4},{16,24},{20,28},{24,16},{28,20},{1,9},{5... | collective-permute-start | bytes 1327112 | tf_op jit(solution)/shard_map/ppermute | solution.py:611
  400.0 17.0 %collective-permute-start.78 = (bf16[96,2304]{1,0:T(8,128)(2,1)S(1)}, bf16[96,2304]{1,0:T(8,128)(2,1)S(1)}, u32[]{:S(2)}, u32[]{:S(2)}) collective-permute-start(bf16[96,2304]{1,0:T(8,128)(2,1)S(1)} %chunk_step.115.refs_2_), channel_id=1, source_target_pairs={{0,4},{4,0},{8,12},{12,8},{16,20},{20,16},{24,28},{28,24},{1,5},{5... | collective-permute-start | bytes 1327112 | tf_op jit(solution)/shard_map/ppermute | solution.py:615
  (106 other events, 1048.5 us)

commit v6 on v5

--- a/solution.py
+++ b/solution.py
@@ -864,6 +864,7 @@
         fill_bias(0)()
         fill_bias(0)()
         fill_bias(0)()
+        send("sums", sums_pair)
         send("hidden", hidden_pair)
         fill_back(1, 1)
         fill_back(1, 0)
@@ -877,6 +878,7 @@
         fill_core(0, 1)
         chunks = products()
         fill_core(0, 0)
+        receive("sums")
         receive("hidden")
         fill_bias(3)()
         fillers = {
@@ -884,10 +886,8 @@
             1: fill((fill_send,)),
             3: fill((receive, ("cross", 0))),
             4: fill((receive, "pair")),
-            CHUNKS: fill((send, "sums", sums_pair)),
             CHUNKS + 2: fill((fill_hidden,)),
             CHUNKS + 3: fill((fill_input,)),
-            CHUNKS + 4: fill((receive, "sums")),
         }
         piped_sums(done, chunks, pairs, fillers, arrived)
         input_grad, hidden = kept["input"], kept["hidden out"]

time: 429 us -> 428 us (level)
    ppermute x2, waiting for transfers between devices: 10.7 us -> 0.01 us  [send(): kept[name] = lax.ppermute(done(value), 'dp', pairs)]
    ppermute x18, waiting for transfers between devices: 2.62 us -> 11 us  [piped_sums(): got_pair[k] = lax.ppermute(final, 'dp', pairs)]
    unnamed x117 -> x109, local copies, waits for them, and re-layouts: 20.2 us -> 19.5 us
where the time goes in v6:
time: 428 us; the launch traced here: 423 us
  Pallas kernels  132 us (31%)
  starting transfers between devices  125 us (29%)
  waiting for transfers between devices  92.3 us (22%)
  matrix products  31.5 us (7%)
  local copies, waits for them, and re-layouts  27.6 us (6%)
  other arithmetic  10.3 us (2%)
    ppermute x21, starting transfers between devices, piped_sums(): got_edge[n + 1] = lax.ppermute(payload, 'dp', edge)  65.6 us
    ppermute x21, waiting for transfers between devices, piped_sums(): got_edge[n + 1] = lax.ppermute(payload, 'dp', edge)  63.5 us
    pallas_call x2, Pallas kernels, gates_pool(): pl.pallas_call(functools.partial(gates_pool_kernel, 1 + len(before)), gri...  41.2 us
    pallas_call x4, Pallas kernels, back_products(): pl.pallas_call(back_kernel, grid_spec=pltpu.PrefetchScalarGridSpec(num_sc...  32.7 us
    dot_general x1, matrix products, cols_dot(): lax.dot_general(left, right, (((1,), (1,)), ((), ())), preferred_element_...  23.6 us
    pallas_call x2, Pallas kernels, gates_step(): pl.pallas_call(functools.partial(gates_kernel, 0 if held is None else 1),...  22.8 us
    ppermute x18, starting transfers between devices, piped_sums(): got_pair[k] = lax.ppermute(final, 'dp', pairs)  22.5 us
    pallas_call x6, Pallas kernels, write_chunks(): pl.pallas_call(functools.partial(write_kernel, count), grid=(2,), in_spec...  20.2 us
  transfers between devices with their start and end apart: 80, of which 26 were waited for; matrix products, arithmetic and copies ran while one was open for 10% of the time, Pallas kernels for 24%

profile of v6, /device:TPU:0, one launch (start us, length us, event | category | flops | bytes accessed | tf_op | source)
XLA Modules:
  0.0 422.7 jit_solution(7243512911088959117)
XLA Ops:
  2.0 3.8 convolution_convert_fusion.2.low_ref
  11.9 4.1 convolution_convert_fusion.1
  19.5 11.8 %gates_step.2 = (f32[2,3,288,1152]{3,2,1,0:T(8,128)}, bf16[2304,2304]{1,0:T(8,128)(2,1)}, bf16[2,3,288,1152]{3,2,1,0:T(8,128)(2,1)}) custom-call(s32[3]{0:T(128)S(1)} %add_add_fusion.1.pick_ref, bf16[576,1152]{1,0:T(8,128)(2,1)} %convolution_convert_fusion.2.low_ref, bf16[576,1152]{1,0:T(8,128)(2,1)S(1)} %copy-done.21, bf16[2,3,576,2304]{3,2,1,0:T(8,128)(2,1)} %bitcast.34), custom_call_target="tpu_custom_call" | custom-call | flops 1 | bytes 1 | tf_op jit(solution)/shard_map/gates_step/pallas_call | solution.py:254
  31.3 7.6 %collective-permute-done.low_ref = bf16[576,1152]{1,0:T(8,128)(2,1)} collective-permute-done((bf16[576,1152]{1,0:T(8,128)(2,1)}, bf16[576,1152]{1,0:T(8,128)(2,1)}, u32[]{:S(2)}, u32[]{:S(2)}) %collective-permute-start) | collective-permute-done | bytes 1327136 | tf_op jit(solution)/shard_map/ppermute | solution.py:662
  45.3 21.0 %gates_pool.2 = (bf16[288,1152]{1,0:T(8,128)(2,1)S(1)}, f32[288,128]{1,0:T(8,128)S(1)}, bf16[2,3,288,2304]{3,2,1,0:T(8,128)(2,1)}, bf16[2304,2304]{1,0:T(8,128)(2,1)}, bf16[2,3,288,1152]{3,2,1,0:T(8,128)(2,1)}) custom-call(s32[3]{0:T(128)S(1)} %add_add_fusion.pick_ref, s32[1]{0:T(128)S(6)} %copy.41.length_ref, ...), custom_call_target="tpu_custom_call", output_to_operand_aliasing={{3}: (8, {})} | custom-call | flops 1 | bytes 1 | tf_op jit(solution)/shard_map/gates_pool/pallas_call | solution.py:319
  74.0 11.0 %gates_step.3 = (f32[2,3,288,1152]{3,2,1,0:T(8,128)}, bf16[2304,2304]{1,0:T(8,128)(2,1)}) custom-call(s32[3]{0:T(128)S(1)} %add_add_fusion.1.pick_ref, bf16[576,1152]{1,0:T(8,128)(2,1)S(1)} %collective-permute-done.3.low_ref, bf16[576,1152]{1,0:T(8,128)(2,1)S(1)} %collective-permute-done.7.high_ref, ...), custom_call_target="tpu_custom_call", output_to_operand_aliasing={{1}: (4, {})} | custom-call | flops 1 | bytes 1 | tf_op jit(solution)/shard_map/gates_step/pallas_call | solution.py:254
  87.4 20.2 %gates_pool.3 = (bf16[288,1152]{1,0:T(8,128)(2,1)S(1)}, f32[288,128]{1,0:T(8,128)S(1)}, bf16[2,3,288,2304]{3,2,1,0:T(8,128)(2,1)}, bf16[2304,2304]{1,0:T(8,128)(2,1)}) custom-call(s32[3]{0:T(128)S(1)} %add_add_fusion.pick_ref, s32[1]{0:T(128)} %bitcast.7.length_ref, ...), custom_call_target="tpu_custom_call", output_to_operand_aliasing={{3}: (8, {}), {2}: (9, {})} | custom-call | flops 1 | bytes 1 | tf_op jit(solution)/shard_map/gates_pool/pallas_call | solution.py:319
  110.9 7.6 %back_products.4 = (f32[576,1152]{1,0:T(8,128)S(1)}, bf16[576,1152]{1,0:T(8,128)(2,1)S(1)}) custom-call(s32[3]{0:T(128)S(1)} %add_add_fusion.1.pick_ref, bf16[1728,1152]{1,0:T(8,128)(2,1)S(1)} %bitcast.31, bf16[1728,2304]{1,0:T(8,128)(2,1)S(1)} %bitcast.25), custom_call_target="tpu_custom_call" | custom-call | flops 1 | bytes 1 | tf_op jit(solution)/shard_map/back_products/pallas_call | solution.py:394
  120.2 8.6 %back_products.5 = (f32[576,1152]{1,0:T(8,128)S(1)}, bf16[576,1152]{1,0:T(8,128)(2,1)}) custom-call(s32[3]{0:T(128)S(1)} %add_add_fusion.1.pick_ref, bf16[1728,1152]{1,0:T(8,128)(2,1)S(1)} %bitcast.29, bf16[1728,2304]{1,0:T(8,128)(2,1)S(1)} %bitcast.26), custom_call_target="tpu_custom_call" | custom-call | flops 1 | bytes 1 | tf_op jit(solution)/shard_map/back_products/pallas_call | solution.py:394
  131.2 8.6 %back_products.6 = (f32[576,1152]{1,0:T(8,128)S(1)}, bf16[576,1152]{1,0:T(8,128)(2,1)}) custom-call(s32[3]{0:T(128)S(1)} %add_add_fusion.1.pick_ref, bf16[1728,1152]{1,0:T(8,128)(2,1)S(1)} %bitcast.32, bf16[1728,2304]{1,0:T(8,128)(2,1)S(1)} %bitcast.27), custom_call_target="tpu_custom_call" | custom-call | flops 1 | bytes 1 | tf_op jit(solution)/shard_map/back_products/pallas_call | solution.py:394
  149.6 7.8 %back_products.7 = (f32[576,1152]{1,0:T(8,128)S(1)}, bf16[576,1152]{1,0:T(8,128)(2,1)S(1)}) custom-call(s32[3]{0:T(128)S(1)} %add_add_fusion.1.pick_ref, bf16[1728,1152]{1,0:T(8,128)(2,1)S(1)} %bitcast.30, bf16[1728,2304]{1,0:T(8,128)(2,1)S(1)} %bitcast.28), custom_call_target="tpu_custom_call" | custom-call | flops 1 | bytes 1 | tf_op jit(solution)/shard_map/back_products/pallas_call | solution.py:394
  160.0 4.4 %collective-permute-start.17 = (f32[288,128]{1,0:T(8,128)S(1)}, f32[288,128]{1,0:T(8,128)S(1)}, u32[]{:S(2)}, u32[]{:S(2)}) collective-permute-start(f32[288,128]{1,0:T(8,128)S(1)} %add.64), channel_id=1, source_target_pairs={{8,0},{12,4},{16,24},{20,28},{0,8},{4,12},{24,16},{28,20},{9,1},{1... | collective-permute-start | bytes 442376 | tf_op jit(solution)/shard_map/ppermute | solution.py:835
  166.0 23.6 %convolution_convert_fusion.refs_0_ = bf16[1728,2304]{1,0:T(8,128)(2,1)S(1)} fusion(bf16[1728,2304]{1,0:T(8,128)(2,1)} %bitcast.24, bf16[2304,2304]{1,0:T(8,128)(2,1)} %get-tuple-element.807), kind=kOutput, calls=%fused_computation | convolution fusion | flops 18349867008 | bytes 26542080 | tf_op jit(solution)/shard_map/dot_general | solution.py:204
  197.4 7.0 %collective-permute-done.18.refs_1_ = bf16[96,2304]{1,0:T(8,128)(2,1)S(1)} collective-permute-done((bf16[96,2304]{1,0:T(8,128)(2,1)S(1)}, bf16[96,2304]{1,0:T(8,128)(2,1)S(1)}, u32[]{:S(2)}, u32[]{:S(2)}) %collective-permute-start.18) | collective-permute-done | bytes 442400 | tf_op jit(solution)/shard_map/ppermute | solution.py:584
  208.1 5.9 %collective-permute-done.22.refs_1_ = bf16[96,2304]{1,0:T(8,128)(2,1)S(1)} collective-permute-done((bf16[96,2304]{1,0:T(8,128)(2,1)S(1)}, bf16[96,2304]{1,0:T(8,128)(2,1)S(1)}, u32[]{:S(2)}, u32[]{:S(2)}) %collective-permute-start.22) | collective-permute-done | bytes 442400 | tf_op jit(solution)/shard_map/ppermute | solution.py:611
  214.9 4.8 %collective-permute-start.28 = (bf16[96,2304]{1,0:T(8,128)(2,1)S(1)}, bf16[96,2304]{1,0:T(8,128)(2,1)S(1)}, u32[]{:S(2)}, u32[]{:S(2)}) collective-permute-start(bf16[96,2304]{1,0:T(8,128)(2,1)S(1)} %chunk_step.64), channel_id=1, source_target_pairs={{0,8},{4,12},{8,0},{12,4},{16,24},{20,28},{24,16},{28,20},{1,9},{5... | collective-permute-start | bytes 1327112 | tf_op jit(solution)/shard_map/ppermute | solution.py:611
  219.7 3.7 collective-permute-done.24.refs_1_
  224.4 4.8 %collective-permute-start.25 = (bf16[96,2304]{1,0:T(8,128)(2,1)S(1)}, bf16[96,2304]{1,0:T(8,128)(2,1)S(1)}, u32[]{:S(2)}, u32[]{:S(2)}) collective-permute-start(bf16[96,2304]{1,0:T(8,128)(2,1)S(1)} %chunk_step.67), channel_id=1, source_target_pairs={{0,8},{4,12},{8,0},{12,4},{16,24},{20,28},{24,16},{28,20},{1,9},{5... | collective-permute-start | bytes 1327112 | tf_op jit(solution)/shard_map/ppermute | solution.py:611
  233.9 4.8 %collective-permute-start.31 = (bf16[96,2304]{1,0:T(8,128)(2,1)S(1)}, bf16[96,2304]{1,0:T(8,128)(2,1)S(1)}, u32[]{:S(2)}, u32[]{:S(2)}) collective-permute-start(bf16[96,2304]{1,0:T(8,128)(2,1)S(1)} %chunk_step.70), channel_id=1, source_target_pairs={{0,8},{4,12},{8,0},{12,4},{16,24},{20,28},{24,16},{28,20},{1,9},{5... | collective-permute-start | bytes 1327112 | tf_op jit(solution)/shard_map/ppermute | solution.py:611
  248.1 3.8 collective-permute-done.31.refs_1_
  257.6 3.7 collective-permute-done.34.refs_1_
  267.1 3.7 collective-permute-done.40.refs_1_
  286.0 3.7 collective-permute-done.42.refs_1_
  295.5 3.7 collective-permute-done.46.refs_1_
  314.5 3.7 collective-permute-done.48.refs_1_
  323.9 3.7 collective-permute-done.54.refs_1_
  342.9 3.7 collective-permute-done.63.refs_1_
  352.4 3.7 collective-permute-done.60.refs_1_
  371.0 4.1 collective-permute-done.68.refs_0_
  379.9 4.7 %collective-permute-done.74.refs_0_ = bf16[96,2304]{1,0:T(8,128)(2,1)} collective-permute-done((bf16[96,2304]{1,0:T(8,128)(2,1)S(1)}, bf16[96,2304]{1,0:T(8,128)(2,1)}, u32[]{:S(2)}, u32[]{:S(2)}) %collective-permute-start.74) | collective-permute-done | bytes 442400 | tf_op jit(solution)/shard_map/ppermute | solution.py:611
  387.0 3.9 write_chunks.10.refs_6_
  408.2 7.5 %collective-permute-done.79.refs_5_ = bf16[96,2304]{1,0:T(8,128)(2,1)S(1)} collective-permute-done((bf16[96,2304]{1,0:T(8,128)(2,1)S(1)}, bf16[96,2304]{1,0:T(8,128)(2,1)S(1)}, u32[]{:S(2)}, u32[]{:S(2)}) %collective-permute-start.79) | collective-permute-done | bytes 442400 | tf_op jit(solution)/shard_map/ppermute | solution.py:615
  (352 shorter events, 194.2 us)
Async XLA Ops:
  6.3 32.6 %collective-permute-start = (bf16[576,1152]{1,0:T(8,128)(2,1)}, bf16[576,1152]{1,0:T(8,128)(2,1)}, u32[]{:S(2)}, u32[]{:S(2)}) collective-permute-start(bf16[576,1152]{1,0:T(8,128)(2,1)} %convolution_convert_fusion.2.low_ref), channel_id=1, source_target_pairs={{0,2},{1,3},{2,0},{3,1},{4,6},{5,7},{6,4},{7,5},{8,10},{9,11},{10,... | collective-permute-start | bytes 3981320 | tf_op jit(solution)/shard_map/ppermute | solution.py:662
  8.8 34.0 %collective-permute-start.3 = (bf16[576,1152]{1,0:T(8,128)(2,1)}, bf16[576,1152]{1,0:T(8,128)(2,1)S(1)}, u32[]{:S(2)}, u32[]{:S(2)}) collective-permute-start(bf16[576,1152]{1,0:T(8,128)(2,1)} %convolution_convert_fusion.2.low_ref), channel_id=1, source_target_pairs={{0,4},{4,0},{8,12},{12,8},{16,20},{20,16},{24,28},{28,24},{1,5},{5... | collective-permute-start | bytes 3981320 | tf_op jit(solution)/shard_map/ppermute | solution.py:663
  41.0 27.1 %collective-permute-start.5 = (bf16[480,1152]{1,0:T(8,128)(2,1)}, bf16[480,1152]{1,0:T(8,128)(2,1)}, u32[]{:S(2)}, u32[]{:S(2)}) collective-permute-start(bf16[480,1152]{1,0:T(8,128)(2,1)} %pad_maximum_fusion.1), channel_id=1, source_target_pairs={{0,4},{4,0},{8,12},{12,8},{16,20},{20,16},{24,28},{28,24},{1,5},{5... | collective-permute-start | bytes 3317768 | tf_op jit(solution)/shard_map/ppermute | solution.py:677
  43.8 22.6 %collective-permute-start.4 = (bf16[384,1152]{1,0:T(8,128)(2,1)}, bf16[384,1152]{1,0:T(8,128)(2,1)}, u32[]{:S(2)}, u32[]{:S(2)}) collective-permute-start(bf16[384,1152]{1,0:T(8,128)(2,1)} %slice.27), channel_id=1, source_target_pairs={{0,2},{1,3},{2,0},{3,1},{4,6},{5,7},{6,4},{7,5},{8,10},{9,11},{10,... | collective-permute-start | bytes 2654216 | tf_op jit(solution)/shard_map/ppermute | solution.py:676
  141.4 18.6 %collective-permute-start.15 = (bf16[576,1152]{1,0:T(8,128)(2,1)}, bf16[576,1152]{1,0:T(8,128)(2,1)}, u32[]{:S(2)}, u32[]{:S(2)}) collective-permute-start(bf16[576,1152]{1,0:T(8,128)(2,1)} %get-tuple-element.795), channel_id=1, source_target_pairs={{0,1},{1,0},{2,3},{3,2},{4,5},{5,4},{6,7},{7,6},{8,9},{9,8},{10,11... | collective-permute-start | bytes 3981320 | tf_op jit(solution)/shard_map/ppermute | solution.py:723
  142.2 47.6 %collective-permute-start.10 = (f32[288,128]{1,0:T(8,128)S(1)}, f32[288,128]{1,0:T(8,128)}, u32[]{:S(2)}, u32[]{:S(2)}) collective-permute-start(f32[288,128]{1,0:T(8,128)S(1)} %get-tuple-element.742), channel_id=1, source_target_pairs={{0,4},{4,0},{8,12},{12,8},{16,20},{20,16},{24,28},{28,24},{1,5},{5... | collective-permute-start | bytes 442376 | tf_op jit(solution)/shard_map/ppermute | solution.py:785
  143.5 46.4 %collective-permute-start.9 = (bf16[288,1152]{1,0:T(8,128)(2,1)S(1)}, bf16[288,1152]{1,0:T(8,128)(2,1)}, u32[]{:S(2)}, u32[]{:S(2)}) collective-permute-start(bf16[288,1152]{1,0:T(8,128)(2,1)S(1)} %get-tuple-element.741), channel_id=1, source_target_pairs={{0,4},{4,0},{8,12},{12,8},{16,20},{20,16},{24,28},{28,24},{1,5},{5... | collective-permute-start | bytes 1990664 | tf_op jit(solution)/shard_map/ppermute | solution.py:785
  157.4 32.2 %collective-permute-start.14 = (bf16[576,1152]{1,0:T(8,128)(2,1)S(1)}, bf16[576,1152]{1,0:T(8,128)(2,1)S(1)}, u32[]{:S(2)}, u32[]{:S(2)}) collective-permute-start(bf16[576,1152]{1,0:T(8,128)(2,1)S(1)} %get-tuple-element.792), channel_id=1, source_target_pairs={{0,1},{1,0},{2,3},{3,2},{4,5},{5,4},{6,7},{7,6},{8,9},{9,8},{10,11... | collective-permute-start | bytes 3981320 | tf_op jit(solution)/shard_map/ppermute | solution.py:723
  157.5 33.9 %collective-permute-start.20 = (bf16[576,1152]{1,0:T(8,128)(2,1)S(1)}, bf16[576,1152]{1,0:T(8,128)(2,1)S(1)}, u32[]{:S(2)}, u32[]{:S(2)}) collective-permute-start(bf16[576,1152]{1,0:T(8,128)(2,1)S(1)} %copy-done.19), channel_id=1, source_target_pairs={{0,2},{1,3},{2,0},{3,1},{4,6},{5,7},{6,4},{7,5},{8,10},{9,11},{10,... | collective-permute-start | bytes 3981320 | tf_op jit(solution)/shard_map/ppermute | solution.py:734
  160.0 29.9 %collective-permute-start.17 = (f32[288,128]{1,0:T(8,128)S(1)}, f32[288,128]{1,0:T(8,128)S(1)}, u32[]{:S(2)}, u32[]{:S(2)}) collective-permute-start(f32[288,128]{1,0:T(8,128)S(1)} %add.64), channel_id=1, source_target_pairs={{8,0},{12,4},{16,24},{20,28},{0,8},{4,12},{24,16},{28,20},{9,1},{1... | collective-permute-start | bytes 442376 | tf_op jit(solution)/shard_map/ppermute | solution.py:835
  191.5 37.7 %collective-permute-start.29 = (bf16[576,1152]{1,0:T(8,128)(2,1)S(1)}, bf16[576,1152]{1,0:T(8,128)(2,1)S(1)}, u32[]{:S(2)}, u32[]{:S(2)}) collective-permute-start(bf16[576,1152]{1,0:T(8,128)(2,1)S(1)} %whole.9), channel_id=1, source_target_pairs={{0,2},{1,3},{2,0},{3,1},{4,6},{5,7},{6,4},{7,5},{8,10},{9,11},{10,... | collective-permute-start | bytes 3981320 | tf_op jit(solution)/shard_map/ppermute | solution.py:734
  193.3 20.7 %collective-permute-start.22 = (bf16[96,2304]{1,0:T(8,128)(2,1)S(1)}, bf16[96,2304]{1,0:T(8,128)(2,1)S(1)}, u32[]{:S(2)}, u32[]{:S(2)}) collective-permute-start(bf16[96,2304]{1,0:T(8,128)(2,1)S(1)} %chunk_step.59), channel_id=1, source_target_pairs={{0,8},{4,12},{8,0},{12,4},{16,24},{20,28},{24,16},{28,20},{1,9},{5... | collective-permute-start | bytes 1327112 | tf_op jit(solution)/shard_map/ppermute | solution.py:611
  204.8 33.8 %collective-permute-start.26 = (bf16[576,1152]{1,0:T(8,128)(2,1)S(1)}, bf16[576,1152]{1,0:T(8,128)(2,1)S(1)}, u32[]{:S(2)}, u32[]{:S(2)}) collective-permute-start(bf16[576,1152]{1,0:T(8,128)(2,1)S(1)} %whole.11), channel_id=1, source_target_pairs={{0,4},{4,0},{8,12},{12,8},{16,20},{20,16},{24,28},{28,24},{1,5},{5... | collective-permute-start | bytes 3981320 | tf_op jit(solution)/shard_map/ppermute | solution.py:775
  206.8 16.6 %collective-permute-start.24 = (bf16[96,2304]{1,0:T(8,128)(2,1)S(1)}, bf16[96,2304]{1,0:T(8,128)(2,1)S(1)}, u32[]{:S(2)}, u32[]{:S(2)}) collective-permute-start(bf16[96,2304]{1,0:T(8,128)(2,1)S(1)} %chunk_step.61), channel_id=1, source_target_pairs={{0,8},{4,12},{8,0},{12,4},{16,24},{20,28},{24,16},{28,20},{1,9},{5... | collective-permute-start | bytes 1327112 | tf_op jit(solution)/shard_map/ppermute | solution.py:611
  214.9 18.0 %collective-permute-start.28 = (bf16[96,2304]{1,0:T(8,128)(2,1)S(1)}, bf16[96,2304]{1,0:T(8,128)(2,1)S(1)}, u32[]{:S(2)}, u32[]{:S(2)}) collective-permute-start(bf16[96,2304]{1,0:T(8,128)(2,1)S(1)} %chunk_step.64), channel_id=1, source_target_pairs={{0,8},{4,12},{8,0},{12,4},{16,24},{20,28},{24,16},{28,20},{1,9},{5... | collective-permute-start | bytes 1327112 | tf_op jit(solution)/shard_map/ppermute | solution.py:611
  224.4 18.0 %collective-permute-start.25 = (bf16[96,2304]{1,0:T(8,128)(2,1)S(1)}, bf16[96,2304]{1,0:T(8,128)(2,1)S(1)}, u32[]{:S(2)}, u32[]{:S(2)}) collective-permute-start(bf16[96,2304]{1,0:T(8,128)(2,1)S(1)} %chunk_step.67), channel_id=1, source_target_pairs={{0,8},{4,12},{8,0},{12,4},{16,24},{20,28},{24,16},{28,20},{1,9},{5... | collective-permute-start | bytes 1327112 | tf_op jit(solution)/shard_map/ppermute | solution.py:611
  233.9 18.0 %collective-permute-start.31 = (bf16[96,2304]{1,0:T(8,128)(2,1)S(1)}, bf16[96,2304]{1,0:T(8,128)(2,1)S(1)}, u32[]{:S(2)}, u32[]{:S(2)}) collective-permute-start(bf16[96,2304]{1,0:T(8,128)(2,1)S(1)} %chunk_step.70), channel_id=1, source_target_pairs={{0,8},{4,12},{8,0},{12,4},{16,24},{20,28},{24,16},{28,20},{1,9},{5... | collective-permute-start | bytes 1327112 | tf_op jit(solution)/shard_map/ppermute | solution.py:611
  244.7 16.6 %collective-permute-start.34 = (bf16[96,2304]{1,0:T(8,128)(2,1)S(1)}, bf16[96,2304]{1,0:T(8,128)(2,1)S(1)}, u32[]{:S(2)}, u32[]{:S(2)}) collective-permute-start(bf16[96,2304]{1,0:T(8,128)(2,1)S(1)} %chunk_step.73), channel_id=1, source_target_pairs={{0,8},{4,12},{8,0},{12,4},{16,24},{20,28},{24,16},{28,20},{1,9},{5... | collective-permute-start | bytes 1327112 | tf_op jit(solution)/shard_map/ppermute | solution.py:611
  254.1 16.7 %collective-permute-start.40 = (bf16[96,2304]{1,0:T(8,128)(2,1)S(1)}, bf16[96,2304]{1,0:T(8,128)(2,1)S(1)}, u32[]{:S(2)}, u32[]{:S(2)}) collective-permute-start(bf16[96,2304]{1,0:T(8,128)(2,1)S(1)} %chunk_step.76), channel_id=1, source_target_pairs={{0,8},{4,12},{8,0},{12,4},{16,24},{20,28},{24,16},{28,20},{1,9},{5... | collective-permute-start | bytes 1327112 | tf_op jit(solution)/shard_map/ppermute | solution.py:611
  264.0 16.3 %collective-permute-start.36 = (bf16[96,2304]{1,0:T(8,128)(2,1)S(1)}, bf16[96,2304]{1,0:T(8,128)(2,1)S(1)}, u32[]{:S(2)}, u32[]{:S(2)}) collective-permute-start(bf16[96,2304]{1,0:T(8,128)(2,1)S(1)} %chunk_step.79), channel_id=1, source_target_pairs={{0,8},{4,12},{8,0},{12,4},{16,24},{20,28},{24,16},{28,20},{1,9},{5... | collective-permute-start | bytes 1327112 | tf_op jit(solution)/shard_map/ppermute | solution.py:611
  273.1 16.7 %collective-permute-start.42 = (bf16[96,2304]{1,0:T(8,128)(2,1)S(1)}, bf16[96,2304]{1,0:T(8,128)(2,1)S(1)}, u32[]{:S(2)}, u32[]{:S(2)}) collective-permute-start(bf16[96,2304]{1,0:T(8,128)(2,1)S(1)} %chunk_step.82), channel_id=1, source_target_pairs={{0,8},{4,12},{8,0},{12,4},{16,24},{20,28},{24,16},{28,20},{1,9},{5... | collective-permute-start | bytes 1327112 | tf_op jit(solution)/shard_map/ppermute | solution.py:611
  282.6 16.7 %collective-permute-start.46 = (bf16[96,2304]{1,0:T(8,128)(2,1)S(1)}, bf16[96,2304]{1,0:T(8,128)(2,1)S(1)}, u32[]{:S(2)}, u32[]{:S(2)}) collective-permute-start(bf16[96,2304]{1,0:T(8,128)(2,1)S(1)} %chunk_step.85), channel_id=1, source_target_pairs={{0,8},{4,12},{8,0},{12,4},{16,24},{20,28},{24,16},{28,20},{1,9},{5... | collective-permute-start | bytes 1327112 | tf_op jit(solution)/shard_map/ppermute | solution.py:611
  292.0 16.7 %collective-permute-start.51 = (bf16[96,2304]{1,0:T(8,128)(2,1)S(1)}, bf16[96,2304]{1,0:T(8,128)(2,1)S(1)}, u32[]{:S(2)}, u32[]{:S(2)}) collective-permute-start(bf16[96,2304]{1,0:T(8,128)(2,1)S(1)} %chunk_step.88), channel_id=1, source_target_pairs={{0,8},{4,12},{8,0},{12,4},{16,24},{20,28},{24,16},{28,20},{1,9},{5... | collective-permute-start | bytes 1327112 | tf_op jit(solution)/shard_map/ppermute | solution.py:611
  301.5 16.7 %collective-permute-start.48 = (bf16[96,2304]{1,0:T(8,128)(2,1)S(1)}, bf16[96,2304]{1,0:T(8,128)(2,1)S(1)}, u32[]{:S(2)}, u32[]{:S(2)}) collective-permute-start(bf16[96,2304]{1,0:T(8,128)(2,1)S(1)} %chunk_step.91), channel_id=1, source_target_pairs={{0,8},{4,12},{8,0},{12,4},{16,24},{20,28},{24,16},{28,20},{1,9},{5... | collective-permute-start | bytes 1327112 | tf_op jit(solution)/shard_map/ppermute | solution.py:611
  311.0 16.6 %collective-permute-start.54 = (bf16[96,2304]{1,0:T(8,128)(2,1)S(1)}, bf16[96,2304]{1,0:T(8,128)(2,1)S(1)}, u32[]{:S(2)}, u32[]{:S(2)}) collective-permute-start(bf16[96,2304]{1,0:T(8,128)(2,1)S(1)} %chunk_step.94), channel_id=1, source_target_pairs={{0,8},{4,12},{8,0},{12,4},{16,24},{20,28},{24,16},{28,20},{1,9},{5... | collective-permute-start | bytes 1327112 | tf_op jit(solution)/shard_map/ppermute | solution.py:611
  320.5 16.7 %collective-permute-start.58 = (bf16[96,2304]{1,0:T(8,128)(2,1)S(1)}, bf16[96,2304]{1,0:T(8,128)(2,1)S(1)}, u32[]{:S(2)}, u32[]{:S(2)}) collective-permute-start(bf16[96,2304]{1,0:T(8,128)(2,1)S(1)} %chunk_step.97), channel_id=1, source_target_pairs={{0,8},{4,12},{8,0},{12,4},{16,24},{20,28},{24,16},{28,20},{1,9},{5... | collective-permute-start | bytes 1327112 | tf_op jit(solution)/shard_map/ppermute | solution.py:611
  330.0 16.7 %collective-permute-start.63 = (bf16[96,2304]{1,0:T(8,128)(2,1)S(1)}, bf16[96,2304]{1,0:T(8,128)(2,1)S(1)}, u32[]{:S(2)}, u32[]{:S(2)}) collective-permute-start(bf16[96,2304]{1,0:T(8,128)(2,1)S(1)} %chunk_step.100), channel_id=1, source_target_pairs={{0,8},{4,12},{8,0},{12,4},{16,24},{20,28},{24,16},{28,20},{1,9},{5... | collective-permute-start | bytes 1327112 | tf_op jit(solution)/shard_map/ppermute | solution.py:611
  339.5 16.7 %collective-permute-start.60 = (bf16[96,2304]{1,0:T(8,128)(2,1)S(1)}, bf16[96,2304]{1,0:T(8,128)(2,1)S(1)}, u32[]{:S(2)}, u32[]{:S(2)}) collective-permute-start(bf16[96,2304]{1,0:T(8,128)(2,1)S(1)} %chunk_step.103), channel_id=1, source_target_pairs={{0,8},{4,12},{8,0},{12,4},{16,24},{20,28},{24,16},{28,20},{1,9},{5... | collective-permute-start | bytes 1327112 | tf_op jit(solution)/shard_map/ppermute | solution.py:611
  348.9 16.7 %collective-permute-start.65 = (bf16[96,2304]{1,0:T(8,128)(2,1)S(1)}, bf16[96,2304]{1,0:T(8,128)(2,1)S(1)}, u32[]{:S(2)}, u32[]{:S(2)}) collective-permute-start(bf16[96,2304]{1,0:T(8,128)(2,1)S(1)} %chunk_step.106), channel_id=1, source_target_pairs={{0,8},{4,12},{8,0},{12,4},{16,24},{20,28},{24,16},{28,20},{1,9},{5... | collective-permute-start | bytes 1327112 | tf_op jit(solution)/shard_map/ppermute | solution.py:611
  358.2 16.8 %collective-permute-start.68 = (bf16[96,2304]{1,0:T(8,128)(2,1)S(1)}, bf16[96,2304]{1,0:T(8,128)(2,1)S(1)}, u32[]{:S(2)}, u32[]{:S(2)}) collective-permute-start(bf16[96,2304]{1,0:T(8,128)(2,1)S(1)} %chunk_step.105.refs_1_), channel_id=1, source_target_pairs={{0,8},{4,12},{8,0},{12,4},{16,24},{20,28},{24,16},{28,20},{1,9},{5... | collective-permute-start | bytes 1327112 | tf_op jit(solution)/shard_map/ppermute | solution.py:611
  368.1 16.6 %collective-permute-start.74 = (bf16[96,2304]{1,0:T(8,128)(2,1)S(1)}, bf16[96,2304]{1,0:T(8,128)(2,1)}, u32[]{:S(2)}, u32[]{:S(2)}) collective-permute-start(bf16[96,2304]{1,0:T(8,128)(2,1)S(1)} %chunk_step.108.refs_1_), channel_id=1, source_target_pairs={{0,8},{4,12},{8,0},{12,4},{16,24},{20,28},{24,16},{28,20},{1,9},{5... | collective-permute-start | bytes 1327112 | tf_op jit(solution)/shard_map/ppermute | solution.py:611
  379.8 16.3 %collective-permute-start.75 = (bf16[96,2304]{1,0:T(8,128)(2,1)S(1)}, bf16[96,2304]{1,0:T(8,128)(2,1)S(1)}, u32[]{:S(2)}, u32[]{:S(2)}) collective-permute-start(bf16[96,2304]{1,0:T(8,128)(2,1)S(1)} %chunk_step.110.refs_1_), channel_id=1, source_target_pairs={{0,8},{4,12},{8,0},{12,4},{16,24},{20,28},{24,16},{28,20},{1,9},{5... | collective-permute-start | bytes 1327112 | tf_op jit(solution)/shard_map/ppermute | solution.py:611
  (102 other events, 1026.8 us)

commit v7 on v5

--- a/solution.py
+++ b/solution.py
@@ -412,7 +412,7 @@
             jax.ShapeDtypeStruct((columns // 2, span), jnp.float32),
             jax.ShapeDtypeStruct((columns // 2, span), jnp.bfloat16),
         ],
-        compiler_params=pltpu.CompilerParams(vmem_limit_bytes=26 * 2**20),
+        compiler_params=pltpu.CompilerParams(vmem_limit_bytes=44 * 2**20),
         cost_estimate=HIDDEN_COST,
         name="back_products",
     )(pick, weights, gg)

time: 429 us -> 431 us (level)
  local copies, waits for them, and re-layouts: 28.3 us -> 16.8 us
  Pallas kernels: 132 us -> 143 us
    unnamed x117 -> x107, local copies, waits for them, and re-layouts: 20.2 us -> 9.74 us
    pallas_call x4, Pallas kernels: 32.7 us -> 40.1 us  [back_products(): pl.pallas_call(back_kernel, grid_spec=pltpu.PrefetchScalarGridSpec(num_sc...]
    ppermute x18, waiting for transfers between devices: 2.62 us -> 8.02 us  [piped_sums(): got_pair[k] = lax.ppermute(final, 'dp', pairs)]
  transfers between devices with their start and end apart: 80 -> 80, of which waited for: 26 -> 28; matrix products, arithmetic and copies ran while one was open for 10% -> 9% of each run, Pallas kernels for 24% -> 26%
where the time goes in v7:
time: 431 us; the launch traced here: 425 us
  Pallas kernels  143 us (33%)
  starting transfers between devices  122 us (28%)
  waiting for transfers between devices  100 us (23%)
  matrix products  31.5 us (7%)
  local copies, waits for them, and re-layouts  16.8 us (4%)
  other arithmetic  7.73 us (2%)
    ppermute x21, waiting for transfers between devices, piped_sums(): got_edge[n + 1] = lax.ppermute(payload, 'dp', edge)  62.8 us
    ppermute x21, starting transfers between devices, piped_sums(): got_edge[n + 1] = lax.ppermute(payload, 'dp', edge)  62.7 us
    pallas_call x2, Pallas kernels, gates_pool(): pl.pallas_call(functools.partial(gates_pool_kernel, 1 + len(before)), gri...  41 us
    pallas_call x4, Pallas kernels, back_products(): pl.pallas_call(back_kernel, grid_spec=pltpu.PrefetchScalarGridSpec(num_sc...  40.1 us
    dot_general x1, matrix products, cols_dot(): lax.dot_general(left, right, (((1,), (1,)), ((), ())), preferred_element_...  23.6 us
    pallas_call x2, Pallas kernels, gates_step(): pl.pallas_call(functools.partial(gates_kernel, 0 if held is None else 1),...  22.9 us
    ppermute x18, starting transfers between devices, piped_sums(): got_pair[k] = lax.ppermute(final, 'dp', pairs)  21.4 us
    pallas_call x6, Pallas kernels, write_chunks(): pl.pallas_call(functools.partial(write_kernel, count), grid=(2,), in_spec...  20.9 us
  transfers between devices with their start and end apart: 80, of which 28 were waited for; matrix products, arithmetic and copies ran while one was open for 9% of the time, Pallas kernels for 26%

profile of v7, /device:TPU:0, one launch (start us, length us, event | category | flops | bytes accessed | tf_op | source)
XLA Modules:
  0.0 425.0 jit_solution(16293956494961973790)
XLA Ops:
  11.9 4.1 convolution_convert_fusion.1
  17.1 11.9 %gates_step.2 = (f32[2,3,288,1152]{3,2,1,0:T(8,128)}, bf16[2304,2304]{1,0:T(8,128)(2,1)}, bf16[2,3,288,1152]{3,2,1,0:T(8,128)(2,1)}) custom-call(s32[3]{0:T(128)S(1)} %add_add_fusion.1.pick_ref, bf16[576,1152]{1,0:T(8,128)(2,1)} %convolution_convert_fusion.2.low_ref, bf16[576,1152]{1,0:T(8,128)(2,1)} %collective-permute-done.1.high_ref, ...), custom_call_target="tpu_custom_call" | custom-call | flops 1 | bytes 1 | tf_op jit(solution)/shard_map/gates_step/pallas_call | solution.py:254
  29.0 9.8 %collective-permute-done.low_ref = bf16[576,1152]{1,0:T(8,128)(2,1)S(1)} collective-permute-done((bf16[576,1152]{1,0:T(8,128)(2,1)}, bf16[576,1152]{1,0:T(8,128)(2,1)S(1)}, u32[]{:S(2)}, u32[]{:S(2)}) %collective-permute-start) | collective-permute-done | bytes 1327136 | tf_op jit(solution)/shard_map/ppermute | solution.py:662
  44.2 20.6 %gates_pool.2 = (bf16[288,1152]{1,0:T(8,128)(2,1)S(1)}, f32[288,128]{1,0:T(8,128)S(1)}, bf16[2,3,288,2304]{3,2,1,0:T(8,128)(2,1)}, bf16[2304,2304]{1,0:T(8,128)(2,1)}, bf16[2,3,288,1152]{3,2,1,0:T(8,128)(2,1)}) custom-call(s32[3]{0:T(128)S(1)} %add_add_fusion.pick_ref, s32[1]{0:T(128)S(6)} %copy.41.length_ref, ...), custom_call_target="tpu_custom_call", output_to_operand_aliasing={{3}: (8, {})} | custom-call | flops 1 | bytes 1 | tf_op jit(solution)/shard_map/gates_pool/pallas_call | solution.py:319
  72.9 10.9 %gates_step.3 = (f32[2,3,288,1152]{3,2,1,0:T(8,128)}, bf16[2304,2304]{1,0:T(8,128)(2,1)}) custom-call(s32[3]{0:T(128)S(1)} %add_add_fusion.1.pick_ref, bf16[576,1152]{1,0:T(8,128)(2,1)S(1)} %collective-permute-done.3.low_ref, bf16[576,1152]{1,0:T(8,128)(2,1)S(1)} %collective-permute-done.7.high_ref, ...), custom_call_target="tpu_custom_call", output_to_operand_aliasing={{1}: (4, {})} | custom-call | flops 1 | bytes 1 | tf_op jit(solution)/shard_map/gates_step/pallas_call | solution.py:254
  86.2 20.3 %gates_pool.3 = (bf16[288,1152]{1,0:T(8,128)(2,1)S(1)}, f32[288,128]{1,0:T(8,128)}, bf16[2,3,288,2304]{3,2,1,0:T(8,128)(2,1)}, bf16[2304,2304]{1,0:T(8,128)(2,1)}) custom-call(s32[3]{0:T(128)S(1)} %add_add_fusion.pick_ref, s32[1]{0:T(128)} %bitcast.7.length_ref, ...), custom_call_target="tpu_custom_call", output_to_operand_aliasing={{3}: (8, {}), {2}: (9, {})} | custom-call | flops 1 | bytes 1 | tf_op jit(solution)/shard_map/gates_pool/pallas_call | solution.py:319
  107.5 9.6 %back_products.4 = (f32[576,1152]{1,0:T(8,128)S(1)}, bf16[576,1152]{1,0:T(8,128)(2,1)S(1)}) custom-call(s32[3]{0:T(128)S(1)} %add_add_fusion.1.pick_ref, bf16[1728,1152]{1,0:T(8,128)(2,1)S(1)} %bitcast.26, bf16[1728,2304]{1,0:T(8,128)(2,1)} %bitcast.33), custom_call_target="tpu_custom_call" | custom-call | flops 1 | bytes 1 | tf_op jit(solution)/shard_map/back_products/pallas_call | solution.py:394
  118.9 10.3 %back_products.5 = (f32[576,1152]{1,0:T(8,128)S(1)}, bf16[576,1152]{1,0:T(8,128)(2,1)}) custom-call(s32[3]{0:T(128)S(1)} %add_add_fusion.1.pick_ref, bf16[1728,1152]{1,0:T(8,128)(2,1)S(1)} %bitcast.24, bf16[1728,2304]{1,0:T(8,128)(2,1)} %bitcast.34), custom_call_target="tpu_custom_call" | custom-call | flops 1 | bytes 1 | tf_op jit(solution)/shard_map/back_products/pallas_call | solution.py:394
  129.6 10.3 %back_products.6 = (f32[576,1152]{1,0:T(8,128)S(1)}, bf16[576,1152]{1,0:T(8,128)(2,1)}) custom-call(s32[3]{0:T(128)S(1)} %add_add_fusion.1.pick_ref, bf16[1728,1152]{1,0:T(8,128)(2,1)S(1)} %bitcast.27, bf16[1728,2304]{1,0:T(8,128)(2,1)} %bitcast.35), custom_call_target="tpu_custom_call" | custom-call | flops 1 | bytes 1 | tf_op jit(solution)/shard_map/back_products/pallas_call | solution.py:394
  146.0 9.8 %back_products.7 = (f32[576,1152]{1,0:T(8,128)S(1)}, bf16[576,1152]{1,0:T(8,128)(2,1)S(1)}) custom-call(s32[3]{0:T(128)S(1)} %add_add_fusion.1.pick_ref, bf16[1728,1152]{1,0:T(8,128)(2,1)S(1)} %bitcast.25, bf16[1728,2304]{1,0:T(8,128)(2,1)} %bitcast.36), custom_call_target="tpu_custom_call" | custom-call | flops 1 | bytes 1 | tf_op jit(solution)/shard_map/back_products/pallas_call | solution.py:394
  158.4 3.9 collective-permute-start.16
  163.9 23.6 %convolution_convert_fusion.refs_0_ = bf16[1728,2304]{1,0:T(8,128)(2,1)S(1)} fusion(bf16[1728,2304]{1,0:T(8,128)(2,1)} %bitcast.37, bf16[2304,2304]{1,0:T(8,128)(2,1)} %get-tuple-element.805), kind=kOutput, calls=%fused_computation | convolution fusion | flops 18349867008 | bytes 26542080 | tf_op jit(solution)/shard_map/dot_general | solution.py:204
  195.3 7.0 %collective-permute-done.17.refs_1_ = bf16[96,2304]{1,0:T(8,128)(2,1)S(1)} collective-permute-done((bf16[96,2304]{1,0:T(8,128)(2,1)S(1)}, bf16[96,2304]{1,0:T(8,128)(2,1)S(1)}, u32[]{:S(2)}, u32[]{:S(2)}) %collective-permute-start.17) | collective-permute-done | bytes 442400 | tf_op jit(solution)/shard_map/ppermute | solution.py:584
  205.9 5.9 %collective-permute-done.21.refs_1_ = bf16[96,2304]{1,0:T(8,128)(2,1)S(1)} collective-permute-done((bf16[96,2304]{1,0:T(8,128)(2,1)S(1)}, bf16[96,2304]{1,0:T(8,128)(2,1)S(1)}, u32[]{:S(2)}, u32[]{:S(2)}) %collective-permute-start.21) | collective-permute-done | bytes 442400 | tf_op jit(solution)/shard_map/ppermute | solution.py:611
  212.8 4.7 %collective-permute-start.27 = (bf16[96,2304]{1,0:T(8,128)(2,1)S(1)}, bf16[96,2304]{1,0:T(8,128)(2,1)S(1)}, u32[]{:S(2)}, u32[]{:S(2)}) collective-permute-start(bf16[96,2304]{1,0:T(8,128)(2,1)S(1)} %chunk_step.64), channel_id=1, source_target_pairs={{0,8},{4,12},{8,0},{12,4},{16,24},{20,28},{24,16},{28,20},{1,9},{5... | collective-permute-start | bytes 1327112 | tf_op jit(solution)/shard_map/ppermute | solution.py:611
  217.5 3.8 collective-permute-done.23.refs_1_
  222.3 4.7 %collective-permute-start.24 = (bf16[96,2304]{1,0:T(8,128)(2,1)S(1)}, bf16[96,2304]{1,0:T(8,128)(2,1)S(1)}, u32[]{:S(2)}, u32[]{:S(2)}) collective-permute-start(bf16[96,2304]{1,0:T(8,128)(2,1)S(1)} %chunk_step.67), channel_id=1, source_target_pairs={{0,8},{4,12},{8,0},{12,4},{16,24},{20,28},{24,16},{28,20},{1,9},{5... | collective-permute-start | bytes 1327112 | tf_op jit(solution)/shard_map/ppermute | solution.py:611
  231.8 4.6 %collective-permute-start.30 = (bf16[96,2304]{1,0:T(8,128)(2,1)S(1)}, bf16[96,2304]{1,0:T(8,128)(2,1)S(1)}, u32[]{:S(2)}, u32[]{:S(2)}) collective-permute-start(bf16[96,2304]{1,0:T(8,128)(2,1)S(1)} %chunk_step.70), channel_id=1, source_target_pairs={{0,8},{4,12},{8,0},{12,4},{16,24},{20,28},{24,16},{28,20},{1,9},{5... | collective-permute-start | bytes 1327112 | tf_op jit(solution)/shard_map/ppermute | solution.py:611
  245.9 3.9 collective-permute-done.30.refs_1_
  255.4 3.9 collective-permute-done.33.refs_1_
  264.9 3.9 collective-permute-done.39.refs_1_
  283.8 3.9 collective-permute-done.41.refs_1_
  293.3 3.9 collective-permute-done.45.refs_1_
  312.3 3.9 collective-permute-done.47.refs_1_
  321.7 3.9 collective-permute-done.53.refs_1_
  340.7 3.9 collective-permute-done.62.refs_1_
  350.2 3.9 collective-permute-done.59.refs_1_
  368.2 4.8 %collective-permute-done.67.refs_0_ = bf16[96,2304]{1,0:T(8,128)(2,1)S(1)} collective-permute-done((bf16[96,2304]{1,0:T(8,128)(2,1)S(1)}, bf16[96,2304]{1,0:T(8,128)(2,1)S(1)}, u32[]{:S(2)}, u32[]{:S(2)}) %collective-permute-start.67) | collective-permute-done | bytes 442400 | tf_op jit(solution)/shard_map/ppermute | solution.py:611
  387.0 4.0 write_chunks.10.refs_6_
  403.5 4.7 %collective-permute-done.77.refs_4_ = bf16[96,2304]{1,0:T(8,128)(2,1)} collective-permute-done((bf16[96,2304]{1,0:T(8,128)(2,1)S(1)}, bf16[96,2304]{1,0:T(8,128)(2,1)}, u32[]{:S(2)}, u32[]{:S(2)}) %collective-permute-start.77) | collective-permute-done | bytes 442400 | tf_op jit(solution)/shard_map/ppermute | solution.py:615
  408.1 9.6 %collective-permute-done.79 = f32[288,128]{1,0:T(8,128)S(1)} collective-permute-done((f32[288,128]{1,0:T(8,128)}, f32[288,128]{1,0:T(8,128)S(1)}, u32[]{:S(2)}, u32[]{:S(2)}) %collective-permute-start.79) | collective-permute-done | bytes 147488 | tf_op jit(solution)/shard_map/ppermute | solution.py:785
  419.4 3.9 write_chunks.11
  (350 shorter events, 184.0 us)
Async XLA Ops:
  6.3 32.5 %collective-permute-start = (bf16[576,1152]{1,0:T(8,128)(2,1)}, bf16[576,1152]{1,0:T(8,128)(2,1)S(1)}, u32[]{:S(2)}, u32[]{:S(2)}) collective-permute-start(bf16[576,1152]{1,0:T(8,128)(2,1)} %convolution_convert_fusion.2.low_ref), channel_id=1, source_target_pairs={{0,2},{1,3},{2,0},{3,1},{4,6},{5,7},{6,4},{7,5},{8,10},{9,11},{10,... | collective-permute-start | bytes 3981320 | tf_op jit(solution)/shard_map/ppermute | solution.py:662
  8.8 32.9 %collective-permute-start.3 = (bf16[576,1152]{1,0:T(8,128)(2,1)}, bf16[576,1152]{1,0:T(8,128)(2,1)S(1)}, u32[]{:S(2)}, u32[]{:S(2)}) collective-permute-start(bf16[576,1152]{1,0:T(8,128)(2,1)} %convolution_convert_fusion.2.low_ref), channel_id=1, source_target_pairs={{0,4},{4,0},{8,12},{12,8},{16,20},{20,16},{24,28},{28,24},{1,5},{5... | collective-permute-start | bytes 3981320 | tf_op jit(solution)/shard_map/ppermute | solution.py:663
  39.9 27.1 %collective-permute-start.5 = (bf16[480,1152]{1,0:T(8,128)(2,1)}, bf16[480,1152]{1,0:T(8,128)(2,1)}, u32[]{:S(2)}, u32[]{:S(2)}) collective-permute-start(bf16[480,1152]{1,0:T(8,128)(2,1)} %pad_maximum_fusion.1), channel_id=1, source_target_pairs={{0,4},{4,0},{8,12},{12,8},{16,20},{20,16},{24,28},{28,24},{1,5},{5... | collective-permute-start | bytes 3317768 | tf_op jit(solution)/shard_map/ppermute | solution.py:677
  42.7 23.0 %collective-permute-start.4 = (bf16[384,1152]{1,0:T(8,128)(2,1)}, bf16[384,1152]{1,0:T(8,128)(2,1)}, u32[]{:S(2)}, u32[]{:S(2)}) collective-permute-start(bf16[384,1152]{1,0:T(8,128)(2,1)} %slice.27), channel_id=1, source_target_pairs={{0,2},{1,3},{2,0},{3,1},{4,6},{5,7},{6,4},{7,5},{8,10},{9,11},{10,... | collective-permute-start | bytes 2654216 | tf_op jit(solution)/shard_map/ppermute | solution.py:676
  141.5 20.8 %collective-permute-start.14 = (bf16[576,1152]{1,0:T(8,128)(2,1)}, bf16[576,1152]{1,0:T(8,128)(2,1)}, u32[]{:S(2)}, u32[]{:S(2)}) collective-permute-start(bf16[576,1152]{1,0:T(8,128)(2,1)} %get-tuple-element.793), channel_id=1, source_target_pairs={{0,1},{1,0},{2,3},{3,2},{4,5},{5,4},{6,7},{7,6},{8,9},{9,8},{10,11... | collective-permute-start | bytes 3981320 | tf_op jit(solution)/shard_map/ppermute | solution.py:723
  143.2 44.6 %collective-permute-start.9 = (bf16[288,1152]{1,0:T(8,128)(2,1)S(1)}, bf16[288,1152]{1,0:T(8,128)(2,1)}, u32[]{:S(2)}, u32[]{:S(2)}) collective-permute-start(bf16[288,1152]{1,0:T(8,128)(2,1)S(1)} %get-tuple-element.740), channel_id=1, source_target_pairs={{0,4},{4,0},{8,12},{12,8},{16,20},{20,16},{24,28},{28,24},{1,5},{5... | collective-permute-start | bytes 1990664 | tf_op jit(solution)/shard_map/ppermute | solution.py:785
  155.8 31.7 %collective-permute-start.13 = (bf16[576,1152]{1,0:T(8,128)(2,1)S(1)}, bf16[576,1152]{1,0:T(8,128)(2,1)S(1)}, u32[]{:S(2)}, u32[]{:S(2)}) collective-permute-start(bf16[576,1152]{1,0:T(8,128)(2,1)S(1)} %get-tuple-element.790), channel_id=1, source_target_pairs={{0,1},{1,0},{2,3},{3,2},{4,5},{5,4},{6,7},{7,6},{8,9},{9,8},{10,11... | collective-permute-start | bytes 3981320 | tf_op jit(solution)/shard_map/ppermute | solution.py:723
  155.9 33.4 %collective-permute-start.19 = (bf16[576,1152]{1,0:T(8,128)(2,1)S(1)}, bf16[576,1152]{1,0:T(8,128)(2,1)S(1)}, u32[]{:S(2)}, u32[]{:S(2)}) collective-permute-start(bf16[576,1152]{1,0:T(8,128)(2,1)S(1)} %copy-done.18), channel_id=1, source_target_pairs={{0,2},{1,3},{2,0},{3,1},{4,6},{5,7},{6,4},{7,5},{8,10},{9,11},{10,... | collective-permute-start | bytes 3981320 | tf_op jit(solution)/shard_map/ppermute | solution.py:734
  158.4 29.4 %collective-permute-start.16 = (f32[288,128]{1,0:T(8,128)S(1)}, f32[288,128]{1,0:T(8,128)S(1)}, u32[]{:S(2)}, u32[]{:S(2)}) collective-permute-start(f32[288,128]{1,0:T(8,128)S(1)} %add.64), channel_id=1, source_target_pairs={{8,0},{12,4},{16,24},{20,28},{0,8},{4,12},{24,16},{28,20},{9,1},{1... | collective-permute-start | bytes 442376 | tf_op jit(solution)/shard_map/ppermute | solution.py:835
  189.4 37.6 %collective-permute-start.28 = (bf16[576,1152]{1,0:T(8,128)(2,1)S(1)}, bf16[576,1152]{1,0:T(8,128)(2,1)S(1)}, u32[]{:S(2)}, u32[]{:S(2)}) collective-permute-start(bf16[576,1152]{1,0:T(8,128)(2,1)S(1)} %whole.9), channel_id=1, source_target_pairs={{0,2},{1,3},{2,0},{3,1},{4,6},{5,7},{6,4},{7,5},{8,10},{9,11},{10,... | collective-permute-start | bytes 3981320 | tf_op jit(solution)/shard_map/ppermute | solution.py:734
  191.1 20.7 %collective-permute-start.21 = (bf16[96,2304]{1,0:T(8,128)(2,1)S(1)}, bf16[96,2304]{1,0:T(8,128)(2,1)S(1)}, u32[]{:S(2)}, u32[]{:S(2)}) collective-permute-start(bf16[96,2304]{1,0:T(8,128)(2,1)S(1)} %chunk_step.59), channel_id=1, source_target_pairs={{0,8},{4,12},{8,0},{12,4},{16,24},{20,28},{24,16},{28,20},{1,9},{5... | collective-permute-start | bytes 1327112 | tf_op jit(solution)/shard_map/ppermute | solution.py:611
  202.7 33.7 %collective-permute-start.25 = (bf16[576,1152]{1,0:T(8,128)(2,1)S(1)}, bf16[576,1152]{1,0:T(8,128)(2,1)S(1)}, u32[]{:S(2)}, u32[]{:S(2)}) collective-permute-start(bf16[576,1152]{1,0:T(8,128)(2,1)S(1)} %whole.11), channel_id=1, source_target_pairs={{0,4},{4,0},{8,12},{12,8},{16,20},{20,16},{24,28},{28,24},{1,5},{5... | collective-permute-start | bytes 3981320 | tf_op jit(solution)/shard_map/ppermute | solution.py:775
  204.6 16.7 %collective-permute-start.23 = (bf16[96,2304]{1,0:T(8,128)(2,1)S(1)}, bf16[96,2304]{1,0:T(8,128)(2,1)S(1)}, u32[]{:S(2)}, u32[]{:S(2)}) collective-permute-start(bf16[96,2304]{1,0:T(8,128)(2,1)S(1)} %chunk_step.61), channel_id=1, source_target_pairs={{0,8},{4,12},{8,0},{12,4},{16,24},{20,28},{24,16},{28,20},{1,9},{5... | collective-permute-start | bytes 1327112 | tf_op jit(solution)/shard_map/ppermute | solution.py:611
  212.8 18.0 %collective-permute-start.27 = (bf16[96,2304]{1,0:T(8,128)(2,1)S(1)}, bf16[96,2304]{1,0:T(8,128)(2,1)S(1)}, u32[]{:S(2)}, u32[]{:S(2)}) collective-permute-start(bf16[96,2304]{1,0:T(8,128)(2,1)S(1)} %chunk_step.64), channel_id=1, source_target_pairs={{0,8},{4,12},{8,0},{12,4},{16,24},{20,28},{24,16},{28,20},{1,9},{5... | collective-permute-start | bytes 1327112 | tf_op jit(solution)/shard_map/ppermute | solution.py:611
  222.3 18.0 %collective-permute-start.24 = (bf16[96,2304]{1,0:T(8,128)(2,1)S(1)}, bf16[96,2304]{1,0:T(8,128)(2,1)S(1)}, u32[]{:S(2)}, u32[]{:S(2)}) collective-permute-start(bf16[96,2304]{1,0:T(8,128)(2,1)S(1)} %chunk_step.67), channel_id=1, source_target_pairs={{0,8},{4,12},{8,0},{12,4},{16,24},{20,28},{24,16},{28,20},{1,9},{5... | collective-permute-start | bytes 1327112 | tf_op jit(solution)/shard_map/ppermute | solution.py:611
  231.8 18.0 %collective-permute-start.30 = (bf16[96,2304]{1,0:T(8,128)(2,1)S(1)}, bf16[96,2304]{1,0:T(8,128)(2,1)S(1)}, u32[]{:S(2)}, u32[]{:S(2)}) collective-permute-start(bf16[96,2304]{1,0:T(8,128)(2,1)S(1)} %chunk_step.70), channel_id=1, source_target_pairs={{0,8},{4,12},{8,0},{12,4},{16,24},{20,28},{24,16},{28,20},{1,9},{5... | collective-permute-start | bytes 1327112 | tf_op jit(solution)/shard_map/ppermute | solution.py:611
  242.5 16.7 %collective-permute-start.33 = (bf16[96,2304]{1,0:T(8,128)(2,1)S(1)}, bf16[96,2304]{1,0:T(8,128)(2,1)S(1)}, u32[]{:S(2)}, u32[]{:S(2)}) collective-permute-start(bf16[96,2304]{1,0:T(8,128)(2,1)S(1)} %chunk_step.73), channel_id=1, source_target_pairs={{0,8},{4,12},{8,0},{12,4},{16,24},{20,28},{24,16},{28,20},{1,9},{5... | collective-permute-start | bytes 1327112 | tf_op jit(solution)/shard_map/ppermute | solution.py:611
  252.0 16.8 %collective-permute-start.39 = (bf16[96,2304]{1,0:T(8,128)(2,1)S(1)}, bf16[96,2304]{1,0:T(8,128)(2,1)S(1)}, u32[]{:S(2)}, u32[]{:S(2)}) collective-permute-start(bf16[96,2304]{1,0:T(8,128)(2,1)S(1)} %chunk_step.76), channel_id=1, source_target_pairs={{0,8},{4,12},{8,0},{12,4},{16,24},{20,28},{24,16},{28,20},{1,9},{5... | collective-permute-start | bytes 1327112 | tf_op jit(solution)/shard_map/ppermute | solution.py:611
  261.6 16.6 %collective-permute-start.35 = (bf16[96,2304]{1,0:T(8,128)(2,1)S(1)}, bf16[96,2304]{1,0:T(8,128)(2,1)S(1)}, u32[]{:S(2)}, u32[]{:S(2)}) collective-permute-start(bf16[96,2304]{1,0:T(8,128)(2,1)S(1)} %chunk_step.79), channel_id=1, source_target_pairs={{0,8},{4,12},{8,0},{12,4},{16,24},{20,28},{24,16},{28,20},{1,9},{5... | collective-permute-start | bytes 1327112 | tf_op jit(solution)/shard_map/ppermute | solution.py:611
  270.9 16.8 %collective-permute-start.41 = (bf16[96,2304]{1,0:T(8,128)(2,1)S(1)}, bf16[96,2304]{1,0:T(8,128)(2,1)S(1)}, u32[]{:S(2)}, u32[]{:S(2)}) collective-permute-start(bf16[96,2304]{1,0:T(8,128)(2,1)S(1)} %chunk_step.82), channel_id=1, source_target_pairs={{0,8},{4,12},{8,0},{12,4},{16,24},{20,28},{24,16},{28,20},{1,9},{5... | collective-permute-start | bytes 1327112 | tf_op jit(solution)/shard_map/ppermute | solution.py:611
  280.4 16.8 %collective-permute-start.45 = (bf16[96,2304]{1,0:T(8,128)(2,1)S(1)}, bf16[96,2304]{1,0:T(8,128)(2,1)S(1)}, u32[]{:S(2)}, u32[]{:S(2)}) collective-permute-start(bf16[96,2304]{1,0:T(8,128)(2,1)S(1)} %chunk_step.85), channel_id=1, source_target_pairs={{0,8},{4,12},{8,0},{12,4},{16,24},{20,28},{24,16},{28,20},{1,9},{5... | collective-permute-start | bytes 1327112 | tf_op jit(solution)/shard_map/ppermute | solution.py:611
  289.9 16.8 %collective-permute-start.50 = (bf16[96,2304]{1,0:T(8,128)(2,1)S(1)}, bf16[96,2304]{1,0:T(8,128)(2,1)S(1)}, u32[]{:S(2)}, u32[]{:S(2)}) collective-permute-start(bf16[96,2304]{1,0:T(8,128)(2,1)S(1)} %chunk_step.88), channel_id=1, source_target_pairs={{0,8},{4,12},{8,0},{12,4},{16,24},{20,28},{24,16},{28,20},{1,9},{5... | collective-permute-start | bytes 1327112 | tf_op jit(solution)/shard_map/ppermute | solution.py:611
  299.4 16.8 %collective-permute-start.47 = (bf16[96,2304]{1,0:T(8,128)(2,1)S(1)}, bf16[96,2304]{1,0:T(8,128)(2,1)S(1)}, u32[]{:S(2)}, u32[]{:S(2)}) collective-permute-start(bf16[96,2304]{1,0:T(8,128)(2,1)S(1)} %chunk_step.91), channel_id=1, source_target_pairs={{0,8},{4,12},{8,0},{12,4},{16,24},{20,28},{24,16},{28,20},{1,9},{5... | collective-permute-start | bytes 1327112 | tf_op jit(solution)/shard_map/ppermute | solution.py:611
  308.8 16.8 %collective-permute-start.53 = (bf16[96,2304]{1,0:T(8,128)(2,1)S(1)}, bf16[96,2304]{1,0:T(8,128)(2,1)S(1)}, u32[]{:S(2)}, u32[]{:S(2)}) collective-permute-start(bf16[96,2304]{1,0:T(8,128)(2,1)S(1)} %chunk_step.94), channel_id=1, source_target_pairs={{0,8},{4,12},{8,0},{12,4},{16,24},{20,28},{24,16},{28,20},{1,9},{5... | collective-permute-start | bytes 1327112 | tf_op jit(solution)/shard_map/ppermute | solution.py:611
  318.3 16.8 %collective-permute-start.57 = (bf16[96,2304]{1,0:T(8,128)(2,1)S(1)}, bf16[96,2304]{1,0:T(8,128)(2,1)S(1)}, u32[]{:S(2)}, u32[]{:S(2)}) collective-permute-start(bf16[96,2304]{1,0:T(8,128)(2,1)S(1)} %chunk_step.97), channel_id=1, source_target_pairs={{0,8},{4,12},{8,0},{12,4},{16,24},{20,28},{24,16},{28,20},{1,9},{5... | collective-permute-start | bytes 1327112 | tf_op jit(solution)/shard_map/ppermute | solution.py:611
  327.8 16.8 %collective-permute-start.62 = (bf16[96,2304]{1,0:T(8,128)(2,1)S(1)}, bf16[96,2304]{1,0:T(8,128)(2,1)S(1)}, u32[]{:S(2)}, u32[]{:S(2)}) collective-permute-start(bf16[96,2304]{1,0:T(8,128)(2,1)S(1)} %chunk_step.100), channel_id=1, source_target_pairs={{0,8},{4,12},{8,0},{12,4},{16,24},{20,28},{24,16},{28,20},{1,9},{5... | collective-permute-start | bytes 1327112 | tf_op jit(solution)/shard_map/ppermute | solution.py:611
  337.3 16.8 %collective-permute-start.59 = (bf16[96,2304]{1,0:T(8,128)(2,1)S(1)}, bf16[96,2304]{1,0:T(8,128)(2,1)S(1)}, u32[]{:S(2)}, u32[]{:S(2)}) collective-permute-start(bf16[96,2304]{1,0:T(8,128)(2,1)S(1)} %chunk_step.103), channel_id=1, source_target_pairs={{0,8},{4,12},{8,0},{12,4},{16,24},{20,28},{24,16},{28,20},{1,9},{5... | collective-permute-start | bytes 1327112 | tf_op jit(solution)/shard_map/ppermute | solution.py:611
  346.8 16.8 %collective-permute-start.64 = (bf16[96,2304]{1,0:T(8,128)(2,1)S(1)}, bf16[96,2304]{1,0:T(8,128)(2,1)S(1)}, u32[]{:S(2)}, u32[]{:S(2)}) collective-permute-start(bf16[96,2304]{1,0:T(8,128)(2,1)S(1)} %chunk_step.106), channel_id=1, source_target_pairs={{0,8},{4,12},{8,0},{12,4},{16,24},{20,28},{24,16},{28,20},{1,9},{5... | collective-permute-start | bytes 1327112 | tf_op jit(solution)/shard_map/ppermute | solution.py:611
  356.1 16.9 %collective-permute-start.67 = (bf16[96,2304]{1,0:T(8,128)(2,1)S(1)}, bf16[96,2304]{1,0:T(8,128)(2,1)S(1)}, u32[]{:S(2)}, u32[]{:S(2)}) collective-permute-start(bf16[96,2304]{1,0:T(8,128)(2,1)S(1)} %chunk_step.105.refs_1_), channel_id=1, source_target_pairs={{0,8},{4,12},{8,0},{12,4},{16,24},{20,28},{24,16},{28,20},{1,9},{5... | collective-permute-start | bytes 1327112 | tf_op jit(solution)/shard_map/ppermute | solution.py:611
  376.0 19.6 %collective-permute-start.74 = (bf16[96,2304]{1,0:T(8,128)(2,1)}, bf16[96,2304]{1,0:T(8,128)(2,1)S(1)}, u32[]{:S(2)}, u32[]{:S(2)}) collective-permute-start(bf16[96,2304]{1,0:T(8,128)(2,1)} %copy-done.11), channel_id=1, source_target_pairs={{0,8},{4,12},{8,0},{12,4},{16,24},{20,28},{24,16},{28,20},{1,9},{5... | collective-permute-start | bytes 1327112 | tf_op jit(solution)/shard_map/ppermute | solution.py:611
  400.4 18.0 %collective-permute-start.78 = (bf16[96,2304]{1,0:T(8,128)(2,1)S(1)}, bf16[96,2304]{1,0:T(8,128)(2,1)S(1)}, u32[]{:S(2)}, u32[]{:S(2)}) collective-permute-start(bf16[96,2304]{1,0:T(8,128)(2,1)S(1)} %chunk_step.115.refs_2_), channel_id=1, source_target_pairs={{0,4},{4,0},{8,12},{12,8},{16,20},{20,16},{24,28},{28,24},{1,5},{5... | collective-permute-start | bytes 1327112 | tf_op jit(solution)/shard_map/ppermute | solution.py:615
  401.6 16.1 %collective-permute-start.79 = (f32[288,128]{1,0:T(8,128)}, f32[288,128]{1,0:T(8,128)S(1)}, u32[]{:S(2)}, u32[]{:S(2)}) collective-permute-start(f32[288,128]{1,0:T(8,128)} %get-tuple-element.1274), channel_id=1, source_target_pairs={{0,4},{4,0},{8,12},{12,8},{16,20},{20,16},{24,28},{28,24},{1,5},{5... | collective-permute-start | bytes 442376 | tf_op jit(solution)/shard_map/ppermute | solution.py:785
  (101 other events, 1024.4 us)
